TPU v7x, 32 devices: a whole 2x2x4 slice. The times are simulated.
32 devices in a mesh: seq: 8 (over z, y), head: 4 (over x, core).
Axes of the slice: x: 2, y: 2, z: 4, core: 2. Of those that a mesh axis runs over, the one named last changes fastest.
Arguments:
- queries: bfloat16 [32768, 2048], P('seq', 'head'), may hold values from -6 to 6
- keys: bfloat16 [32768, 2048], P('seq', 'head'), may hold values from -0.59765625 to 0.59765625
- values: bfloat16 [32768, 2048], P('seq', 'head'), may hold values from -6 to 6
- norm_gain: float32 [2048], replicated, may hold values from 0.1 to 1.9
Outputs:
- normed: bfloat16 [32768, 2048], P(('seq', 'head'))
All inputs are finite; a program needn't handle non-finite values.
Results may differ from a plain program's by a relative error of at most 0.0058.
Values may be sent and summed in bfloat16 or wider, within the bound.
No kernel may reach another device: no remote copies, remote signals or barrier semaphores. Data moves between devices by JAX's collectives and lax.ppermute only.
A program may use at most 128 MiB of HBM per device.

v0:
```python
import jax
import jax.numpy as jnp
from jax import lax
from jax.sharding import PartitionSpec as P

DH = 128
BLK = 512


def add_lower(piece, mine):
    ranks = jnp.arange(piece.shape[0], dtype=jnp.int32)
    keep = (ranks < mine).astype(jnp.float32)[:, None, None, None]
    return jnp.sum(piece * keep, axis=0)


def shards(queries, keys, values, norm_gain):
    rows, width = queries.shape
    heads = width // DH
    blocks = rows // BLK
    query_rows = queries.reshape(blocks, BLK, heads, DH)
    key_rows = keys.reshape(blocks, BLK, heads, DH)
    value_rows = values.reshape(blocks, BLK, heads, DH)
    block_state = jnp.einsum(
        "nbhd,nbhe->nhde", key_rows, value_rows, preferred_element_type=jnp.float32
    )
    total = jnp.sum(block_state, axis=0)
    mine = lax.axis_index("seq")
    before = add_lower(lax.all_gather(total[None], "seq", axis=0, tiled=True), mine)
    running = jnp.cumsum(block_state, axis=0)
    within = jnp.concatenate([jnp.zeros_like(block_state[:1]), running[:-1]], axis=0)
    prefix_low = (before[None] + within).astype(jnp.bfloat16)
    inter = jnp.einsum(
        "nbhd,nhde->nbhe", query_rows, prefix_low, preferred_element_type=jnp.float32
    )
    scores = jnp.einsum("nbhd,nchd->nhbc", query_rows, key_rows, preferred_element_type=jnp.float32)
    causal = jnp.arange(BLK)[:, None] >= jnp.arange(BLK)[None, :]
    scores = jnp.where(causal[None, None], scores, jnp.zeros_like(scores)).astype(jnp.bfloat16)
    intra = jnp.einsum("nhbc,nche->nbhe", scores, value_rows, preferred_element_type=jnp.float32)
    attention = (inter + intra).astype(jnp.bfloat16).reshape(rows, width)
    regrouped = lax.all_to_all(attention, "head", split_axis=0, concat_axis=1, tiled=True)
    widened = regrouped.astype(jnp.float32)
    meansq = jnp.mean(widened * widened, axis=-1, keepdims=True)
    return (widened * lax.rsqrt(meansq + 1e-06) * norm_gain[None, :]).astype(jnp.bfloat16)


def solution(mesh):
    return jax.shard_map(
        shards,
        mesh=mesh,
        in_specs=(P("seq", "head"), P("seq", "head"), P("seq", "head"), P()),
        out_specs=P(("seq", "head"), None),
        check_vma=False,
    )
```

profile of v0, /device:TPU:1, one launch (start us, length us, event | category | flops | bytes accessed | tf_op | source)
XLA Modules:
  0.0 201.7 jit_solution(15274765452510856249)
XLA Ops:
  6.5 0.0 all-gather.3.cloned.1.call-start
  6.5 6.9 %reshape.43 = bf16[8,512,4,128]{3,2,1,0:T(4,128)(2,1)} reshape(bf16[4096,512]{1,0:T(8,128)(2,1)} %param.5) | data formatting | bytes 8388608 | tf_op jit(solution)/shard_map/reshape | solution.py:21
  13.4 6.9 %reshape.44 = bf16[8,512,4,128]{3,2,1,0:T(4,128)(2,1)} reshape(bf16[4096,512]{1,0:T(8,128)(2,1)} %param.6) | data formatting | bytes 8388608 | tf_op jit(solution)/shard_map/reshape | solution.py:22
  20.4 5.9 %fusion.28 = (f32[4,128,128]{2,1,0:T(8,128)}, f32[8,4,128,128]{3,2,1,0:T(8,128)S(1)}) fusion(bf16[8,512,4,128]{3,2,1,0:T(4,128)(2,1)} %reshape.44, bf16[8,512,4,128]{3,2,1,0:T(4,128)(2,1)} %reshape.43), kind=kOutput, calls=%fused_computation.29 | convolution fusion | flops 537329664 | bytes 10747904 | tf_op jit(solution)/shard_map/nbhd,nbhe->nhde/dot_general | solution.py:23
  26.3 0.0 all-gather.3.cloned.1.call-update
  26.3 6.9 %reshape.45 = bf16[8,512,4,128]{3,2,1,0:T(4,128)(2,1)} reshape(bf16[4096,512]{1,0:T(8,128)(2,1)} %param.4) | data formatting | bytes 8388608 | tf_op jit(solution)/shard_map/reshape | solution.py:20
  33.2 1.9 fusion.29
  35.2 0.2 slice.4
  35.4 0.1 iota_compare_fusion
  35.5 41.3 %all-gather.3.cloned.1.call-done = f32[32,128,128]{2,1,0:T(8,128)} async-done(((f32[4,128,128]{2,1,0:T(8,128)}), f32[32,128,128]{2,1,0:T(8,128)}) %all-gather.3.cloned.1.call-update) | async-done | bytes 2097168 | tf_op jit(solution)/shard_map/all_gather | solution.py:28
  76.8 1.9 multiply_reduce_fusion
  78.6 6.8 %fusion.15 = f32[8,4,128,512]{3,2,1,0:T(8,128)} fusion(bf16[8,512,4,128]{3,2,1,0:T(4,128)(2,1)} %reshape.45, f32[7,4,128,128]{3,2,1,0:T(8,128)S(1)} %slice.4, f32[4,128,128]{2,1,0:T(8,128)S(1)} %multiply_reduce_fusion), kind=kOutput, calls=%fused_computation.17 | convolution fusion | flops 537919488 | bytes 14680064 | tf_op jit(solution)/shard_map/nbhd,nhde->nbhe/dot_general | solution.py:32
  85.5 16.4 %fusion.8 = bf16[8,512,4,128]{1,3,2,0:T(8,128)(2,1)} fusion(f32[8,4,128,512]{3,2,1,0:T(8,128)} %fusion.15, bf16[8,512,4,128]{3,2,1,0:T(4,128)(2,1)} %reshape.44, pred[512,512]{1,0:T(8,128)(4,1)S(1)} %iota_compare_fusion, bf16[8,512,4,128]{3,2,1,0:T(4,128)(2,1)} %reshape.43, bf16[8,512,4,128]{3,2,1,0:T(4,128)(2,1)} %reshape.45), kind=kOutput, calls=%fused_computation.12 | convolution fusion | flops 4315938816 | bytes 25427968 | tf_op jit(solution)/shard_map/nhbc,nche->nbhe/dot_general | solution.py:38
  101.9 7.4 %copy.37 = bf16[8,512,4,128]{3,2,1,0:T(4,128)(2,1)} copy(bf16[8,512,4,128]{1,3,2,0:T(8,128)(2,1)} %fusion.8) | data formatting | bytes 8388608 | tf_op jit(solution)/shard_map/convert_element_type | solution.py:39
  109.3 7.2 %all_to_all.10 = bf16[4,1024,512]{2,1,0:T(8,128)(2,1)} reshape(bf16[8,512,4,128]{3,2,1,0:T(4,128)(2,1)} %copy.37) | data formatting | bytes 8388608 | tf_op jit(solution)/shard_map/all_to_all | solution.py:40
  116.5 52.7 %all_to_all.13 = bf16[4,1024,512]{2,1,0:T(8,128)(2,1)S(1)} all-to-all(bf16[4,1024,512]{2,1,0:T(8,128)(2,1)} %all_to_all.10), channel_id=1, replica_groups=mesh['seq'=8,'head'=4] {'head'}, dimensions={0} | all-to-all | bytes 8388608 | tf_op jit(solution)/shard_map/all_to_all | solution.py:40
  169.2 0.9 fusion.5
  170.1 4.4 %convert_bitcast_fusion = f32[1024,4,512]{2,0,1:T(8,128)} fusion(bf16[4,1024,512]{2,1,0:T(8,128)(2,1)S(1)} %all_to_all.13), kind=kLoop, calls=%fused_computation.6 | loop fusion | flops 2097152 | bytes 12582912 | tf_op jit(solution)/shard_map/convert_element_type | solution.py:41
  174.5 0.0 copy-start
  174.5 8.7 %copy.38 = f32[1024,4,512]{0,2,1:T(8,128)} copy(f32[1024,4,512]{2,0,1:T(8,128)} %convert_bitcast_fusion) | data formatting | bytes 16777216 | tf_op jit(solution)/shard_map/convert_element_type | solution.py:41
  183.2 0.0 copy-done
  183.2 5.2 %fusion.7 = bf16[1024,2048]{0,1:T(8,128)(2,1)} fusion(f32[1024,4,512]{0,2,1:T(8,128)} %copy.38, f32[2048]{0:T(1024)S(1)} %copy-done, f32[1024]{0:T(1024)S(1)} %add_rsqrt_fusion), kind=kLoop, calls=%fused_computation.10 | loop fusion | flops 6291456 | bytes 12595200 | tf_op jit(solution)/shard_map/convert_element_type | solution.py:43
  188.4 6.4 %copy.39 = bf16[1024,2048]{1,0:T(8,128)(2,1)} copy(bf16[1024,2048]{0,1:T(8,128)(2,1)} %fusion.7) | data formatting | bytes 8388608 | tf_op jit(solution)/shard_map/convert_element_type | solution.py:43
  (2 shorter events, 0.0 us)
Async XLA Ops:
  6.5 70.2 %all-gather.3.cloned.1.call-start = ((), (), s32[]{:S(2)}) async-start(), calls=%async_computation.1 | async-start | bytes 2359296 | tf_op jit(solution)/shard_map/all_gather | solution.py:28
  174.5 8.8 %copy-start = (f32[2048]{0:T(1024)S(1)}, f32[2048]{0:T(1024)}, u32[]{:S(2)}) copy-start(f32[2048]{0:T(1024)} %param.7) | copy-start | bytes 24580
Sparse Core Ops, SparseCore 0:
  26.5 50.2 all-gather.2
where the time goes:
time: 204 us; the launch traced here: 202 us
  blocking collectives  52.7 us (26%)
  local copies, waits for them, and re-layouts  50.7 us (25%)
  waiting for transfers between devices  41.3 us (20%)
  matrix products  29.2 us (14%)
  other arithmetic  14.3 us (7%)
  between operations  13.4 us (7%)
    all_to_all x1, blocking collectives, shards(): lax.all_to_all(attention, 'head', split_axis=0, concat_axis=1, tiled=True)  52.7 us
    all_gather x1, waiting for transfers between devices, shards(): lax.all_gather(total[None], 'seq', axis=0, tiled=True)  41.3 us
    dot_general x1, matrix products, shards(): jnp.einsum('nhbc,nche->nbhe', scores, value_rows, preferred_element_type=...  16.4 us
    convert_element_type x1, local copies, waits for them, and re-layouts, shards(): widened = regrouped.astype(jnp.float32)  8.75 us
    convert_element_type x1, local copies, waits for them, and re-layouts, shards(): attention = (inter + intra).astype(jnp.bfloat16).reshape(rows, width)  7.44 us
    all_to_all x1, local copies, waits for them, and re-layouts, shards(): lax.all_to_all(attention, 'head', split_axis=0, concat_axis=1, tiled=True)  7.21 us
    reshape x1, local copies, waits for them, and re-layouts, shards(): value_rows = values.reshape(blocks, BLK, heads, DH)  6.93 us
    reshape x1, local copies, waits for them, and re-layouts, shards(): key_rows = keys.reshape(blocks, BLK, heads, DH)  6.91 us
  transfers between devices with their start and end apart: 1, of which 1 were waited for; matrix products, arithmetic and copies ran while one was open for 5% of the time, Pallas kernels for 0%

commit v1 on v0

v1 whole, which is shorter than its diff:
```python
import jax
import jax.numpy as jnp
from jax import lax
from jax.experimental import pallas as pl
from jax.experimental.pallas import tpu as pltpu
from jax.sharding import PartitionSpec as P

DH = 128
BLK = 512
HALF = 256
EPS = 1e-06
VMEM = 48 * 1024 * 1024


def params():
    return pltpu.CompilerParams(vmem_limit_bytes=VMEM)


def state_kernel(k_ref, v_ref, within_ref, total_ref, acc):
    step = pl.program_id(0)

    @pl.when(step == 0)
    def _():
        acc[...] = jnp.zeros_like(acc)

    heads = acc.shape[0]
    for h in range(heads):
        cols = pl.ds(h * DH, DH)
        within_ref[0, h] = acc[h]
        acc[h] += lax.dot_general(
            k_ref[:, cols], v_ref[:, cols], (((0,), (0,)), ((), ())),
            preferred_element_type=jnp.float32,
        )

    @pl.when(step == pl.num_programs(0) - 1)
    def _():
        total_ref[...] = acc[...].astype(jnp.bfloat16)


def block_states(keys, values):
    rows, width = keys.shape
    heads, blocks = width // DH, rows // BLK
    block = pl.BlockSpec((BLK, width), lambda n: (n, 0))
    return pl.pallas_call(
        state_kernel,
        grid=(blocks,),
        in_specs=[block, block],
        out_specs=[
            pl.BlockSpec((1, heads, DH, DH), lambda n: (n, 0, 0, 0)),
            pl.BlockSpec((heads, DH, DH), lambda n: (0, 0, 0)),
        ],
        out_shape=[
            jax.ShapeDtypeStruct((blocks, heads, DH, DH), jnp.float32),
            jax.ShapeDtypeStruct((heads, DH, DH), jnp.bfloat16),
        ],
        scratch_shapes=[pltpu.VMEM((heads, DH, DH), jnp.float32)],
        compiler_params=params(),
        cost_estimate=pl.CostEstimate(
            flops=4 * rows * width * DH, bytes_accessed=4 * rows * width, transcendentals=0
        ),
        name="block_states",
    )(keys, values)


def attention_kernel(first, count, with_before, quarter_ref, q_ref, k_ref, v_ref, within_ref, *rest):
    if with_before:
        before_ref, out_ref = rest
        state = (within_ref[0, 0] + before_ref[0]).astype(jnp.bfloat16)
    else:
        (out_ref,) = rest
        state = within_ref[0, 0].astype(jnp.bfloat16)
    row = lax.broadcasted_iota(jnp.int32, (HALF, HALF), 0)
    col = lax.broadcasted_iota(jnp.int32, (HALF, HALF), 1)
    for i in range(count):
        here = pl.ds(i * HALF, HALF)
        q = q_ref[here, :]
        out = jnp.dot(q, state, preferred_element_type=jnp.float32)
        for j in range(first + i + 1):
            there = pl.ds(j * HALF, HALF)
            scores = lax.dot_general(
                q, k_ref[there, :], (((1,), (1,)), ((), ())), preferred_element_type=jnp.float32
            )
            if j == first + i:
                scores = jnp.where(row >= col, scores, 0.0)
            out += jnp.dot(
                scores.astype(jnp.bfloat16), v_ref[there, :], preferred_element_type=jnp.float32
            )
        out_ref[here, :] = out.astype(jnp.bfloat16)


def attention_rows(queries, keys, values, within, before, quarter, start, size, head, heads):
    rows, width = queries.shape
    share = rows // 4
    halves = min(size, BLK) // HALF
    first = (start % BLK) // HALF
    steps = size // (halves * HALF)
    whole = (steps, heads)
    q_block = halves * HALF
    q_base, q_quarter = start // q_block, share // q_block
    k_base, k_quarter = start // BLK, share // BLK
    k_rows = BLK if first + halves > 1 else HALF
    k_scale = BLK // k_rows
    in_specs = [
        pl.BlockSpec((q_block, DH), lambda n, h, s: (s[0] * q_quarter + q_base + n, head + h)),
        pl.BlockSpec((k_rows, DH), lambda n, h, s: ((s[0] * k_quarter + k_base + n) * k_scale, head + h)),
        pl.BlockSpec((k_rows, DH), lambda n, h, s: ((s[0] * k_quarter + k_base + n) * k_scale, head + h)),
        pl.BlockSpec((1, 1, DH, DH), lambda n, h, s: (s[0] * k_quarter + k_base + n, head + h, 0, 0)),
    ]
    operands = [queries, keys, values, within]
    if before is not None:
        in_specs.append(pl.BlockSpec((1, DH, DH), lambda n, h, s: (head + h, 0, 0)))
        operands.append(before)

    def kernel(*refs):
        attention_kernel(first, halves, before is not None, *refs)

    return pl.pallas_call(
        kernel,
        grid_spec=pltpu.PrefetchScalarGridSpec(
            num_scalar_prefetch=1,
            grid=whole,
            in_specs=in_specs,
            out_specs=pl.BlockSpec((q_block, DH), lambda n, h, s: (n, h)),
        ),
        out_shape=jax.ShapeDtypeStruct((size, heads * DH), jnp.bfloat16),
        compiler_params=params(),
        cost_estimate=pl.CostEstimate(
            flops=4 * size * heads * DH * BLK, bytes_accessed=8 * size * heads * DH, transcendentals=0
        ),
        name="attention_rows",
    )(quarter, *operands)


def norm_kernel(head_ref, gain_ref, own_ref, mate_ref, x2_ref, x3_ref, l2_ref, l3_ref, q2_ref, q3_ref,
                b2_ref, b3_ref, *rest):
    out_ref = rest[-1]
    head = head_ref[0]
    width = own_ref.shape[1]
    early = l2_ref.shape[1]
    pieces = [(own_ref[...], 0, 0), (mate_ref[...], 1, 0)]
    for partner, x_ref, l_ref, q_ref, b_ref in ((2, x2_ref, l2_ref, q2_ref, b2_ref), (3, x3_ref, l3_ref, q3_ref, b3_ref)):
        late = l_ref[...].astype(jnp.float32) + jnp.dot(
            q_ref[...], b_ref[...], preferred_element_type=jnp.float32
        )
        pieces.append((late.astype(jnp.bfloat16), partner, 0))
        pieces.append((x_ref[...], partner, early))
    total = 0.0
    for piece, _, _ in pieces:
        wide = piece.astype(jnp.float32)
        total += jnp.sum(wide * wide, axis=-1, keepdims=True)
    scale = lax.rsqrt(total / (4 * width) + EPS)
    for piece, partner, offset in pieces:
        at = pl.multiple_of((head ^ partner) * width + offset, DH)
        cols = pl.ds(at, piece.shape[1])
        out_ref[:, cols] = (piece.astype(jnp.float32) * scale * gain_ref[:, cols]).astype(jnp.bfloat16)


def norm_rows(head, gain, own, mate, x2, x3, l2, l3, q2, q3, b2, b3, start, size, out):
    share, width = own.shape
    tile = min(size, 256)
    base = start // tile
    whole = pl.BlockSpec((tile, width), lambda n, s: (base + n, 0))
    main = pl.BlockSpec((tile, x2.shape[1]), lambda n, s: (n, 0))
    early = pl.BlockSpec((tile, DH), lambda n, s: (base + n, 0))
    state = pl.BlockSpec((DH, DH), lambda n, s: (0, 0))
    in_specs = [
        pl.BlockSpec((1, 4 * width), lambda n, s: (0, 0)),
        whole, whole, main, main, early, early, early, early, state, state,
    ]
    operands = [gain, own, mate, x2, x3, l2, l3, q2, q3, b2, b3]
    aliases = {}
    if out is not None:
        in_specs.append(pl.BlockSpec(memory_space=pl.ANY))
        operands.append(out)
        aliases = {len(operands): 0}
    return pl.pallas_call(
        norm_kernel,
        grid_spec=pltpu.PrefetchScalarGridSpec(
            num_scalar_prefetch=1,
            grid=(size // tile,),
            in_specs=in_specs,
            out_specs=pl.BlockSpec((tile, 4 * width), lambda n, s: (base + n, 0)),
        ),
        out_shape=jax.ShapeDtypeStruct((share, 4 * width), jnp.bfloat16),
        input_output_aliases=aliases,
        compiler_params=params(),
        cost_estimate=pl.CostEstimate(
            flops=16 * size * width, bytes_accessed=16 * size * width, transcendentals=size
        ),
        name="norm_rows",
    )(head, *operands)


def swap(x, axis, size, bit):
    return lax.ppermute(x, axis, [(i, i ^ bit) for i in range(size)])


def sums_before(total, size):
    mine = lax.axis_index("seq")
    group = total.astype(jnp.float32)
    before = jnp.zeros_like(group)
    bit = 1
    if size % 4 == 0:
        got = [swap(total, "seq", size, k).astype(jnp.float32) for k in (1, 2, 3)]
        for k, piece in zip((1, 2, 3), got):
            before += jnp.where((mine ^ k) < mine, piece, 0.0)
            group += piece
        bit = 4
    while bit < size:
        piece = swap(group.astype(jnp.bfloat16), "seq", size, bit).astype(jnp.float32)
        before += jnp.where((mine & bit) > 0, piece, 0.0)
        group += piece
        bit *= 2
    return before


CHUNKS = ((0, 512), (512, 256), (768, 256))


def shards(seq_size, queries, keys, values, norm_gain):
    rows, width = queries.shape
    heads = width // DH
    share = rows // 4
    head = lax.axis_index("head")
    quarter = [jnp.full((1,), head ^ k, jnp.int32) for k in range(4)]

    early_q = [
        swap(lax.dynamic_slice(queries, ((head ^ k) * share, 0), (share, DH)), "head", 4, k) for k in (2, 3)
    ]
    within, total = block_states(keys, values)
    early_l = [
        swap(attention_rows(queries, keys, values, within, None, quarter[k], 0, share, 0, 1), "head", 4, k)
        for k in (2, 3)
    ]
    before = sums_before(total, seq_size)
    before_low = before[0].astype(jnp.bfloat16)
    early_b = [swap(before_low, "head", 4, k) for k in (2, 3)]
    main = []
    for start, size in CHUNKS:
        main.append([
            swap(
                attention_rows(queries, keys, values, within, before, quarter[k], start, size, 1, heads - 1),
                "head", 4, k,
            )
            for k in (2, 3)
        ])
    mate = swap(attention_rows(queries, keys, values, within, before, quarter[1], 0, share, 0, heads), "head", 4, 1)
    own = attention_rows(queries, keys, values, within, before, quarter[0], 0, share, 0, heads)
    gain = norm_gain.reshape(1, -1)
    out = None
    for (start, size), (x2, x3) in zip(CHUNKS, main):
        out = norm_rows(
            quarter[0], gain, own, mate, x2, x3, early_l[0], early_l[1], early_q[0], early_q[1],
            early_b[0], early_b[1], start, size, out,
        )
    return out


def solution(mesh):
    seq_size = mesh.shape["seq"]

    def body(queries, keys, values, norm_gain):
        return shards(seq_size, queries, keys, values, norm_gain)

    return jax.shard_map(
        body,
        mesh=mesh,
        in_specs=(P("seq", "head"), P("seq", "head"), P("seq", "head"), P()),
        out_specs=P(("seq", "head"), None),
        check_vma=False,
    )
```

time: 204 us -> 106 us (0.52)
  blocking collectives: 52.7 us -> 0 us
  Pallas kernels: 0 us -> 50.7 us
  local copies, waits for them, and re-layouts: 50.7 us -> 1.08 us
  matrix products: 29.2 us -> 0 us
  starting transfers between devices: 0.01 us -> 20.6 us
  other arithmetic: 14.3 us -> 0.17 us
  between operations: 13.4 us -> 0.16 us
  waiting for transfers between devices: 41.3 us -> 32.4 us
    all_to_all x1 -> x0, blocking collectives: 52.7 us -> none  [shards(): lax.all_to_all(attention, 'head', split_axis=0, concat_axis=1, tiled=True)]
    pallas_call x0 -> x14, Pallas kernels: none -> 50.7 us  [the longest x10 38.5 us: attention_rows(): pl.pallas_call(kernel, grid_spec=pltpu.PrefetchScalarGridSpec(num_scalar_...]
    all_gather x1 -> x0, waiting for transfers between devices: 41.3 us -> none  [shards(): lax.all_gather(total[None], 'seq', axis=0, tiled=True)]
    ppermute x0 -> x17, waiting for transfers between devices: none -> 32.4 us  [swap(): return lax.ppermute(x, axis, [(i, i ^ bit) for i in range(size)])]
    dot_general x3 -> x0, matrix products: 29.2 us -> none  [the longest x1 16.4 us: shards(): jnp.einsum('nhbc,nche->nbhe', scores, value_rows, preferred_element_type=...]
    convert_element_type x3 -> x1, local copies, waits for them, and re-layouts: 22.6 us -> 0.01 us  [shards(): before_low = before[0].astype(jnp.bfloat16)]
    reshape x3 -> x0, local copies, waits for them, and re-layouts: 20.7 us -> none  [the longest x1 6.93 us: shards(): value_rows = values.reshape(blocks, BLK, heads, DH)]
    ppermute x0 -> x17, starting transfers between devices: none -> 20.6 us  [swap(): return lax.ppermute(x, axis, [(i, i ^ bit) for i in range(size)])]
  transfers between devices with their start and end apart: 1 -> 17, of which waited for: 1 -> 7; matrix products, arithmetic and copies ran while one was open for 5% -> 1% of each run, Pallas kernels for 0% -> 32%
where the time goes in v1:
time: 106 us; the launch traced here: 105 us
  Pallas kernels  50.7 us (48%)
  waiting for transfers between devices  32.4 us (31%)
  starting transfers between devices  20.6 us (19%)
  local copies, waits for them, and re-layouts  1.08 us (1%)
    pallas_call x10, Pallas kernels, attention_rows(): pl.pallas_call(kernel, grid_spec=pltpu.PrefetchScalarGridSpec(num_scalar_...  38.5 us
    ppermute x17, waiting for transfers between devices, swap(): return lax.ppermute(x, axis, [(i, i ^ bit) for i in range(size)])  32.4 us
    ppermute x17, starting transfers between devices, swap(): return lax.ppermute(x, axis, [(i, i ^ bit) for i in range(size)])  20.6 us
    pallas_call x1, Pallas kernels, block_states(): pl.pallas_call(state_kernel, grid=(blocks,), in_specs=[block, block], out...  6.87 us
    pallas_call x3, Pallas kernels, norm_rows(): pl.pallas_call(norm_kernel, grid_spec=pltpu.PrefetchScalarGridSpec(num_sc...  5.3 us
  transfers between devices with their start and end apart: 17, of which 7 were waited for; matrix products, arithmetic and copies ran while one was open for 1% of the time, Pallas kernels for 32%

profile of v1, /device:TPU:1, one launch (start us, length us, event | category | flops | bytes accessed | tf_op | source)
XLA Modules:
  0.0 105.2 jit_solution(2370683454916756410)
XLA Ops:
  0.0 6.9 %block_states.1 = (f32[8,4,128,128]{3,2,1,0:T(8,128)S(1)}, bf16[4,128,128]{2,1,0:T(8,128)(2,1)S(1)}) custom-call(bf16[4096,512]{1,0:T(8,128)(2,1)} %refs_2_.19, bf16[4096,512]{1,0:T(8,128)(2,1)} %refs_3_.19), custom_call_target="tpu_custom_call" | custom-call | flops 1073741824 | bytes 8388608 | tf_op jit(solution)/shard_map/block_states/pallas_call | solution.py:44
  6.9 3.1 %collective-permute-start.2 = (bf16[4,128,128]{2,1,0:T(8,128)(2,1)S(1)}, bf16[4,128,128]{2,1,0:T(8,128)(2,1)S(1)}, u32[]{:S(2)}, u32[]{:S(2)}) collective-permute-start(bf16[4,128,128]{2,1,0:T(8,128)(2,1)S(1)} %get-tuple-element.8), channel_id=1, source_target_pairs={{0,12},{4,8},{8,4},{12,0},{16,28},{20,24},{24,20},{28,16},{1,13},{... | collective-permute-start | bytes 393224 | tf_op jit(solution)/shard_map/ppermute | solution.py:195
  10.0 0.2 collective-permute-start.1
  10.2 0.2 collective-permute-start
  10.4 2.9 %collective-permute-done.2 = bf16[4,128,128]{2,1,0:T(8,128)(2,1)S(1)} collective-permute-done((bf16[4,128,128]{2,1,0:T(8,128)(2,1)S(1)}, bf16[4,128,128]{2,1,0:T(8,128)(2,1)S(1)}, u32[]{:S(2)}, u32[]{:S(2)}) %collective-permute-start.2) | collective-permute-done | bytes 131104 | tf_op jit(solution)/shard_map/ppermute | solution.py:195
  13.2 2.7 %collective-permute-done.1 = bf16[4,128,128]{2,1,0:T(8,128)(2,1)S(1)} collective-permute-done((bf16[4,128,128]{2,1,0:T(8,128)(2,1)S(1)}, bf16[4,128,128]{2,1,0:T(8,128)(2,1)S(1)}, u32[]{:S(2)}, u32[]{:S(2)}) %collective-permute-start.1) | collective-permute-done | bytes 131104 | tf_op jit(solution)/shard_map/ppermute | solution.py:195
  15.9 0.2 collective-permute-done
  16.1 0.1 fusion.3
  16.2 2.4 %collective-permute-start.3 = (bf16[4,128,128]{2,1,0:T(8,128)(2,1)S(1)}, bf16[4,128,128]{2,1,0:T(8,128)(2,1)S(1)}, u32[]{:S(2)}, u32[]{:S(2)}) collective-permute-start(bf16[4,128,128]{2,1,0:T(8,128)(2,1)S(1)} %fusion.3), channel_id=1, source_target_pairs={{0,16},{4,20},{8,24},{12,28},{16,0},{20,4},{24,8},{28,12},{1,17},{... | collective-permute-start | bytes 393224 | tf_op jit(solution)/shard_map/ppermute | solution.py:195
  18.6 5.7 %collective-permute-done.3 = bf16[4,128,128]{2,1,0:T(8,128)(2,1)S(1)} collective-permute-done((bf16[4,128,128]{2,1,0:T(8,128)(2,1)S(1)}, bf16[4,128,128]{2,1,0:T(8,128)(2,1)S(1)}, u32[]{:S(2)}, u32[]{:S(2)}) %collective-permute-start.3) | collective-permute-done | bytes 131104 | tf_op jit(solution)/shard_map/ppermute | solution.py:195
  24.3 0.1 fusion.2.refs_5_
  24.4 8.3 %attention_rows.11 = bf16[1024,512]{1,0:T(8,128)(2,1)} custom-call(s32[1]{0:T(128)} %bitcast.2.refs_0_, bf16[4096,512]{1,0:T(8,128)(2,1)} %refs_1_.19, bf16[4096,512]{1,0:T(8,128)(2,1)} %refs_2_.19, bf16[4096,512]{1,0:T(8,128)(2,1)} %refs_3_.19, f32[8,4,128,128]{3,2,1,0:T(8,128)S(1)} %get-tuple-element.7.refs_4_, f32[4,128,128]{2,1,0:T(8,128)S(1)} %fusion.2.refs_5_), custom_call_target="tpu_custom_call" | custom-call | flops 1073741824 | bytes 4194304 | tf_op jit(solution)/shard_map/attention_rows/pallas_call | solution.py:117
  32.7 1.6 %collective-permute-start.4 = (bf16[1024,512]{1,0:T(8,128)(2,1)}, bf16[1024,512]{1,0:T(8,128)(2,1)S(1)}, u32[]{:S(2)}, u32[]{:S(2)}) collective-permute-start(bf16[1024,512]{1,0:T(8,128)(2,1)} %attention_rows.11), channel_id=1, source_target_pairs={{0,1},{1,0},{2,3},{3,2},{4,5},{5,4},{6,7},{7,6},{8,9},{9,8},{10,11... | collective-permute-start | bytes 3145736 | tf_op jit(solution)/shard_map/ppermute | solution.py:195
  34.3 1.1 %constant_dynamic-slice_fusion = (bf16[1024,128]{1,0:T(8,128)(2,1)S(1)}, bf16[1024,128]{1,0:T(8,128)(2,1)S(1)}) fusion(bf16[4096,512]{1,0:T(8,128)(2,1)} %refs_1_.19, s32[]{:T(128)S(6)} %select_n.41, s32[]{:T(128)S(6)} %select_n.40), kind=kLoop, calls=%fused_computation.12 | loop fusion | bytes 1048584 | tf_op jit(solution)/shard_map/dynamic_slice | solution.py:228
  35.4 1.2 %collective-permute-start.10 = (bf16[1024,128]{1,0:T(8,128)(2,1)S(1)}, bf16[1024,128]{1,0:T(8,128)(2,1)S(1)}, u32[]{:S(2)}, u32[]{:S(2)}) collective-permute-start(bf16[1024,128]{1,0:T(8,128)(2,1)S(1)} %get-tuple-element.9), channel_id=1, source_target_pairs={{0,3},{1,2},{2,1},{3,0},{4,7},{5,6},{6,5},{7,4},{8,11},{9,10},{10,... | collective-permute-start | bytes 786440 | tf_op jit(solution)/shard_map/ppermute | solution.py:195
  36.5 0.3 collective-permute-start.9
  36.8 3.4 %attention_rows.19 = bf16[512,384]{1,0:T(8,128)(2,1)S(1)} custom-call(s32[1]{0:T(128)} %bitcast.4.refs_0_, bf16[4096,512]{1,0:T(8,128)(2,1)} %refs_1_.19, bf16[4096,512]{1,0:T(8,128)(2,1)} %refs_2_.19, bf16[4096,512]{1,0:T(8,128)(2,1)} %refs_3_.19, f32[8,4,128,128]{3,2,1,0:T(8,128)S(1)} %get-tuple-element.7.refs_4_, f32[4,128,128]{2,1,0:T(8,128)S(1)} %fusion.2.refs_5_), custom_call_target="tpu_custom_call" | custom-call | flops 402653184 | bytes 1572864 | tf_op jit(solution)/shard_map/attention_rows/pallas_call | solution.py:117
  40.2 1.9 %collective-permute-start.16 = (bf16[512,384]{1,0:T(8,128)(2,1)S(1)}, bf16[512,384]{1,0:T(8,128)(2,1)S(1)}, u32[]{:S(2)}, u32[]{:S(2)}) collective-permute-start(bf16[512,384]{1,0:T(8,128)(2,1)S(1)} %attention_rows.19), channel_id=1, source_target_pairs={{0,3},{1,2},{2,1},{3,0},{4,7},{5,6},{6,5},{7,4},{8,11},{9,10},{10,... | collective-permute-start | bytes 1179656 | tf_op jit(solution)/shard_map/ppermute | solution.py:195
  42.1 3.4 %attention_rows.18 = bf16[512,384]{1,0:T(8,128)(2,1)S(1)} custom-call(s32[1]{0:T(128)} %bitcast.3.refs_0_, bf16[4096,512]{1,0:T(8,128)(2,1)} %refs_1_.19, bf16[4096,512]{1,0:T(8,128)(2,1)} %refs_2_.19, bf16[4096,512]{1,0:T(8,128)(2,1)} %refs_3_.19, f32[8,4,128,128]{3,2,1,0:T(8,128)S(1)} %get-tuple-element.7.refs_4_, f32[4,128,128]{2,1,0:T(8,128)S(1)} %fusion.2.refs_5_), custom_call_target="tpu_custom_call" | custom-call | flops 402653184 | bytes 1572864 | tf_op jit(solution)/shard_map/attention_rows/pallas_call | solution.py:117
  45.5 0.3 collective-permute-start.15
  45.9 2.4 %attention_rows.15 = bf16[1024,128]{1,0:T(8,128)(2,1)S(1)} custom-call(s32[1]{0:T(128)} %bitcast.4.refs_0_, bf16[4096,512]{1,0:T(8,128)(2,1)} %refs_1_.19, bf16[4096,512]{1,0:T(8,128)(2,1)} %refs_2_.19, bf16[4096,512]{1,0:T(8,128)(2,1)} %refs_3_.19, f32[8,4,128,128]{3,2,1,0:T(8,128)S(1)} %get-tuple-element.7.refs_4_), custom_call_target="tpu_custom_call" | custom-call | flops 268435456 | bytes 1048576 | tf_op jit(solution)/shard_map/attention_rows/pallas_call | solution.py:117
  48.2 2.4 %attention_rows.14 = bf16[1024,128]{1,0:T(8,128)(2,1)S(1)} custom-call(s32[1]{0:T(128)} %bitcast.3.refs_0_, bf16[4096,512]{1,0:T(8,128)(2,1)} %refs_1_.19, bf16[4096,512]{1,0:T(8,128)(2,1)} %refs_2_.19, bf16[4096,512]{1,0:T(8,128)(2,1)} %refs_3_.19, f32[8,4,128,128]{3,2,1,0:T(8,128)S(1)} %get-tuple-element.7.refs_4_), custom_call_target="tpu_custom_call" | custom-call | flops 268435456 | bytes 1048576 | tf_op jit(solution)/shard_map/attention_rows/pallas_call | solution.py:117
  50.6 0.0 collective-permute-done.10.q3_ref
  50.6 1.3 %collective-permute-start.7 = (bf16[1024,128]{1,0:T(8,128)(2,1)S(1)}, bf16[1024,128]{1,0:T(8,128)(2,1)S(1)}, u32[]{:S(2)}, u32[]{:S(2)}) collective-permute-start(bf16[1024,128]{1,0:T(8,128)(2,1)S(1)} %attention_rows.14), channel_id=1, source_target_pairs={{0,2},{1,3},{2,0},{3,1},{4,6},{5,7},{6,4},{7,5},{8,10},{9,11},{10,... | collective-permute-start | bytes 786440 | tf_op jit(solution)/shard_map/ppermute | solution.py:195
  51.9 0.0 collective-permute-done.9.q2_ref
  51.9 0.6 collective-permute-start.8
  52.5 2.6 %attention_rows.17 = bf16[256,384]{1,0:T(8,128)(2,1)S(1)} custom-call(s32[1]{0:T(128)} %bitcast.4.refs_0_, bf16[4096,512]{1,0:T(8,128)(2,1)} %refs_1_.19, bf16[4096,512]{1,0:T(8,128)(2,1)} %refs_2_.19, bf16[4096,512]{1,0:T(8,128)(2,1)} %refs_3_.19, f32[8,4,128,128]{3,2,1,0:T(8,128)S(1)} %get-tuple-element.7.refs_4_, f32[4,128,128]{2,1,0:T(8,128)S(1)} %fusion.2.refs_5_), custom_call_target="tpu_custom_call" | custom-call | flops 201326592 | bytes 786432 | tf_op jit(solution)/shard_map/attention_rows/pallas_call | solution.py:117
  55.2 15.9 %collective-permute-done.7.l2_ref = bf16[1024,128]{1,0:T(8,128)(2,1)S(1)} collective-permute-done((bf16[1024,128]{1,0:T(8,128)(2,1)S(1)}, bf16[1024,128]{1,0:T(8,128)(2,1)S(1)}, u32[]{:S(2)}, u32[]{:S(2)}) %collective-permute-start.7) | collective-permute-done | bytes 262176 | tf_op jit(solution)/shard_map/ppermute | solution.py:195
  71.1 2.8 %collective-permute-start.12 = (bf16[128,128]{1,0:T(8,128)(2,1)S(1)}, bf16[128,128]{1,0:T(8,128)(2,1)S(1)}, u32[]{:S(2)}, u32[]{:S(2)}) collective-permute-start(bf16[128,128]{1,0:T(8,128)(2,1)S(1)} %fusion.4), channel_id=1, source_target_pairs={{0,3},{1,2},{2,1},{3,0},{4,7},{5,6},{6,5},{7,4},{8,11},{9,10},{10,... | collective-permute-start | bytes 98312 | tf_op jit(solution)/shard_map/ppermute | solution.py:195
  73.9 3.5 %collective-permute-done.8.l3_ref = bf16[1024,128]{1,0:T(8,128)(2,1)S(1)} collective-permute-done((bf16[1024,128]{1,0:T(8,128)(2,1)S(1)}, bf16[1024,128]{1,0:T(8,128)(2,1)S(1)}, u32[]{:S(2)}, u32[]{:S(2)}) %collective-permute-start.8) | collective-permute-done | bytes 262176 | tf_op jit(solution)/shard_map/ppermute | solution.py:195
  77.4 1.2 %collective-permute-start.11 = (bf16[128,128]{1,0:T(8,128)(2,1)S(1)}, bf16[128,128]{1,0:T(8,128)(2,1)S(1)}, u32[]{:S(2)}, u32[]{:S(2)}) collective-permute-start(bf16[128,128]{1,0:T(8,128)(2,1)S(1)} %fusion.4), channel_id=1, source_target_pairs={{0,2},{1,3},{2,0},{3,1},{4,6},{5,7},{6,4},{7,5},{8,10},{9,11},{10,... | collective-permute-start | bytes 98312 | tf_op jit(solution)/shard_map/ppermute | solution.py:195
  78.6 2.6 %attention_rows.16 = bf16[256,384]{1,0:T(8,128)(2,1)S(1)} custom-call(s32[1]{0:T(128)} %bitcast.3.refs_0_, bf16[4096,512]{1,0:T(8,128)(2,1)} %refs_1_.19, bf16[4096,512]{1,0:T(8,128)(2,1)} %refs_2_.19, bf16[4096,512]{1,0:T(8,128)(2,1)} %refs_3_.19, f32[8,4,128,128]{3,2,1,0:T(8,128)S(1)} %get-tuple-element.7.refs_4_, f32[4,128,128]{2,1,0:T(8,128)S(1)} %fusion.2.refs_5_), custom_call_target="tpu_custom_call" | custom-call | flops 201326592 | bytes 786432 | tf_op jit(solution)/shard_map/attention_rows/pallas_call | solution.py:117
  81.3 3.0 %attention_rows.13 = bf16[256,384]{1,0:T(8,128)(2,1)S(1)} custom-call(s32[1]{0:T(128)} %bitcast.4.refs_0_, bf16[4096,512]{1,0:T(8,128)(2,1)} %refs_1_.19, bf16[4096,512]{1,0:T(8,128)(2,1)} %refs_2_.19, bf16[4096,512]{1,0:T(8,128)(2,1)} %refs_3_.19, f32[8,4,128,128]{3,2,1,0:T(8,128)S(1)} %get-tuple-element.7.refs_4_, f32[4,128,128]{2,1,0:T(8,128)S(1)} %fusion.2.refs_5_), custom_call_target="tpu_custom_call" | custom-call | flops 201326592 | bytes 786432 | tf_op jit(solution)/shard_map/attention_rows/pallas_call | solution.py:117
  84.3 0.0 collective-permute-done.12.b3_ref
  84.3 0.3 collective-permute-start.13
  84.6 0.0 collective-permute-done.11.b2_ref
  84.6 1.3 %collective-permute-start.14 = (bf16[256,384]{1,0:T(8,128)(2,1)S(1)}, bf16[256,384]{1,0:T(8,128)(2,1)S(1)}, u32[]{:S(2)}, u32[]{:S(2)}) collective-permute-start(bf16[256,384]{1,0:T(8,128)(2,1)S(1)} %attention_rows.17), channel_id=1, source_target_pairs={{0,3},{1,2},{2,1},{3,0},{4,7},{5,6},{6,5},{7,4},{8,11},{9,10},{10,... | collective-permute-start | bytes 589832 | tf_op jit(solution)/shard_map/ppermute | solution.py:195
  85.9 2.9 %attention_rows.12 = bf16[256,384]{1,0:T(8,128)(2,1)S(1)} custom-call(s32[1]{0:T(128)} %bitcast.3.refs_0_, bf16[4096,512]{1,0:T(8,128)(2,1)} %refs_1_.19, bf16[4096,512]{1,0:T(8,128)(2,1)} %refs_2_.19, bf16[4096,512]{1,0:T(8,128)(2,1)} %refs_3_.19, f32[8,4,128,128]{3,2,1,0:T(8,128)S(1)} %get-tuple-element.7.refs_4_, f32[4,128,128]{2,1,0:T(8,128)S(1)} %fusion.2.refs_5_), custom_call_target="tpu_custom_call" | custom-call | flops 201326592 | bytes 786432 | tf_op jit(solution)/shard_map/attention_rows/pallas_call | solution.py:117
  88.9 0.3 collective-permute-start.5
  89.2 1.6 %collective-permute-start.6 = (bf16[256,384]{1,0:T(8,128)(2,1)S(1)}, bf16[256,384]{1,0:T(8,128)(2,1)S(1)}, u32[]{:S(2)}, u32[]{:S(2)}) collective-permute-start(bf16[256,384]{1,0:T(8,128)(2,1)S(1)} %attention_rows.13), channel_id=1, source_target_pairs={{0,3},{1,2},{2,1},{3,0},{4,7},{5,6},{6,5},{7,4},{8,11},{9,10},{10,... | collective-permute-start | bytes 589832 | tf_op jit(solution)/shard_map/ppermute | solution.py:195
  90.9 7.5 %attention_rows.10.own_ref = bf16[1024,512]{1,0:T(8,128)(2,1)S(1)} custom-call(s32[1]{0:T(128)} %bitcast.refs_0_.head_ref, bf16[4096,512]{1,0:T(8,128)(2,1)} %refs_1_.19, bf16[4096,512]{1,0:T(8,128)(2,1)} %refs_2_.19, bf16[4096,512]{1,0:T(8,128)(2,1)} %refs_3_.19, f32[8,4,128,128]{3,2,1,0:T(8,128)S(1)} %get-tuple-element.7.refs_4_, ...), custom_call_target="tpu_custom_call" | custom-call | flops 1073741824 | bytes 4194304 | tf_op jit(solution)/shard_map/attention_rows/pallas_call | solution.py:117
  98.4 2.2 %norm_rows.3.rest_0_ = bf16[1024,2048]{1,0:T(8,128)(2,1)} custom-call(s32[1]{0:T(128)} %bitcast.refs_0_.head_ref, f32[1,2048]{1,0:T(1,128)S(1)} %bitcast.7, bf16[1024,512]{1,0:T(8,128)(2,1)S(1)} %attention_rows.10.own_ref, bf16[1024,512]{1,0:T(8,128)(2,1)S(1)} %collective-permute-done.4.mate_ref, bf16[512,384]{1,0:T(8,128)(2,1)S(1)} %collective-permute-done.15.x2_ref, ...), custom_call_target="tpu_custom_call" | custom-call | flops 4194304 | bytes 4194304 | tf_op jit(solution)/shard_map/norm_rows/pallas_call | solution.py:176
  100.6 0.0 collective-permute-done.13.x2_ref
  100.6 0.0 collective-permute-done.14.x3_ref
  100.6 1.6 %norm_rows.4.rest_0_ = bf16[1024,2048]{1,0:T(8,128)(2,1)} custom-call(s32[1]{0:T(128)} %bitcast.refs_0_.head_ref, f32[1,2048]{1,0:T(1,128)S(1)} %bitcast.8, bf16[1024,512]{1,0:T(8,128)(2,1)S(1)} %attention_rows.10.own_ref, bf16[1024,512]{1,0:T(8,128)(2,1)S(1)} %collective-permute-done.4.mate_ref, ...), custom_call_target="tpu_custom_call", output_to_operand_aliasing={{}: (12, {})} | custom-call | flops 2097152 | bytes 2097152 | tf_op jit(solution)/shard_map/norm_rows/pallas_call | solution.py:176
  102.2 0.0 collective-permute-done.5.x2_ref
  102.2 1.4 %collective-permute-done.6.x3_ref = bf16[256,384]{1,0:T(8,128)(2,1)S(1)} collective-permute-done((bf16[256,384]{1,0:T(8,128)(2,1)S(1)}, bf16[256,384]{1,0:T(8,128)(2,1)S(1)}, u32[]{:S(2)}, u32[]{:S(2)}) %collective-permute-start.6) | collective-permute-done | bytes 196640 | tf_op jit(solution)/shard_map/ppermute | solution.py:195
  103.6 1.6 %norm_rows.5 = bf16[1024,2048]{1,0:T(8,128)(2,1)} custom-call(s32[1]{0:T(128)} %bitcast.refs_0_.head_ref, f32[1,2048]{1,0:T(1,128)S(1)} %bitcast.9, bf16[1024,512]{1,0:T(8,128)(2,1)S(1)} %attention_rows.10.own_ref, bf16[1024,512]{1,0:T(8,128)(2,1)S(1)} %collective-permute-done.4.mate_ref, ...), custom_call_target="tpu_custom_call", output_to_operand_aliasing={{}: (12, {})} | custom-call | flops 2097152 | bytes 2097152 | tf_op jit(solution)/shard_map/norm_rows/pallas_call | solution.py:176
  (6 shorter events, 0.0 us)
Async XLA Ops:
  6.9 6.4 %collective-permute-start.2 = (bf16[4,128,128]{2,1,0:T(8,128)(2,1)S(1)}, bf16[4,128,128]{2,1,0:T(8,128)(2,1)S(1)}, u32[]{:S(2)}, u32[]{:S(2)}) collective-permute-start(bf16[4,128,128]{2,1,0:T(8,128)(2,1)S(1)} %get-tuple-element.8), channel_id=1, source_target_pairs={{0,12},{4,8},{8,4},{12,0},{16,28},{20,24},{24,20},{28,16},{1,13},{... | collective-permute-start | bytes 393224 | tf_op jit(solution)/shard_map/ppermute | solution.py:195
  10.0 5.9 %collective-permute-start.1 = (bf16[4,128,128]{2,1,0:T(8,128)(2,1)S(1)}, bf16[4,128,128]{2,1,0:T(8,128)(2,1)S(1)}, u32[]{:S(2)}, u32[]{:S(2)}) collective-permute-start(bf16[4,128,128]{2,1,0:T(8,128)(2,1)S(1)} %get-tuple-element.8), channel_id=1, source_target_pairs={{0,8},{4,12},{8,0},{12,4},{16,24},{20,28},{24,16},{28,20},{1,9},{5... | collective-permute-start | bytes 393224 | tf_op jit(solution)/shard_map/ppermute | solution.py:195
  10.2 6.0 %collective-permute-start = (bf16[4,128,128]{2,1,0:T(8,128)(2,1)S(1)}, bf16[4,128,128]{2,1,0:T(8,128)(2,1)S(1)}, u32[]{:S(2)}, u32[]{:S(2)}) collective-permute-start(bf16[4,128,128]{2,1,0:T(8,128)(2,1)S(1)} %get-tuple-element.8), channel_id=1, source_target_pairs={{0,4},{4,0},{8,12},{12,8},{16,20},{20,16},{24,28},{28,24},{1,5},{5... | collective-permute-start | bytes 393224 | tf_op jit(solution)/shard_map/ppermute | solution.py:195
  16.2 8.1 %collective-permute-start.3 = (bf16[4,128,128]{2,1,0:T(8,128)(2,1)S(1)}, bf16[4,128,128]{2,1,0:T(8,128)(2,1)S(1)}, u32[]{:S(2)}, u32[]{:S(2)}) collective-permute-start(bf16[4,128,128]{2,1,0:T(8,128)(2,1)S(1)} %fusion.3), channel_id=1, source_target_pairs={{0,16},{4,20},{8,24},{12,28},{16,0},{20,4},{24,8},{28,12},{1,17},{... | collective-permute-start | bytes 393224 | tf_op jit(solution)/shard_map/ppermute | solution.py:195
  32.7 65.7 %collective-permute-start.4 = (bf16[1024,512]{1,0:T(8,128)(2,1)}, bf16[1024,512]{1,0:T(8,128)(2,1)S(1)}, u32[]{:S(2)}, u32[]{:S(2)}) collective-permute-start(bf16[1024,512]{1,0:T(8,128)(2,1)} %attention_rows.11), channel_id=1, source_target_pairs={{0,1},{1,0},{2,3},{3,2},{4,5},{5,4},{6,7},{7,6},{8,9},{9,8},{10,11... | collective-permute-start | bytes 3145736 | tf_op jit(solution)/shard_map/ppermute | solution.py:195
  35.4 15.2 %collective-permute-start.10 = (bf16[1024,128]{1,0:T(8,128)(2,1)S(1)}, bf16[1024,128]{1,0:T(8,128)(2,1)S(1)}, u32[]{:S(2)}, u32[]{:S(2)}) collective-permute-start(bf16[1024,128]{1,0:T(8,128)(2,1)S(1)} %get-tuple-element.9), channel_id=1, source_target_pairs={{0,3},{1,2},{2,1},{3,0},{4,7},{5,6},{6,5},{7,4},{8,11},{9,10},{10,... | collective-permute-start | bytes 786440 | tf_op jit(solution)/shard_map/ppermute | solution.py:195
  36.5 15.4 %collective-permute-start.9 = (bf16[1024,128]{1,0:T(8,128)(2,1)S(1)}, bf16[1024,128]{1,0:T(8,128)(2,1)S(1)}, u32[]{:S(2)}, u32[]{:S(2)}) collective-permute-start(bf16[1024,128]{1,0:T(8,128)(2,1)S(1)} %get-tuple-element.10), channel_id=1, source_target_pairs={{0,2},{1,3},{2,0},{3,1},{4,6},{5,7},{6,4},{7,5},{8,10},{9,11},{10,... | collective-permute-start | bytes 786440 | tf_op jit(solution)/shard_map/ppermute | solution.py:195
  40.2 48.7 %collective-permute-start.16 = (bf16[512,384]{1,0:T(8,128)(2,1)S(1)}, bf16[512,384]{1,0:T(8,128)(2,1)S(1)}, u32[]{:S(2)}, u32[]{:S(2)}) collective-permute-start(bf16[512,384]{1,0:T(8,128)(2,1)S(1)} %attention_rows.19), channel_id=1, source_target_pairs={{0,3},{1,2},{2,1},{3,0},{4,7},{5,6},{6,5},{7,4},{8,11},{9,10},{10,... | collective-permute-start | bytes 1179656 | tf_op jit(solution)/shard_map/ppermute | solution.py:195
  45.5 43.7 %collective-permute-start.15 = (bf16[512,384]{1,0:T(8,128)(2,1)S(1)}, bf16[512,384]{1,0:T(8,128)(2,1)S(1)}, u32[]{:S(2)}, u32[]{:S(2)}) collective-permute-start(bf16[512,384]{1,0:T(8,128)(2,1)S(1)} %attention_rows.18), channel_id=1, source_target_pairs={{0,2},{1,3},{2,0},{3,1},{4,6},{5,7},{6,4},{7,5},{8,10},{9,11},{10,... | collective-permute-start | bytes 1179656 | tf_op jit(solution)/shard_map/ppermute | solution.py:195
  50.6 20.5 %collective-permute-start.7 = (bf16[1024,128]{1,0:T(8,128)(2,1)S(1)}, bf16[1024,128]{1,0:T(8,128)(2,1)S(1)}, u32[]{:S(2)}, u32[]{:S(2)}) collective-permute-start(bf16[1024,128]{1,0:T(8,128)(2,1)S(1)} %attention_rows.14), channel_id=1, source_target_pairs={{0,2},{1,3},{2,0},{3,1},{4,6},{5,7},{6,4},{7,5},{8,10},{9,11},{10,... | collective-permute-start | bytes 786440 | tf_op jit(solution)/shard_map/ppermute | solution.py:195
  51.9 25.5 %collective-permute-start.8 = (bf16[1024,128]{1,0:T(8,128)(2,1)S(1)}, bf16[1024,128]{1,0:T(8,128)(2,1)S(1)}, u32[]{:S(2)}, u32[]{:S(2)}) collective-permute-start(bf16[1024,128]{1,0:T(8,128)(2,1)S(1)} %attention_rows.15), channel_id=1, source_target_pairs={{0,3},{1,2},{2,1},{3,0},{4,7},{5,6},{6,5},{7,4},{8,11},{9,10},{10,... | collective-permute-start | bytes 786440 | tf_op jit(solution)/shard_map/ppermute | solution.py:195
  71.1 13.2 %collective-permute-start.12 = (bf16[128,128]{1,0:T(8,128)(2,1)S(1)}, bf16[128,128]{1,0:T(8,128)(2,1)S(1)}, u32[]{:S(2)}, u32[]{:S(2)}) collective-permute-start(bf16[128,128]{1,0:T(8,128)(2,1)S(1)} %fusion.4), channel_id=1, source_target_pairs={{0,3},{1,2},{2,1},{3,0},{4,7},{5,6},{6,5},{7,4},{8,11},{9,10},{10,... | collective-permute-start | bytes 98312 | tf_op jit(solution)/shard_map/ppermute | solution.py:195
  77.4 7.2 %collective-permute-start.11 = (bf16[128,128]{1,0:T(8,128)(2,1)S(1)}, bf16[128,128]{1,0:T(8,128)(2,1)S(1)}, u32[]{:S(2)}, u32[]{:S(2)}) collective-permute-start(bf16[128,128]{1,0:T(8,128)(2,1)S(1)} %fusion.4), channel_id=1, source_target_pairs={{0,2},{1,3},{2,0},{3,1},{4,6},{5,7},{6,4},{7,5},{8,10},{9,11},{10,... | collective-permute-start | bytes 98312 | tf_op jit(solution)/shard_map/ppermute | solution.py:195
  84.3 16.3 %collective-permute-start.13 = (bf16[256,384]{1,0:T(8,128)(2,1)S(1)}, bf16[256,384]{1,0:T(8,128)(2,1)S(1)}, u32[]{:S(2)}, u32[]{:S(2)}) collective-permute-start(bf16[256,384]{1,0:T(8,128)(2,1)S(1)} %attention_rows.16), channel_id=1, source_target_pairs={{0,2},{1,3},{2,0},{3,1},{4,6},{5,7},{6,4},{7,5},{8,10},{9,11},{10,... | collective-permute-start | bytes 589832 | tf_op jit(solution)/shard_map/ppermute | solution.py:195
  84.6 16.0 %collective-permute-start.14 = (bf16[256,384]{1,0:T(8,128)(2,1)S(1)}, bf16[256,384]{1,0:T(8,128)(2,1)S(1)}, u32[]{:S(2)}, u32[]{:S(2)}) collective-permute-start(bf16[256,384]{1,0:T(8,128)(2,1)S(1)} %attention_rows.17), channel_id=1, source_target_pairs={{0,3},{1,2},{2,1},{3,0},{4,7},{5,6},{6,5},{7,4},{8,11},{9,10},{10,... | collective-permute-start | bytes 589832 | tf_op jit(solution)/shard_map/ppermute | solution.py:195
  88.9 13.3 %collective-permute-start.5 = (bf16[256,384]{1,0:T(8,128)(2,1)S(1)}, bf16[256,384]{1,0:T(8,128)(2,1)S(1)}, u32[]{:S(2)}, u32[]{:S(2)}) collective-permute-start(bf16[256,384]{1,0:T(8,128)(2,1)S(1)} %attention_rows.12), channel_id=1, source_target_pairs={{0,2},{1,3},{2,0},{3,1},{4,6},{5,7},{6,4},{7,5},{8,10},{9,11},{10,... | collective-permute-start | bytes 589832 | tf_op jit(solution)/shard_map/ppermute | solution.py:195
  89.2 14.4 %collective-permute-start.6 = (bf16[256,384]{1,0:T(8,128)(2,1)S(1)}, bf16[256,384]{1,0:T(8,128)(2,1)S(1)}, u32[]{:S(2)}, u32[]{:S(2)}) collective-permute-start(bf16[256,384]{1,0:T(8,128)(2,1)S(1)} %attention_rows.13), channel_id=1, source_target_pairs={{0,3},{1,2},{2,1},{3,0},{4,7},{5,6},{6,5},{7,4},{8,11},{9,10},{10,... | collective-permute-start | bytes 589832 | tf_op jit(solution)/shard_map/ppermute | solution.py:195
  90.9 7.5 %copy-start = (f32[2048]{0:T(1024)S(1)}, f32[2048]{0:T(1024)}, u32[]{:S(2)}) copy-start(f32[2048]{0:T(1024)} %param.7) | copy-start | bytes 24580

commit v2 on v0

v2 whole, which is shorter than its diff:
```python
import functools

import jax
import jax.numpy as jnp
from jax import lax
from jax.experimental import pallas as pl
from jax.experimental.pallas import tpu as pltpu
from jax.sharding import PartitionSpec as P

DH = 128
BLK = 512
HALF = 256
EXTRA = 48
EPS = 1e-06
COST = pl.CostEstimate(flops=1024, bytes_accessed=1024, transcendentals=0)
LONG = pl.CostEstimate(flops=10**12, bytes_accessed=1024, transcendentals=0)


def params(mib=50):
    return pltpu.CompilerParams(vmem_limit_bytes=mib * 1024 * 1024)


def state_kernel(parts, tokens, head_ref, k_ref, v_ref, q2_ref, q3_ref, *rest):
    within_ref, total_ref, *rest = rest[tokens:]
    outs, (k_buf, v_buf, k_sem, v_sem) = rest[:-4], rest[-4:]
    rows, width = k_buf.shape
    heads, part, share = width // DH, rows // parts, rows // 4
    copies = []
    for p in range(parts):
        at = pl.ds(p * part, part)
        pair = (
            pltpu.make_async_copy(k_ref.at[at], k_buf.at[at], k_sem.at[p]),
            pltpu.make_async_copy(v_ref.at[at], v_buf.at[at], v_sem.at[p]),
        )
        for copy in pair:
            copy.start()
        copies.append(pair)
    acc = [jnp.zeros((DH, DH), jnp.float32) for _ in range(heads)]
    for p in range(parts):
        for copy in copies[p]:
            copy.wait()
        for n in range(p * part // BLK, (p + 1) * part // BLK):
            at = pl.ds(n * BLK, BLK)
            for h in range(heads):
                cols = pl.ds(h * DH, DH)
                within_ref[n, h] = acc[h]
                acc[h] = acc[h] + lax.dot_general(
                    k_buf[at, cols], v_buf[at, cols], (((0,), (0,)), ((), ())),
                    preferred_element_type=jnp.float32,
                )
    for h in range(heads):
        total_ref[h] = acc[h].astype(jnp.bfloat16)
    blocks = share // BLK
    cols = pl.ds(width - DH, DH)
    for side, q_ref in ((2, q2_ref), (3, q3_ref)):
        for n in range(blocks):
            block = (head_ref[0] ^ side) * blocks + n
            at = pl.ds(pl.multiple_of(block * BLK, BLK), BLK)
            attend(
                0, BLK // HALF, 1, q_ref.at[pl.ds(n * BLK, BLK)], k_buf.at[at, cols], v_buf.at[at, cols],
                within_ref.at[pl.ds(block, 1), pl.ds(heads - 1, 1)], None, outs[(side - 2) * blocks + n],
            )


def block_states(head, keys, values, slices, *tokens):
    rows, width = keys.shape
    heads, blocks = width // DH, rows // BLK
    parts = 4 if blocks % 4 == 0 else 1
    anywhere = pl.BlockSpec(memory_space=pl.ANY)
    vmem = pl.BlockSpec(memory_space=pltpu.VMEM)
    pieces = 2 * (blocks // 4)
    return pl.pallas_call(
        functools.partial(state_kernel, parts, len(tokens)),
        in_specs=[pl.BlockSpec(memory_space=pltpu.SMEM), anywhere, anywhere, vmem, vmem] + [anywhere] * len(tokens),
        out_specs=[vmem] * (2 + pieces),
        out_shape=[
            jax.ShapeDtypeStruct((blocks, heads, DH, DH), jnp.float32),
            jax.ShapeDtypeStruct((heads, DH, DH), jnp.bfloat16),
        ] + [jax.ShapeDtypeStruct((BLK, DH), jnp.bfloat16)] * pieces,
        scratch_shapes=[
            pltpu.VMEM((rows, width), jnp.bfloat16),
            pltpu.VMEM((rows, width), jnp.bfloat16),
            pltpu.SemaphoreType.DMA((parts,)),
            pltpu.SemaphoreType.DMA((parts,)),
        ],
        compiler_params=params(62),
        cost_estimate=COST,
        name="block_states",
    )(head, keys, values, *slices, *tokens)


def attend(first, halves, heads, q_ref, k_ref, v_ref, within_ref, before_ref, out_ref):
    row = lax.broadcasted_iota(jnp.int32, (HALF, HALF), 0)
    col = lax.broadcasted_iota(jnp.int32, (HALF, HALF), 1)
    for h in range(heads):
        cols = pl.ds(h * DH, DH)
        state = within_ref[0, h]
        if before_ref is not None:
            state = state + before_ref[h]
        q = q_ref[:, cols]
        out = jnp.dot(q, state.astype(jnp.bfloat16), preferred_element_type=jnp.float32)
        outs = [out[i * HALF:(i + 1) * HALF] for i in range(halves)]
        for j in range(first + halves):
            start = max(j - first, 0)
            there = pl.ds(j * HALF, HALF)
            scores = lax.dot_general(
                q[start * HALF:], k_ref[there, cols], (((1,), (1,)), ((), ())),
                preferred_element_type=jnp.float32,
            )
            low = []
            for i in range(start, halves):
                piece = scores[(i - start) * HALF:(i - start + 1) * HALF]
                if first + i == j:
                    piece = jnp.where(row >= col, piece, 0.0)
                low.append(piece.astype(jnp.bfloat16))
            low = jnp.concatenate(low, axis=0) if len(low) > 1 else low[0]
            more = jnp.dot(low, v_ref[there, cols], preferred_element_type=jnp.float32)
            for i in range(start, halves):
                outs[i] = outs[i] + more[(i - start) * HALF:(i - start + 1) * HALF]
        for i in range(halves):
            out_ref[pl.ds(i * HALF, HALF), cols] = outs[i].astype(out_ref.dtype)


def attention_rows(arrays, before, at, sides, start, size, head, heads, kind, tokens, cost=None):
    queries, keys, values, within = arrays
    rows, width = queries.shape
    share = rows // 4
    halves = size // HALF
    first = (start % BLK) // HALF
    k_rows = BLK if first + halves > 1 else HALF
    span = heads * DH
    across = head // heads
    count = len(sides)

    def quarter(n, s):
        side = sides[0]
        for i in range(1, count):
            side = jnp.where(n == i, sides[i], side)
        return s[0] ^ side

    def block(n, s):
        return quarter(n, s) * (share // BLK) + start // BLK

    keys_spec = pl.BlockSpec((k_rows, span), lambda n, s: (block(n, s) * (BLK // k_rows), across))
    in_specs = [
        pl.BlockSpec((size, span), lambda n, s: (quarter(n, s) * (share // size) + start // size, across)),
        keys_spec,
        keys_spec,
        pl.BlockSpec((1, heads, DH, DH), lambda n, s: (block(n, s), across, 0, 0)),
    ]
    operands = [queries, keys, values, within]
    if before is not None:
        in_specs.append(pl.BlockSpec(before.shape, lambda n, s: (0, 0, 0)))
        operands.append(before)
    in_specs += [pl.BlockSpec(memory_space=pl.ANY)] * len(tokens)

    def kernel(ids_ref, q_ref, k_ref, v_ref, within_ref, *rest):
        before_ref = None if before is None else rest[0]
        outs = rest[len(rest) - count:]
        for n in range(count):
            @pl.when(pl.program_id(0) == n)
            def _(n=n):
                attend(first, halves, heads, q_ref, k_ref, v_ref, within_ref, before_ref, outs[n])

    return pl.pallas_call(
        kernel,
        grid_spec=pltpu.PrefetchScalarGridSpec(
            num_scalar_prefetch=1,
            grid=(count,),
            in_specs=in_specs,
            out_specs=[pl.BlockSpec((size, span), lambda n, s: (0, 0))] * count,
        ),
        out_shape=[jax.ShapeDtypeStruct((size, span), kind)] * count,
        compiler_params=params(),
        cost_estimate=COST if cost is None else cost,
        name="attention_rows",
    )(at, *operands, *tokens)


def attention_quarter(arrays, before, at, side, kind, tokens):
    queries, keys, values, within = arrays
    rows, width = queries.shape
    share = rows // 4
    heads, blocks = width // DH, share // BLK
    block = pl.BlockSpec((BLK, width), lambda n, s: ((s[0] ^ side) * blocks + n, 0))
    state = pl.BlockSpec((1, heads, DH, DH), lambda n, s: ((s[0] ^ side) * blocks + n, 0, 0, 0))
    in_specs = [block, block, block, state]
    operands = [queries, keys, values, within]
    if before is not None:
        in_specs.append(pl.BlockSpec(before.shape, lambda n, s: (0, 0, 0)))
        operands.append(before)
    in_specs += [pl.BlockSpec(memory_space=pl.ANY)] * len(tokens)

    def kernel(quarter_ref, q_ref, k_ref, v_ref, within_ref, *rest):
        before_ref = None if before is None else rest[0]
        attend(0, BLK // HALF, heads, q_ref, k_ref, v_ref, within_ref, before_ref, rest[-1])

    return pl.pallas_call(
        kernel,
        grid_spec=pltpu.PrefetchScalarGridSpec(
            num_scalar_prefetch=1,
            grid=(blocks,),
            in_specs=in_specs,
            out_specs=pl.BlockSpec((BLK, width), lambda n, s: (n, 0)),
        ),
        out_shape=jax.ShapeDtypeStruct((share, width), kind),
        compiler_params=params(),
        cost_estimate=COST,
        name="attention_quarter",
    )(at, *operands, *tokens)


def late_kernel(count, heads, embed, ids_ref, *refs):
    before_ref = refs[2 * count]
    outs = refs[len(refs) - count:]
    for n in range(count):
        q_ref, local_ref, out_ref = refs[2 * n], refs[2 * n + 1], outs[n]
        size = q_ref.shape[0]
        for h in range(heads):
            cols = pl.ds(h * DH, DH)
            out = local_ref[:, cols] + jnp.dot(
                q_ref[:, cols], before_ref[h].astype(jnp.bfloat16), preferred_element_type=jnp.float32
            )
            out_ref[pl.ds(0, size), cols] = out.astype(jnp.bfloat16)
        if embed:
            low = before_ref[heads].astype(jnp.bfloat16)
            for c in range(heads):
                high = min((c + 1) * EXTRA, DH)
                out_ref[pl.ds(size, high - c * EXTRA), pl.ds(c * DH, DH)] = low[c * EXTRA:high]


def late_rows(queries, before, at, sides, locals_, heads, embed, tokens):
    count = len(sides)
    size, span = locals_[0].shape
    steps = 1 if embed else size // BLK
    rows = size // steps
    share = queries.shape[0] // 4
    in_specs, operands = [], []
    for n in range(count):
        in_specs.append(pl.BlockSpec((rows, span), lambda i, s, side=sides[n]: ((s[0] ^ side) * (share // rows) + i, 0)))
        in_specs.append(pl.BlockSpec((rows, span), lambda i, s: (i, 0)))
        operands += [queries, locals_[n]]
    in_specs.append(pl.BlockSpec(before.shape, lambda i, s: (0, 0, 0)))
    in_specs += [pl.BlockSpec(memory_space=pl.ANY)] * len(tokens)
    more = EXTRA if embed else 0
    return pl.pallas_call(
        functools.partial(late_kernel, count, heads, embed),
        grid_spec=pltpu.PrefetchScalarGridSpec(
            num_scalar_prefetch=1,
            grid=(steps,),
            in_specs=in_specs,
            out_specs=[pl.BlockSpec((rows + more, span), lambda i, s: (i, 0))] * count,
        ),
        out_shape=[jax.ShapeDtypeStruct((size + more, span), jnp.bfloat16)] * count,
        compiler_params=params(),
        cost_estimate=COST,
        name="late_rows",
    )(at, *operands, before, *tokens)


def norm_kernel(head_ref, gain_ref, own_ref, mate_ref, x2_ref, x3_ref, l2_ref, l3_ref, q2_ref, q3_ref,
                b2_ref, b3_ref, *rest):
    out_ref = rest[-1]
    head = head_ref[0]
    tile, width = own_ref.shape
    pieces = [(own_ref[...], 0, 0), (mate_ref[...], 1, 0)]
    sides = ((2, x2_ref, l2_ref, q2_ref, b2_ref), (3, x3_ref, l3_ref, q3_ref, b3_ref))
    for partner, x_ref, l_ref, q_ref, b_ref in sides:
        base = b_ref.shape[0] - EXTRA
        parts = []
        for c in range(b_ref.shape[1] // DH):
            high = min((c + 1) * EXTRA, DH)
            parts.append(b_ref[pl.ds(base, high - c * EXTRA), pl.ds(c * DH, DH)])
        state = jnp.concatenate(parts, axis=0)
        late = l_ref[...].astype(jnp.float32) + jnp.dot(q_ref[...], state, preferred_element_type=jnp.float32)
        pieces.append((x_ref[...], partner, 0))
        pieces.append((late.astype(jnp.bfloat16), partner, width - DH))
    total = 0.0
    for piece, _, _ in pieces:
        wide = piece.astype(jnp.float32)
        total += jnp.sum(wide * wide, axis=-1, keepdims=True)
    scale = lax.rsqrt(total / (4 * width) + EPS)
    for piece, partner, offset in pieces:
        at = pl.multiple_of((head ^ partner) * width + offset, DH)
        cols = pl.ds(at, piece.shape[1])
        out_ref[:, cols] = (piece.astype(jnp.float32) * scale * gain_ref[:, cols]).astype(jnp.bfloat16)


def norm_rows(head, gain, share, row, own, mate, x2, x3, l2, l3, q2, q3, b2, b3, out):
    def at(pair, cols):
        index = pair[1] // HALF
        return pl.BlockSpec((HALF, cols), lambda n, s: (index, 0))

    def full(array):
        return pl.BlockSpec(array.shape, lambda n, s: (0, 0))

    width = own[0].shape[1]
    in_specs = [full(gain), at(own, width), at(mate, width), at(x2, width - DH), at(x3, width - DH)]
    in_specs += [at(l2, DH), at(l3, DH), at(q2, DH), at(q3, DH), full(b2), full(b3)]
    operands = [gain, own[0], mate[0], x2[0], x3[0], l2[0], l3[0], q2[0], q3[0], b2, b3]
    aliases = {}
    if out is not None:
        in_specs.append(pl.BlockSpec(memory_space=pl.ANY))
        operands.append(out)
        aliases = {len(operands): 0}
    index = row // HALF
    return pl.pallas_call(
        norm_kernel,
        grid_spec=pltpu.PrefetchScalarGridSpec(
            num_scalar_prefetch=1,
            grid=(1,),
            in_specs=in_specs,
            out_specs=pl.BlockSpec((HALF, 4 * width), lambda n, s: (index, 0)),
        ),
        out_shape=jax.ShapeDtypeStruct((share, 4 * width), jnp.bfloat16),
        input_output_aliases=aliases,
        compiler_params=params(),
        cost_estimate=COST,
        name="norm_rows",
    )(head, *operands)


def add_kernel(bit, with_before, mine_ref, total_ref, got_ref, *rest):
    group_ref, after_ref = rest[-2:]
    got = got_ref[...].astype(jnp.float32)
    late = jnp.where((mine_ref[0] & bit) > 0, got, 0.0)
    if with_before:
        late = late + rest[0][...]
    after_ref[...] = late
    group_ref[...] = (total_ref[...].astype(jnp.float32) + got).astype(jnp.bfloat16)


def add_step(mine, bit, total, got, before, tokens):
    vmem = pl.BlockSpec(memory_space=pltpu.VMEM)
    states = [total, got] + ([] if before is None else [before])
    return pl.pallas_call(
        functools.partial(add_kernel, bit, before is not None),
        in_specs=[pl.BlockSpec(memory_space=pltpu.SMEM)] + [vmem] * len(states)
        + [pl.BlockSpec(memory_space=pl.ANY)] * len(tokens),
        out_specs=[vmem, vmem],
        out_shape=[
            jax.ShapeDtypeStruct(total.shape, jnp.bfloat16),
            jax.ShapeDtypeStruct(total.shape, jnp.float32),
        ],
        compiler_params=params(),
        cost_estimate=COST,
        name="add_step",
    )(mine, *states, *tokens)


def swap(x, axis, size, bit):
    return lax.ppermute(x, axis, [(i, i ^ bit) for i in range(size)])


def across(pair):
    return [swap(x, "head", 4, k) for x, k in zip(pair, (2, 3))]


def shards(seq_size, queries, keys, values, norm_gain):
    rows, width = queries.shape
    heads = width // DH
    share = rows // 4
    units = share // HALF
    head = lax.axis_index("head")
    at = jnp.full((1,), head, jnp.int32)
    mine = jnp.full((1,), lax.axis_index("seq"), jnp.int32)
    gain = norm_gain.reshape(1, -1)
    far = (2, 3)

    slices = [lax.dynamic_slice(queries, ((head ^ k) * share, width - DH), (share, DH)) for k in far]
    early_q = across(slices)
    within, total, *early = block_states(at, keys, values, slices)
    early_l = [across([early[n], early[n + share // BLK]]) for n in range(share // BLK)]
    arrays = (queries, keys, values, within)
    group, before, bit, step = total, None, 1, 0
    while bit < seq_size:
        got = swap(group, "seq", seq_size, bit)
        tokens = []
        if step == 0:
            first = attention_rows(arrays, None, at, far, 0, BLK, 0, heads - 1, jnp.float32, [group])
            tokens = [*first, *early_q]
        elif step == 1:
            mate = attention_quarter(arrays, None, at, 1, jnp.float32, [group])
            tokens = [mate, *early_l[0]]
        elif step == 2:
            tokens = [*early_l[1]]
        group, before = add_step(mine, bit, group, got, before, tokens)
        bit, step = bit * 2, step + 1

    def far_unit(i, tokens, cost=None):
        return attention_rows(
            arrays, before, at, far, i * HALF, HALF, 0, heads - 1, jnp.bfloat16, tokens, cost
        )

    one = late_rows(queries, before, at, far, first, heads - 1, True, [])
    x1 = across(one)
    (mate,) = late_rows(queries, before, at, (1,), [mate], heads, False, one)
    mated = swap(mate, "head", 4, 1)
    two = far_unit(2, [mate])
    x2 = across(two)
    three = far_unit(3, [*two, *x1], LONG)
    x3 = across(three)
    own = attention_quarter(arrays, before, at, 0, jnp.bfloat16, three)
    x = [[(y, 0) for y in x1], [(y, HALF) for y in x1], [(y, 0) for y in x2], [(y, 0) for y in x3]]
    out = None
    for i in range(units):
        block, row = i * HALF // BLK, i * HALF % BLK
        out = norm_rows(
            at, gain, share, i * HALF, (own, i * HALF), (mated, i * HALF),
            x[i][0], x[i][1], (early_l[block][0], row), (early_l[block][1], row),
            (early_q[0], i * HALF), (early_q[1], i * HALF), x1[0], x1[1], out,
        )
    return out


def solution(mesh):
    seq_size = mesh.shape["seq"]

    def body(queries, keys, values, norm_gain):
        return shards(seq_size, queries, keys, values, norm_gain)

    return jax.shard_map(
        body,
        mesh=mesh,
        in_specs=(P("seq", "head"), P("seq", "head"), P("seq", "head"), P()),
        out_specs=P(("seq", "head"), None),
        check_vma=False,
    )
```

time: 204 us -> 81.5 us (0.40)
  blocking collectives: 52.7 us -> 0 us
  local copies, waits for them, and re-layouts: 50.7 us -> 3.59 us
  Pallas kernels: 0 us -> 41.3 us
  matrix products: 29.2 us -> 0 us
  waiting for transfers between devices: 41.3 us -> 18.1 us
  starting transfers between devices: 0.01 us -> 17.4 us
  other arithmetic: 14.3 us -> 0 us
  between operations: 13.4 us -> 0.21 us
    all_to_all x1 -> x0, blocking collectives: 52.7 us -> none  [shards(): lax.all_to_all(attention, 'head', split_axis=0, concat_axis=1, tiled=True)]
    all_gather x1 -> x0, waiting for transfers between devices: 41.3 us -> none  [shards(): lax.all_gather(total[None], 'seq', axis=0, tiled=True)]
    pallas_call x0 -> x15, Pallas kernels: none -> 41.3 us  [the longest x4 10.2 us: norm_rows(): pl.pallas_call(norm_kernel, grid_spec=pltpu.PrefetchScalarGridSpec(num_sc...]
    dot_general x3 -> x0, matrix products: 29.2 us -> none  [the longest x1 16.4 us: shards(): jnp.einsum('nhbc,nche->nbhe', scores, value_rows, preferred_element_type=...]
    convert_element_type x3 -> x0, local copies, waits for them, and re-layouts: 22.6 us -> none  [the longest x1 8.75 us: shards(): widened = regrouped.astype(jnp.float32)]
    reshape x3 -> x0, local copies, waits for them, and re-layouts: 20.7 us -> none  [the longest x1 6.93 us: shards(): value_rows = values.reshape(blocks, BLK, heads, DH)]
    ppermute x0 -> x16, waiting for transfers between devices: none -> 18.1 us  [swap(): return lax.ppermute(x, axis, [(i, i ^ bit) for i in range(size)])]
    ppermute x0 -> x16, starting transfers between devices: none -> 17.4 us  [swap(): return lax.ppermute(x, axis, [(i, i ^ bit) for i in range(size)])]
  transfers between devices with their start and end apart: 1 -> 16, of which waited for: 1 -> 3; matrix products, arithmetic and copies ran while one was open for 5% -> 0% of each run, Pallas kernels for 0% -> 45%
where the time goes in v2:
time: 81.5 us; the launch traced here: 80.6 us
  Pallas kernels  41.3 us (51%)
  waiting for transfers between devices  18.1 us (22%)
  starting transfers between devices  17.4 us (21%)
  local copies, waits for them, and re-layouts  3.59 us (4%)
    ppermute x16, waiting for transfers between devices, swap(): return lax.ppermute(x, axis, [(i, i ^ bit) for i in range(size)])  18.1 us
    ppermute x16, starting transfers between devices, swap(): return lax.ppermute(x, axis, [(i, i ^ bit) for i in range(size)])  17.4 us
    pallas_call x4, Pallas kernels, norm_rows(): pl.pallas_call(norm_kernel, grid_spec=pltpu.PrefetchScalarGridSpec(num_sc...  10.2 us
    pallas_call x3, Pallas kernels, attention_rows(): pl.pallas_call(kernel, grid_spec=pltpu.PrefetchScalarGridSpec(num_scalar_...  10.1 us
    pallas_call x2, Pallas kernels, attention_quarter(): pl.pallas_call(kernel, grid_spec=pltpu.PrefetchScalarGridSpec(num_scalar_...  8.84 us
    pallas_call x1, Pallas kernels, block_states(): pl.pallas_call(functools.partial(state_kernel, parts, len(tokens)), in_sp...  6.92 us
    pallas_call x2, Pallas kernels, late_rows(): pl.pallas_call(functools.partial(late_kernel, count, heads, embed), grid_...  4.41 us
    unnamed x18, local copies, waits for them, and re-layouts  2.52 us
  transfers between devices with their start and end apart: 16, of which 3 were waited for; matrix products, arithmetic and copies ran while one was open for 0% of the time, Pallas kernels for 45%

profile of v2, /device:TPU:1, one launch (start us, length us, event | category | flops | bytes accessed | tf_op | source)
XLA Modules:
  0.0 80.6 jit_solution(5985947224905552242)
XLA Ops:
  0.0 1.1 %constant_dynamic-slice_fusion = (bf16[1024,128]{1,0:T(8,128)(2,1)S(1)}, bf16[1024,128]{1,0:T(8,128)(2,1)S(1)}) fusion(bf16[4096,512]{1,0:T(8,128)(2,1)} %q_ref.9, s32[]{:T(128)S(6)} %select_n.7, s32[]{:T(128)S(6)} %select_n.6), kind=kLoop, calls=%fused_computation | loop fusion | bytes 1048584 | tf_op jit(solution)/shard_map/dynamic_slice | solution.py:370
  1.1 2.7 %collective-permute-start.2 = (bf16[1024,128]{1,0:T(8,128)(2,1)S(1)}, bf16[1024,128]{1,0:T(8,128)(2,1)S(1)}, u32[]{:S(2)}, u32[]{:S(2)}) collective-permute-start(bf16[1024,128]{1,0:T(8,128)(2,1)S(1)} %get-tuple-element.43.q3_ref), channel_id=1, source_target_pairs={{0,3},{1,2},{2,1},{3,0},{4,7},{5,6},{6,5},{7,4},{8,11},{9,10},{10,... | collective-permute-start | bytes 786440 | tf_op jit(solution)/shard_map/ppermute | solution.py:352
  3.8 0.0 collective-permute-start.1
  3.8 6.9 %block_states.1 = (f32[8,4,128,128]{3,2,1,0:T(8,128)}, bf16[4,128,128]{2,1,0:T(8,128)(2,1)}, bf16[512,128]{1,0:T(8,128)(2,1)}, bf16[512,128]{1,0:T(8,128)(2,1)},...) custom-call(s32[1]{0:T(128)} %bitcast.head_ref.ids_ref.quarter_ref, bf16[4096,512]{1,0:T(8,128)(2,1)} %k_ref.11, ...), custom_call_target="tpu_custom_call" | custom-call | flops 1024 | bytes 1024 | tf_op jit(solution)/shard_map/block_states/pallas_call | solution.py:72
  10.7 1.5 %collective-permute-start = (bf16[4,128,128]{2,1,0:T(8,128)(2,1)}, bf16[4,128,128]{2,1,0:T(8,128)(2,1)S(1)}, u32[]{:S(2)}, u32[]{:S(2)}) collective-permute-start(bf16[4,128,128]{2,1,0:T(8,128)(2,1)} %get-tuple-element.25.rest_0_.total_ref), channel_id=1, source_target_pairs={{0,4},{4,0},{8,12},{12,8},{16,20},{20,16},{24,28},{28,24},{1,5},{5... | collective-permute-start | bytes 393224 | tf_op jit(solution)/shard_map/ppermute | solution.py:352
  12.2 1.2 %collective-permute-start.4 = (bf16[512,128]{1,0:T(8,128)(2,1)}, bf16[512,128]{1,0:T(8,128)(2,1)S(1)}, u32[]{:S(2)}, u32[]{:S(2)}) collective-permute-start(bf16[512,128]{1,0:T(8,128)(2,1)} %get-tuple-element.30), channel_id=1, source_target_pairs={{0,2},{1,3},{2,0},{3,1},{4,6},{5,7},{6,4},{7,5},{8,10},{9,11},{10,... | collective-permute-start | bytes 393224 | tf_op jit(solution)/shard_map/ppermute | solution.py:352
  13.5 0.9 %collective-permute-start.5 = (bf16[512,128]{1,0:T(8,128)(2,1)}, bf16[512,128]{1,0:T(8,128)(2,1)S(1)}, u32[]{:S(2)}, u32[]{:S(2)}) collective-permute-start(bf16[512,128]{1,0:T(8,128)(2,1)} %get-tuple-element.31), channel_id=1, source_target_pairs={{0,3},{1,2},{2,1},{3,0},{4,7},{5,6},{6,5},{7,4},{8,11},{9,10},{10,... | collective-permute-start | bytes 393224 | tf_op jit(solution)/shard_map/ppermute | solution.py:352
  14.4 1.6 %copy-done = f32[8,4,128,128]{3,2,1,0:T(8,128)S(1)} copy-done((f32[8,4,128,128]{3,2,1,0:T(8,128)S(1)}, f32[8,4,128,128]{3,2,1,0:T(8,128)}, u32[]{:S(2)}) %copy-start) | copy-done | bytes 2097176
  16.0 0.9 %copy-done.5 = bf16[4,128,128]{2,1,0:T(8,128)(2,1)S(1)} copy-done((bf16[4,128,128]{2,1,0:T(8,128)(2,1)S(1)}, bf16[4,128,128]{2,1,0:T(8,128)(2,1)}, u32[]{:S(2)}) %copy-start.5) | copy-done | bytes 131096
  16.9 3.7 %attention_rows.3 = (f32[512,384]{1,0:T(8,128)S(1)}, f32[512,384]{1,0:T(8,128)S(1)}) custom-call(s32[1]{0:T(128)} %bitcast.head_ref.ids_ref.quarter_ref, bf16[4096,512]{1,0:T(8,128)(2,1)} %q_ref.9, bf16[4096,512]{1,0:T(8,128)(2,1)} %k_ref.11, bf16[4096,512]{1,0:T(8,128)(2,1)} %v_ref.11, f32[8,4,128,128]{3,2,1,0:T(8,128)S(1)} %copy-done, ...), custom_call_target="tpu_custom_call" | custom-call | flops 1024 | bytes 1024 | tf_op jit(solution)/shard_map/attention_rows/pallas_call | solution.py:165
  20.6 0.0 collective-permute-done.got_ref
  20.6 0.0 collective-permute-done.2.rest_3_.q3_ref
  20.6 0.0 collective-permute-done.1.rest_2_.q2_ref
  20.6 0.1 add_step.3
  20.7 1.4 %collective-permute-start.3 = (bf16[4,128,128]{2,1,0:T(8,128)(2,1)S(1)}, bf16[4,128,128]{2,1,0:T(8,128)(2,1)S(1)}, u32[]{:S(2)}, u32[]{:S(2)}) collective-permute-start(bf16[4,128,128]{2,1,0:T(8,128)(2,1)S(1)} %get-tuple-element.28.rest_0_.total_ref), channel_id=1, source_target_pairs={{0,8},{4,12},{8,0},{12,4},{16,24},{20,28},{24,16},{28,20},{1,9},{5... | collective-permute-start | bytes 393224 | tf_op jit(solution)/shard_map/ppermute | solution.py:352
  22.0 1.2 %collective-permute-start.7 = (bf16[512,128]{1,0:T(8,128)(2,1)}, bf16[512,128]{1,0:T(8,128)(2,1)S(1)}, u32[]{:S(2)}, u32[]{:S(2)}) collective-permute-start(bf16[512,128]{1,0:T(8,128)(2,1)} %get-tuple-element.34), channel_id=1, source_target_pairs={{0,2},{1,3},{2,0},{3,1},{4,6},{5,7},{6,4},{7,5},{8,10},{9,11},{10,... | collective-permute-start | bytes 393224 | tf_op jit(solution)/shard_map/ppermute | solution.py:352
  23.2 0.5 collective-permute-start.8
  23.7 4.5 %attention_quarter.2.rest_1_.refs_1_ = f32[1024,512]{1,0:T(8,128)S(1)} custom-call(s32[1]{0:T(128)} %bitcast.head_ref.ids_ref.quarter_ref, bf16[4096,512]{1,0:T(8,128)(2,1)} %q_ref.9, bf16[4096,512]{1,0:T(8,128)(2,1)} %k_ref.11, bf16[4096,512]{1,0:T(8,128)(2,1)} %v_ref.11, f32[8,4,128,128]{3,2,1,0:T(8,128)} %get-tuple-element.24.within_ref, ...), custom_call_target="tpu_custom_call" | custom-call | flops 1024 | bytes 1024 | tf_op jit(solution)/shard_map/attention_quarter/pallas_call | solution.py:198
  28.2 0.0 collective-permute-done.4.rest_2_.l2_ref
  28.2 0.0 collective-permute-done.5.rest_3_.l3_ref
  28.2 0.0 collective-permute-done.3.got_ref
  28.2 0.1 add_step.4
  28.3 2.4 %collective-permute-start.6 = (bf16[4,128,128]{2,1,0:T(8,128)(2,1)S(1)}, bf16[4,128,128]{2,1,0:T(8,128)(2,1)S(1)}, u32[]{:S(2)}, u32[]{:S(2)}) collective-permute-start(bf16[4,128,128]{2,1,0:T(8,128)(2,1)S(1)} %get-tuple-element.32.total_ref), channel_id=1, source_target_pairs={{0,16},{4,20},{8,24},{12,28},{16,0},{20,4},{24,8},{28,12},{1,17},{... | collective-permute-start | bytes 393224 | tf_op jit(solution)/shard_map/ppermute | solution.py:352
  30.7 0.0 collective-permute-done.7.rest_1_.l2_ref
  30.7 0.0 collective-permute-done.8.rest_2_.l3_ref
  30.7 6.7 %collective-permute-done.6.got_ref = bf16[4,128,128]{2,1,0:T(8,128)(2,1)S(1)} collective-permute-done((bf16[4,128,128]{2,1,0:T(8,128)(2,1)S(1)}, bf16[4,128,128]{2,1,0:T(8,128)(2,1)S(1)}, u32[]{:S(2)}, u32[]{:S(2)}) %collective-permute-start.6) | collective-permute-done | bytes 131104 | tf_op jit(solution)/shard_map/ppermute | solution.py:352
  37.4 0.7 add_step.5
  38.1 1.5 %late_rows.2 = (bf16[560,384]{1,0:T(8,128)(2,1)S(1)}, bf16[560,384]{1,0:T(8,128)(2,1)S(1)}) custom-call(s32[1]{0:T(128)} %bitcast.head_ref.ids_ref.quarter_ref, bf16[4096,512]{1,0:T(8,128)(2,1)} %q_ref.9, f32[512,384]{1,0:T(8,128)S(1)} %get-tuple-element.26.rest_0_.refs_1_, bf16[4096,512]{1,0:T(8,128)(2,1)} %q_ref.9, ...), custom_call_target="tpu_custom_call" | custom-call | flops 1024 | bytes 1024 | tf_op jit(solution)/shard_map/late_rows/pallas_call | solution.py:246
  39.6 1.2 %collective-permute-start.9 = (bf16[560,384]{1,0:T(8,128)(2,1)S(1)}, bf16[560,384]{1,0:T(8,128)(2,1)S(1)}, u32[]{:S(2)}, u32[]{:S(2)}) collective-permute-start(bf16[560,384]{1,0:T(8,128)(2,1)S(1)} %get-tuple-element.37.refs_3_), channel_id=1, source_target_pairs={{0,2},{1,3},{2,0},{3,1},{4,6},{5,7},{6,4},{7,5},{8,10},{9,11},{10,... | collective-permute-start | bytes 1290248 | tf_op jit(solution)/shard_map/ppermute | solution.py:352
  40.8 0.9 %collective-permute-start.10 = (bf16[560,384]{1,0:T(8,128)(2,1)S(1)}, bf16[560,384]{1,0:T(8,128)(2,1)S(1)}, u32[]{:S(2)}, u32[]{:S(2)}) collective-permute-start(bf16[560,384]{1,0:T(8,128)(2,1)S(1)} %get-tuple-element.38.refs_4_), channel_id=1, source_target_pairs={{0,3},{1,2},{2,1},{3,0},{4,7},{5,6},{6,5},{7,4},{8,11},{9,10},{10,... | collective-permute-start | bytes 1290248 | tf_op jit(solution)/shard_map/ppermute | solution.py:352
  41.7 2.9 %late_rows.3.rest_1_ = bf16[1024,512]{1,0:T(8,128)(2,1)} custom-call(s32[1]{0:T(128)} %bitcast.head_ref.ids_ref.quarter_ref, bf16[4096,512]{1,0:T(8,128)(2,1)} %q_ref.9, f32[1024,512]{1,0:T(8,128)} %copy-done.2, f32[4,128,128]{2,1,0:T(8,128)S(1)} %get-tuple-element.36.refs_4_.refs_2_.rest_0_, bf16[560,384]{1,0:T(8,128)(2,1)S(1)} %get-tuple-element.37.refs_3_, ...), custom_call_target="tpu_custom_call" | custom-call | flops 1024 | bytes 1024 | tf_op jit(solution)/shard_map/late_rows/pallas_call | solution.py:246
  44.7 3.2 %attention_rows.4 = (bf16[256,384]{1,0:T(8,128)(2,1)}, bf16[256,384]{1,0:T(8,128)(2,1)}) custom-call(s32[1]{0:T(128)} %bitcast.head_ref.ids_ref.quarter_ref, bf16[4096,512]{1,0:T(8,128)(2,1)} %q_ref.9, bf16[4096,512]{1,0:T(8,128)(2,1)} %k_ref.11, bf16[4096,512]{1,0:T(8,128)(2,1)} %v_ref.11, f32[8,4,128,128]{3,2,1,0:T(8,128)S(1)} %copy-done.1, ...), custom_call_target="tpu_custom_call" | custom-call | flops 1024 | bytes 1024 | tf_op jit(solution)/shard_map/attention_rows/pallas_call | solution.py:165
  47.9 0.0 collective-permute-start.11
  47.9 1.2 %collective-permute-start.14 = (bf16[256,384]{1,0:T(8,128)(2,1)}, bf16[256,384]{1,0:T(8,128)(2,1)}, u32[]{:S(2)}, u32[]{:S(2)}) collective-permute-start(bf16[256,384]{1,0:T(8,128)(2,1)} %get-tuple-element.39.rest_1_), channel_id=1, source_target_pairs={{0,2},{1,3},{2,0},{3,1},{4,6},{5,7},{6,4},{7,5},{8,10},{9,11},{10,... | collective-permute-start | bytes 589832 | tf_op jit(solution)/shard_map/ppermute | solution.py:352
  49.1 1.0 %collective-permute-start.15 = (bf16[256,384]{1,0:T(8,128)(2,1)}, bf16[256,384]{1,0:T(8,128)(2,1)}, u32[]{:S(2)}, u32[]{:S(2)}) collective-permute-start(bf16[256,384]{1,0:T(8,128)(2,1)} %get-tuple-element.40.rest_2_), channel_id=1, source_target_pairs={{0,3},{1,2},{2,1},{3,0},{4,7},{5,6},{6,5},{7,4},{8,11},{9,10},{10,... | collective-permute-start | bytes 589832 | tf_op jit(solution)/shard_map/ppermute | solution.py:352
  50.0 0.6 collective-permute-done.9.rest_3_.x2_ref.b2_ref
  50.7 10.7 %collective-permute-done.10.rest_4_.x3_ref.b3_ref = bf16[560,384]{1,0:T(8,128)(2,1)S(1)} collective-permute-done((bf16[560,384]{1,0:T(8,128)(2,1)S(1)}, bf16[560,384]{1,0:T(8,128)(2,1)S(1)}, u32[]{:S(2)}, u32[]{:S(2)}) %collective-permute-start.10) | collective-permute-done | bytes 430112 | tf_op jit(solution)/shard_map/ppermute | solution.py:352
  61.4 3.2 %attention_rows.5 = (bf16[256,384]{1,0:T(8,128)(2,1)S(1)}, bf16[256,384]{1,0:T(8,128)(2,1)S(1)}) custom-call(s32[1]{0:T(128)} %bitcast.head_ref.ids_ref.quarter_ref, bf16[4096,512]{1,0:T(8,128)(2,1)} %q_ref.9, bf16[4096,512]{1,0:T(8,128)(2,1)} %k_ref.11, bf16[4096,512]{1,0:T(8,128)(2,1)} %v_ref.11, f32[8,4,128,128]{3,2,1,0:T(8,128)S(1)} %copy-done.1, ...), custom_call_target="tpu_custom_call" | custom-call | flops 999999995904 | bytes 1024 | tf_op jit(solution)/shard_map/attention_rows/pallas_call | solution.py:165
  64.6 1.2 %collective-permute-start.12 = (bf16[256,384]{1,0:T(8,128)(2,1)S(1)}, bf16[256,384]{1,0:T(8,128)(2,1)S(1)}, u32[]{:S(2)}, u32[]{:S(2)}) collective-permute-start(bf16[256,384]{1,0:T(8,128)(2,1)S(1)} %get-tuple-element.41.rest_1_), channel_id=1, source_target_pairs={{0,2},{1,3},{2,0},{3,1},{4,6},{5,7},{6,4},{7,5},{8,10},{9,11},{10,... | collective-permute-start | bytes 589832 | tf_op jit(solution)/shard_map/ppermute | solution.py:352
  65.8 0.1 collective-permute-start.13
  66.0 4.4 %attention_quarter.3.own_ref = bf16[1024,512]{1,0:T(8,128)(2,1)S(1)} custom-call(s32[1]{0:T(128)} %bitcast.head_ref.ids_ref.quarter_ref, bf16[4096,512]{1,0:T(8,128)(2,1)} %q_ref.9, bf16[4096,512]{1,0:T(8,128)(2,1)} %k_ref.11, bf16[4096,512]{1,0:T(8,128)(2,1)} %v_ref.11, f32[8,4,128,128]{3,2,1,0:T(8,128)S(1)} %copy-done.1, ...), custom_call_target="tpu_custom_call" | custom-call | flops 1024 | bytes 1024 | tf_op jit(solution)/shard_map/attention_quarter/pallas_call | solution.py:198
  70.4 0.0 collective-permute-done.11.mate_ref
  70.4 2.5 %norm_rows.4.rest_0_ = bf16[1024,2048]{1,0:T(8,128)(2,1)} custom-call(s32[1]{0:T(128)} %bitcast.head_ref.ids_ref.quarter_ref, f32[1,2048]{1,0:T(1,128)S(1)} %bitcast.3, bf16[1024,512]{1,0:T(8,128)(2,1)S(1)} %attention_quarter.3.own_ref, bf16[1024,512]{1,0:T(8,128)(2,1)} %collective-permute-done.11.mate_ref, ...), custom_call_target="tpu_custom_call" | custom-call | flops 1024 | bytes 1024 | tf_op jit(solution)/shard_map/norm_rows/pallas_call | solution.py:307
  72.9 2.5 %norm_rows.5.rest_0_ = bf16[1024,2048]{1,0:T(8,128)(2,1)} custom-call(s32[1]{0:T(128)} %bitcast.head_ref.ids_ref.quarter_ref, f32[1,2048]{1,0:T(1,128)S(1)} %bitcast.4, bf16[1024,512]{1,0:T(8,128)(2,1)S(1)} %attention_quarter.3.own_ref, bf16[1024,512]{1,0:T(8,128)(2,1)} %collective-permute-done.11.mate_ref, ...), custom_call_target="tpu_custom_call", output_to_operand_aliasing={{}: (12, {})} | custom-call | flops 1024 | bytes 1024 | tf_op jit(solution)/shard_map/norm_rows/pallas_call | solution.py:307
  75.4 0.0 collective-permute-done.14.x2_ref
  75.4 0.0 collective-permute-done.15.x3_ref
  75.4 2.7 %norm_rows.6.rest_0_ = bf16[1024,2048]{1,0:T(8,128)(2,1)} custom-call(s32[1]{0:T(128)} %bitcast.head_ref.ids_ref.quarter_ref, f32[1,2048]{1,0:T(1,128)S(1)} %bitcast.5, bf16[1024,512]{1,0:T(8,128)(2,1)S(1)} %attention_quarter.3.own_ref, bf16[1024,512]{1,0:T(8,128)(2,1)} %collective-permute-done.11.mate_ref, ...), custom_call_target="tpu_custom_call", output_to_operand_aliasing={{}: (12, {})} | custom-call | flops 1024 | bytes 1024 | tf_op jit(solution)/shard_map/norm_rows/pallas_call | solution.py:307
  78.1 2.5 %norm_rows.7 = bf16[1024,2048]{1,0:T(8,128)(2,1)} custom-call(s32[1]{0:T(128)} %bitcast.head_ref.ids_ref.quarter_ref, f32[1,2048]{1,0:T(1,128)S(1)} %bitcast.6, bf16[1024,512]{1,0:T(8,128)(2,1)S(1)} %attention_quarter.3.own_ref, bf16[1024,512]{1,0:T(8,128)(2,1)} %collective-permute-done.11.mate_ref, ...), custom_call_target="tpu_custom_call", output_to_operand_aliasing={{}: (12, {})} | custom-call | flops 1024 | bytes 1024 | tf_op jit(solution)/shard_map/norm_rows/pallas_call | solution.py:307
  (18 shorter events, 0.0 us)
Async XLA Ops:
  1.1 2.7 %copy-start.7 = (bf16[1024,128]{1,0:T(8,128)(2,1)}, bf16[1024,128]{1,0:T(8,128)(2,1)S(1)}, u32[]{:S(2)}) copy-start(bf16[1024,128]{1,0:T(8,128)(2,1)S(1)} %get-tuple-element.44.q2_ref) | copy-start | bytes 786436
  1.1 2.7 %copy-start.8 = (bf16[1024,128]{1,0:T(8,128)(2,1)}, bf16[1024,128]{1,0:T(8,128)(2,1)S(1)}, u32[]{:S(2)}) copy-start(bf16[1024,128]{1,0:T(8,128)(2,1)S(1)} %get-tuple-element.43.q3_ref) | copy-start | bytes 786436
  1.1 19.5 %collective-permute-start.2 = (bf16[1024,128]{1,0:T(8,128)(2,1)S(1)}, bf16[1024,128]{1,0:T(8,128)(2,1)S(1)}, u32[]{:S(2)}, u32[]{:S(2)}) collective-permute-start(bf16[1024,128]{1,0:T(8,128)(2,1)S(1)} %get-tuple-element.43.q3_ref), channel_id=1, source_target_pairs={{0,3},{1,2},{2,1},{3,0},{4,7},{5,6},{6,5},{7,4},{8,11},{9,10},{10,... | collective-permute-start | bytes 786440 | tf_op jit(solution)/shard_map/ppermute | solution.py:352
  3.8 16.8 %collective-permute-start.1 = (bf16[1024,128]{1,0:T(8,128)(2,1)S(1)}, bf16[1024,128]{1,0:T(8,128)(2,1)S(1)}, u32[]{:S(2)}, u32[]{:S(2)}) collective-permute-start(bf16[1024,128]{1,0:T(8,128)(2,1)S(1)} %get-tuple-element.44.q2_ref), channel_id=1, source_target_pairs={{0,2},{1,3},{2,0},{3,1},{4,6},{5,7},{6,4},{7,5},{8,10},{9,11},{10,... | collective-permute-start | bytes 786440 | tf_op jit(solution)/shard_map/ppermute | solution.py:352
  10.7 9.9 %collective-permute-start = (bf16[4,128,128]{2,1,0:T(8,128)(2,1)}, bf16[4,128,128]{2,1,0:T(8,128)(2,1)S(1)}, u32[]{:S(2)}, u32[]{:S(2)}) collective-permute-start(bf16[4,128,128]{2,1,0:T(8,128)(2,1)} %get-tuple-element.25.rest_0_.total_ref), channel_id=1, source_target_pairs={{0,4},{4,0},{8,12},{12,8},{16,20},{20,16},{24,28},{28,24},{1,5},{5... | collective-permute-start | bytes 393224 | tf_op jit(solution)/shard_map/ppermute | solution.py:352
  12.2 15.9 %collective-permute-start.4 = (bf16[512,128]{1,0:T(8,128)(2,1)}, bf16[512,128]{1,0:T(8,128)(2,1)S(1)}, u32[]{:S(2)}, u32[]{:S(2)}) collective-permute-start(bf16[512,128]{1,0:T(8,128)(2,1)} %get-tuple-element.30), channel_id=1, source_target_pairs={{0,2},{1,3},{2,0},{3,1},{4,6},{5,7},{6,4},{7,5},{8,10},{9,11},{10,... | collective-permute-start | bytes 393224 | tf_op jit(solution)/shard_map/ppermute | solution.py:352
  13.5 14.7 %collective-permute-start.5 = (bf16[512,128]{1,0:T(8,128)(2,1)}, bf16[512,128]{1,0:T(8,128)(2,1)S(1)}, u32[]{:S(2)}, u32[]{:S(2)}) collective-permute-start(bf16[512,128]{1,0:T(8,128)(2,1)} %get-tuple-element.31), channel_id=1, source_target_pairs={{0,3},{1,2},{2,1},{3,0},{4,7},{5,6},{6,5},{7,4},{8,11},{9,10},{10,... | collective-permute-start | bytes 393224 | tf_op jit(solution)/shard_map/ppermute | solution.py:352
  14.4 1.6 %copy-start = (f32[8,4,128,128]{3,2,1,0:T(8,128)S(1)}, f32[8,4,128,128]{3,2,1,0:T(8,128)}, u32[]{:S(2)}) copy-start(f32[8,4,128,128]{3,2,1,0:T(8,128)} %get-tuple-element.24.within_ref) | copy-start | bytes 6291460
  16.0 0.9 %copy-start.5 = (bf16[4,128,128]{2,1,0:T(8,128)(2,1)S(1)}, bf16[4,128,128]{2,1,0:T(8,128)(2,1)}, u32[]{:S(2)}) copy-start(bf16[4,128,128]{2,1,0:T(8,128)(2,1)} %get-tuple-element.25.rest_0_.total_ref) | copy-start | bytes 393220
  20.7 7.6 %collective-permute-start.3 = (bf16[4,128,128]{2,1,0:T(8,128)(2,1)S(1)}, bf16[4,128,128]{2,1,0:T(8,128)(2,1)S(1)}, u32[]{:S(2)}, u32[]{:S(2)}) collective-permute-start(bf16[4,128,128]{2,1,0:T(8,128)(2,1)S(1)} %get-tuple-element.28.rest_0_.total_ref), channel_id=1, source_target_pairs={{0,8},{4,12},{8,0},{12,4},{16,24},{20,28},{24,16},{28,20},{1,9},{5... | collective-permute-start | bytes 393224 | tf_op jit(solution)/shard_map/ppermute | solution.py:352
  22.0 8.7 %collective-permute-start.7 = (bf16[512,128]{1,0:T(8,128)(2,1)}, bf16[512,128]{1,0:T(8,128)(2,1)S(1)}, u32[]{:S(2)}, u32[]{:S(2)}) collective-permute-start(bf16[512,128]{1,0:T(8,128)(2,1)} %get-tuple-element.34), channel_id=1, source_target_pairs={{0,2},{1,3},{2,0},{3,1},{4,6},{5,7},{6,4},{7,5},{8,10},{9,11},{10,... | collective-permute-start | bytes 393224 | tf_op jit(solution)/shard_map/ppermute | solution.py:352
  23.2 7.5 %collective-permute-start.8 = (bf16[512,128]{1,0:T(8,128)(2,1)}, bf16[512,128]{1,0:T(8,128)(2,1)S(1)}, u32[]{:S(2)}, u32[]{:S(2)}) collective-permute-start(bf16[512,128]{1,0:T(8,128)(2,1)} %get-tuple-element.35), channel_id=1, source_target_pairs={{0,3},{1,2},{2,1},{3,0},{4,7},{5,6},{6,5},{7,4},{8,11},{9,10},{10,... | collective-permute-start | bytes 393224 | tf_op jit(solution)/shard_map/ppermute | solution.py:352
  28.2 11.4 %copy-start.2 = (f32[1024,512]{1,0:T(8,128)}, f32[1024,512]{1,0:T(8,128)S(1)}, u32[]{:S(2)}) copy-start(f32[1024,512]{1,0:T(8,128)S(1)} %attention_quarter.2.rest_1_.refs_1_) | copy-start | bytes 6291460
  28.3 9.1 %collective-permute-start.6 = (bf16[4,128,128]{2,1,0:T(8,128)(2,1)S(1)}, bf16[4,128,128]{2,1,0:T(8,128)(2,1)S(1)}, u32[]{:S(2)}, u32[]{:S(2)}) collective-permute-start(bf16[4,128,128]{2,1,0:T(8,128)(2,1)S(1)} %get-tuple-element.32.total_ref), channel_id=1, source_target_pairs={{0,16},{4,20},{8,24},{12,28},{16,0},{20,4},{24,8},{28,12},{1,17},{... | collective-permute-start | bytes 393224 | tf_op jit(solution)/shard_map/ppermute | solution.py:352
  30.7 8.9 %copy-start.3 = (bf16[512,128]{1,0:T(8,128)(2,1)}, bf16[512,128]{1,0:T(8,128)(2,1)S(1)}, u32[]{:S(2)}) copy-start(bf16[512,128]{1,0:T(8,128)(2,1)S(1)} %collective-permute-done.8.rest_2_.l3_ref) | copy-start | bytes 393220
  39.6 11.1 %collective-permute-start.9 = (bf16[560,384]{1,0:T(8,128)(2,1)S(1)}, bf16[560,384]{1,0:T(8,128)(2,1)S(1)}, u32[]{:S(2)}, u32[]{:S(2)}) collective-permute-start(bf16[560,384]{1,0:T(8,128)(2,1)S(1)} %get-tuple-element.37.refs_3_), channel_id=1, source_target_pairs={{0,2},{1,3},{2,0},{3,1},{4,6},{5,7},{6,4},{7,5},{8,10},{9,11},{10,... | collective-permute-start | bytes 1290248 | tf_op jit(solution)/shard_map/ppermute | solution.py:352
  40.8 3.9 %copy-start.1 = (f32[8,4,128,128]{3,2,1,0:T(8,128)S(1)}, f32[8,4,128,128]{3,2,1,0:T(8,128)}, u32[]{:S(2)}) copy-start(f32[8,4,128,128]{3,2,1,0:T(8,128)} %get-tuple-element.24.within_ref) | copy-start | bytes 6291460
  40.8 20.6 %collective-permute-start.10 = (bf16[560,384]{1,0:T(8,128)(2,1)S(1)}, bf16[560,384]{1,0:T(8,128)(2,1)S(1)}, u32[]{:S(2)}, u32[]{:S(2)}) collective-permute-start(bf16[560,384]{1,0:T(8,128)(2,1)S(1)} %get-tuple-element.38.refs_4_), channel_id=1, source_target_pairs={{0,3},{1,2},{2,1},{3,0},{4,7},{5,6},{6,5},{7,4},{8,11},{9,10},{10,... | collective-permute-start | bytes 1290248 | tf_op jit(solution)/shard_map/ppermute | solution.py:352
  47.9 22.5 %collective-permute-start.11 = (bf16[1024,512]{1,0:T(8,128)(2,1)}, bf16[1024,512]{1,0:T(8,128)(2,1)}, u32[]{:S(2)}, u32[]{:S(2)}) collective-permute-start(bf16[1024,512]{1,0:T(8,128)(2,1)} %late_rows.3.rest_1_), channel_id=1, source_target_pairs={{0,1},{1,0},{2,3},{3,2},{4,5},{5,4},{6,7},{7,6},{8,9},{9,8},{10,11... | collective-permute-start | bytes 3145736 | tf_op jit(solution)/shard_map/ppermute | solution.py:352
  47.9 27.5 %collective-permute-start.14 = (bf16[256,384]{1,0:T(8,128)(2,1)}, bf16[256,384]{1,0:T(8,128)(2,1)}, u32[]{:S(2)}, u32[]{:S(2)}) collective-permute-start(bf16[256,384]{1,0:T(8,128)(2,1)} %get-tuple-element.39.rest_1_), channel_id=1, source_target_pairs={{0,2},{1,3},{2,0},{3,1},{4,6},{5,7},{6,4},{7,5},{8,10},{9,11},{10,... | collective-permute-start | bytes 589832 | tf_op jit(solution)/shard_map/ppermute | solution.py:352
  49.1 26.4 %collective-permute-start.15 = (bf16[256,384]{1,0:T(8,128)(2,1)}, bf16[256,384]{1,0:T(8,128)(2,1)}, u32[]{:S(2)}, u32[]{:S(2)}) collective-permute-start(bf16[256,384]{1,0:T(8,128)(2,1)} %get-tuple-element.40.rest_2_), channel_id=1, source_target_pairs={{0,3},{1,2},{2,1},{3,0},{4,7},{5,6},{6,5},{7,4},{8,11},{9,10},{10,... | collective-permute-start | bytes 589832 | tf_op jit(solution)/shard_map/ppermute | solution.py:352
  64.6 13.5 %collective-permute-start.12 = (bf16[256,384]{1,0:T(8,128)(2,1)S(1)}, bf16[256,384]{1,0:T(8,128)(2,1)S(1)}, u32[]{:S(2)}, u32[]{:S(2)}) collective-permute-start(bf16[256,384]{1,0:T(8,128)(2,1)S(1)} %get-tuple-element.41.rest_1_), channel_id=1, source_target_pairs={{0,2},{1,3},{2,0},{3,1},{4,6},{5,7},{6,4},{7,5},{8,10},{9,11},{10,... | collective-permute-start | bytes 589832 | tf_op jit(solution)/shard_map/ppermute | solution.py:352
  65.8 4.5 %copy-start.6 = (f32[2048]{0:T(1024)S(1)}, f32[2048]{0:T(1024)}, u32[]{:S(2)}) copy-start(f32[2048]{0:T(1024)} %param.7) | copy-start | bytes 24580
  65.8 12.3 %collective-permute-start.13 = (bf16[256,384]{1,0:T(8,128)(2,1)S(1)}, bf16[256,384]{1,0:T(8,128)(2,1)S(1)}, u32[]{:S(2)}, u32[]{:S(2)}) collective-permute-start(bf16[256,384]{1,0:T(8,128)(2,1)S(1)} %get-tuple-element.42.rest_2_), channel_id=1, source_target_pairs={{0,3},{1,2},{2,1},{3,0},{4,7},{5,6},{6,5},{7,4},{8,11},{9,10},{10,... | collective-permute-start | bytes 589832 | tf_op jit(solution)/shard_map/ppermute | solution.py:352
  72.9 2.5 %copy-start.4 = (bf16[512,128]{1,0:T(8,128)(2,1)S(1)}, bf16[512,128]{1,0:T(8,128)(2,1)}, u32[]{:S(2)}) copy-start(bf16[512,128]{1,0:T(8,128)(2,1)} %copy-done.3) | copy-start | bytes 393220

commit v3 on v2

--- a/solution.py
+++ b/solution.py
@@ -11,6 +11,7 @@
 BLK = 512
 HALF = 256
 EXTRA = 48
+TILE = 128
 EPS = 1e-06
 COST = pl.CostEstimate(flops=1024, bytes_accessed=1024, transcendentals=0)
 LONG = pl.CostEstimate(flops=10**12, bytes_accessed=1024, transcendentals=0)
@@ -20,11 +21,10 @@
     return pltpu.CompilerParams(vmem_limit_bytes=mib * 1024 * 1024)
 
 
-def state_kernel(parts, tokens, head_ref, k_ref, v_ref, q2_ref, q3_ref, *rest):
-    within_ref, total_ref, *rest = rest[tokens:]
-    outs, (k_buf, v_buf, k_sem, v_sem) = rest[:-4], rest[-4:]
+def state_kernel(parts, tokens, k_ref, v_ref, *rest):
+    within_ref, total_ref, k_buf, v_buf, k_sem, v_sem = rest[tokens:]
     rows, width = k_buf.shape
-    heads, part, share = width // DH, rows // parts, rows // 4
+    heads, part = width // DH, rows // parts
     copies = []
     for p in range(parts):
         at = pl.ds(p * part, part)
@@ -50,43 +50,32 @@
                 )
     for h in range(heads):
         total_ref[h] = acc[h].astype(jnp.bfloat16)
-    blocks = share // BLK
-    cols = pl.ds(width - DH, DH)
-    for side, q_ref in ((2, q2_ref), (3, q3_ref)):
-        for n in range(blocks):
-            block = (head_ref[0] ^ side) * blocks + n
-            at = pl.ds(pl.multiple_of(block * BLK, BLK), BLK)
-            attend(
-                0, BLK // HALF, 1, q_ref.at[pl.ds(n * BLK, BLK)], k_buf.at[at, cols], v_buf.at[at, cols],
-                within_ref.at[pl.ds(block, 1), pl.ds(heads - 1, 1)], None, outs[(side - 2) * blocks + n],
-            )
-
-
-def block_states(head, keys, values, slices, *tokens):
+
+
+def block_states(keys, values, *tokens):
     rows, width = keys.shape
     heads, blocks = width // DH, rows // BLK
     parts = 4 if blocks % 4 == 0 else 1
     anywhere = pl.BlockSpec(memory_space=pl.ANY)
     vmem = pl.BlockSpec(memory_space=pltpu.VMEM)
-    pieces = 2 * (blocks // 4)
     return pl.pallas_call(
         functools.partial(state_kernel, parts, len(tokens)),
-        in_specs=[pl.BlockSpec(memory_space=pltpu.SMEM), anywhere, anywhere, vmem, vmem] + [anywhere] * len(tokens),
-        out_specs=[vmem] * (2 + pieces),
+        in_specs=[anywhere, anywhere] + [anywhere] * len(tokens),
+        out_specs=[vmem, vmem],
         out_shape=[
             jax.ShapeDtypeStruct((blocks, heads, DH, DH), jnp.float32),
             jax.ShapeDtypeStruct((heads, DH, DH), jnp.bfloat16),
-        ] + [jax.ShapeDtypeStruct((BLK, DH), jnp.bfloat16)] * pieces,
+        ],
         scratch_shapes=[
             pltpu.VMEM((rows, width), jnp.bfloat16),
             pltpu.VMEM((rows, width), jnp.bfloat16),
             pltpu.SemaphoreType.DMA((parts,)),
             pltpu.SemaphoreType.DMA((parts,)),
         ],
-        compiler_params=params(62),
+        compiler_params=params(),
         cost_estimate=COST,
         name="block_states",
-    )(head, keys, values, *slices, *tokens)
+    )(keys, values, *tokens)
 
 
 def attend(first, halves, heads, q_ref, k_ref, v_ref, within_ref, before_ref, out_ref):
@@ -210,9 +199,55 @@
     )(at, *operands, *tokens)
 
 
-def late_kernel(count, heads, embed, ids_ref, *refs):
+def early_kernel(tail, head_ref, q_ref, k_ref, v_ref, within_ref, *rest):
+    outs = rest[len(rest) - 2:]
+    if tail:
+        tail_ref = rest[0]
+    for side in range(2):
+        @pl.when(pl.program_id(0) == side)
+        def _(side=side):
+            attend(0, BLK // HALF, 1, q_ref, k_ref, v_ref, within_ref, None, outs[side])
+            if tail:
+                outs[side][pl.ds(BLK, tail), :] = tail_ref[...]
+
+
+def early_rows(head, queries, keys, values, within, n, tail, tokens):
+    rows, width = keys.shape
+    share, last = rows // 4, width // DH - 1
+    blocks = share // BLK
+    block = pl.BlockSpec((BLK, DH), lambda i, s: ((s[0] ^ (2 + i)) * blocks + n, last))
+    in_specs = [
+        block, block, block, pl.BlockSpec((1, 1, DH, DH), lambda i, s: ((s[0] ^ (2 + i)) * blocks + n, last, 0, 0)),
+    ]
+    operands = [queries, keys, values, within]
+    if tail:
+        per = share // tail
+        in_specs.append(pl.BlockSpec((tail, DH), lambda i, s: ((s[0] ^ (2 + i)) * per + per - 1, last)))
+        operands.append(queries)
+    in_specs += [pl.BlockSpec(memory_space=pl.ANY)] * len(tokens)
+    return pl.pallas_call(
+        functools.partial(early_kernel, tail),
+        grid_spec=pltpu.PrefetchScalarGridSpec(
+            num_scalar_prefetch=1,
+            grid=(2,),
+            in_specs=in_specs,
+            out_specs=[pl.BlockSpec((BLK + tail, DH), lambda i, s: (0, 0))] * 2,
+        ),
+        out_shape=[jax.ShapeDtypeStruct((BLK + tail, DH), jnp.bfloat16)] * 2,
+        compiler_params=params(),
+        cost_estimate=COST,
+        name="early_rows",
+    )(head, *operands, *tokens)
+
+
+def late_kernel(count, heads, embed, bit, head_ref, *refs):
     before_ref = refs[2 * count]
     outs = refs[len(refs) - count:]
+    if bit is not None:
+        mine_ref, got_ref = refs[2 * count + 1:2 * count + 3]
+        outs, after_ref = refs[len(refs) - count - 1:-1], refs[-1]
+        after_ref[...] = before_ref[...] + jnp.where((mine_ref[0] & bit) > 0, got_ref[...].astype(jnp.float32), 0.0)
+        before_ref = after_ref
     for n in range(count):
         q_ref, local_ref, out_ref = refs[2 * n], refs[2 * n + 1], outs[n]
         size = q_ref.shape[0]
@@ -229,7 +264,7 @@
                 out_ref[pl.ds(size, high - c * EXTRA), pl.ds(c * DH, DH)] = low[c * EXTRA:high]
 
 
-def late_rows(queries, before, at, sides, locals_, heads, embed, tokens):
+def late_rows(queries, before, at, sides, start, locals_, heads, embed, tokens, last=None):
     count = len(sides)
     size, span = locals_[0].shape
     steps = 1 if embed else size // BLK
@@ -237,80 +272,108 @@
     share = queries.shape[0] // 4
     in_specs, operands = [], []
     for n in range(count):
-        in_specs.append(pl.BlockSpec((rows, span), lambda i, s, side=sides[n]: ((s[0] ^ side) * (share // rows) + i, 0)))
+        in_specs.append(pl.BlockSpec((rows, span), lambda i, s, side=sides[n]: ((s[0] ^ side) * (share // rows) + start // rows + i, 0)))
         in_specs.append(pl.BlockSpec((rows, span), lambda i, s: (i, 0)))
         operands += [queries, locals_[n]]
-    in_specs.append(pl.BlockSpec(before.shape, lambda i, s: (0, 0, 0)))
+    state = pl.BlockSpec(before.shape, lambda i, s: (0, 0, 0))
+    in_specs.append(state)
+    operands.append(before)
+    bit, out_specs, out_shape = None, [], []
+    if last is not None:
+        mine, bit, got = last
+        in_specs += [pl.BlockSpec(memory_space=pltpu.SMEM), state]
+        operands += [mine, got]
+        out_specs, out_shape = [state], [jax.ShapeDtypeStruct(before.shape, jnp.float32)]
     in_specs += [pl.BlockSpec(memory_space=pl.ANY)] * len(tokens)
     more = EXTRA if embed else 0
     return pl.pallas_call(
-        functools.partial(late_kernel, count, heads, embed),
+        functools.partial(late_kernel, count, heads, embed, bit),
         grid_spec=pltpu.PrefetchScalarGridSpec(
             num_scalar_prefetch=1,
             grid=(steps,),
             in_specs=in_specs,
-            out_specs=[pl.BlockSpec((rows + more, span), lambda i, s: (i, 0))] * count,
+            out_specs=[pl.BlockSpec((rows + more, span), lambda i, s: (i, 0))] * count + out_specs,
         ),
-        out_shape=[jax.ShapeDtypeStruct((size + more, span), jnp.bfloat16)] * count,
+        out_shape=[jax.ShapeDtypeStruct((size + more, span), jnp.bfloat16)] * count + out_shape,
         compiler_params=params(),
         cost_estimate=COST,
         name="late_rows",
-    )(at, *operands, before, *tokens)
-
-
-def norm_kernel(head_ref, gain_ref, own_ref, mate_ref, x2_ref, x3_ref, l2_ref, l3_ref, q2_ref, q3_ref,
-                b2_ref, b3_ref, *rest):
-    out_ref = rest[-1]
-    head = head_ref[0]
-    tile, width = own_ref.shape
-    pieces = [(own_ref[...], 0, 0), (mate_ref[...], 1, 0)]
-    sides = ((2, x2_ref, l2_ref, q2_ref, b2_ref), (3, x3_ref, l3_ref, q3_ref, b3_ref))
-    for partner, x_ref, l_ref, q_ref, b_ref in sides:
-        base = b_ref.shape[0] - EXTRA
+    )(at, *operands, *tokens)
+
+
+def early_out_kernel(l2_ref, l3_ref, q2_ref, q3_ref, b2_ref, b3_ref, o2_ref, o3_ref):
+    for l_ref, q_ref, b_ref, o_ref in ((l2_ref, q2_ref, b2_ref, o2_ref), (l3_ref, q3_ref, b3_ref, o3_ref)):
         parts = []
         for c in range(b_ref.shape[1] // DH):
             high = min((c + 1) * EXTRA, DH)
-            parts.append(b_ref[pl.ds(base, high - c * EXTRA), pl.ds(c * DH, DH)])
+            parts.append(b_ref[pl.ds(b_ref.shape[0] - EXTRA, high - c * EXTRA), pl.ds(c * DH, DH)])
         state = jnp.concatenate(parts, axis=0)
-        late = l_ref[...].astype(jnp.float32) + jnp.dot(q_ref[...], state, preferred_element_type=jnp.float32)
-        pieces.append((x_ref[...], partner, 0))
-        pieces.append((late.astype(jnp.bfloat16), partner, width - DH))
+        out = l_ref[...].astype(jnp.float32) + jnp.dot(q_ref[...], state, preferred_element_type=jnp.float32)
+        o_ref[...] = out.astype(jnp.bfloat16)
+
+
+def early_out(size, l2, l3, q2, q3, b2, b3):
+    def at(pair):
+        index = pair[1] // size
+        return pl.BlockSpec((size, DH), lambda n: (index, 0))
+
+    def full(array):
+        return pl.BlockSpec(array.shape, lambda n: (0, 0))
+
+    out = jax.ShapeDtypeStruct((size, DH), jnp.bfloat16)
+    return pl.pallas_call(
+        early_out_kernel,
+        grid=(1,),
+        in_specs=[at(l2), at(l3), at(q2), at(q3), full(b2), full(b3)],
+        out_specs=[pl.BlockSpec((size, DH), lambda n: (0, 0))] * 2,
+        out_shape=[out, out],
+        compiler_params=params(),
+        cost_estimate=COST,
+        name="early_out",
+    )(l2[0], l3[0], q2[0], q3[0], b2, b3)
+
+
+def norm_kernel(head_ref, gain_ref, own_ref, mate_ref, x2_ref, x3_ref, o2_ref, o3_ref, *rest):
+    out_ref = rest[-1]
+    head = head_ref[0]
+    width = own_ref.shape[1]
+    pieces = (
+        (own_ref, 0, 0), (mate_ref, 1, 0), (x2_ref, 2, 0), (o2_ref, 2, width - DH), (x3_ref, 3, 0),
+        (o3_ref, 3, width - DH),
+    )
     total = 0.0
-    for piece, _, _ in pieces:
-        wide = piece.astype(jnp.float32)
+    for ref, _, _ in pieces:
+        wide = ref[...].astype(jnp.float32)
         total += jnp.sum(wide * wide, axis=-1, keepdims=True)
     scale = lax.rsqrt(total / (4 * width) + EPS)
-    for piece, partner, offset in pieces:
+    for ref, partner, offset in pieces:
         at = pl.multiple_of((head ^ partner) * width + offset, DH)
-        cols = pl.ds(at, piece.shape[1])
-        out_ref[:, cols] = (piece.astype(jnp.float32) * scale * gain_ref[:, cols]).astype(jnp.bfloat16)
-
-
-def norm_rows(head, gain, share, row, own, mate, x2, x3, l2, l3, q2, q3, b2, b3, out):
+        cols = pl.ds(at, ref.shape[1])
+        out_ref[:, cols] = (ref[...].astype(jnp.float32) * scale * gain_ref[:, cols]).astype(jnp.bfloat16)
+
+
+def norm_rows(head, gain, share, row, size, own, mate, x2, x3, o2, o3, out):
     def at(pair, cols):
-        index = pair[1] // HALF
-        return pl.BlockSpec((HALF, cols), lambda n, s: (index, 0))
-
-    def full(array):
-        return pl.BlockSpec(array.shape, lambda n, s: (0, 0))
+        index = pair[1] // TILE
+        return pl.BlockSpec((TILE, cols), lambda n, s: (index + n, 0))
 
     width = own[0].shape[1]
-    in_specs = [full(gain), at(own, width), at(mate, width), at(x2, width - DH), at(x3, width - DH)]
-    in_specs += [at(l2, DH), at(l3, DH), at(q2, DH), at(q3, DH), full(b2), full(b3)]
-    operands = [gain, own[0], mate[0], x2[0], x3[0], l2[0], l3[0], q2[0], q3[0], b2, b3]
+    in_specs = [pl.BlockSpec(gain.shape, lambda n, s: (0, 0)), at(own, width), at(mate, width)]
+    in_specs += [at(x2, width - DH), at(x3, width - DH), at(o2, DH), at(o3, DH)]
+    operands = [gain, own[0], mate[0], x2[0], x3[0], o2[0], o3[0]]
     aliases = {}
     if out is not None:
         in_specs.append(pl.BlockSpec(memory_space=pl.ANY))
         operands.append(out)
         aliases = {len(operands): 0}
-    index = row // HALF
+    index = row // TILE
     return pl.pallas_call(
         norm_kernel,
         grid_spec=pltpu.PrefetchScalarGridSpec(
             num_scalar_prefetch=1,
-            grid=(1,),
+            grid=(size // TILE,),
             in_specs=in_specs,
-            out_specs=pl.BlockSpec((HALF, 4 * width), lambda n, s: (index, 0)),
+            out_specs=pl.BlockSpec((TILE, 4 * width), lambda n, s: (index + n, 0)),
         ),
         out_shape=jax.ShapeDtypeStruct((share, 4 * width), jnp.bfloat16),
         input_output_aliases=aliases,
@@ -360,55 +423,53 @@
     rows, width = queries.shape
     heads = width // DH
     share = rows // 4
-    units = share // HALF
     head = lax.axis_index("head")
     at = jnp.full((1,), head, jnp.int32)
     mine = jnp.full((1,), lax.axis_index("seq"), jnp.int32)
     gain = norm_gain.reshape(1, -1)
     far = (2, 3)
 
-    slices = [lax.dynamic_slice(queries, ((head ^ k) * share, width - DH), (share, DH)) for k in far]
+    tail = HALF
+    slices = [lax.dynamic_slice(queries, ((head ^ k) * share, width - DH), (share - tail, DH)) for k in far]
     early_q = across(slices)
-    within, total, *early = block_states(at, keys, values, slices)
-    early_l = [across([early[n], early[n + share // BLK]]) for n in range(share // BLK)]
+    within, total = block_states(keys, values, *slices)
     arrays = (queries, keys, values, within)
     group, before, bit, step = total, None, 1, 0
+    early_l = []
     while bit < seq_size:
         got = swap(group, "seq", seq_size, bit)
         tokens = []
-        if step == 0:
-            first = attention_rows(arrays, None, at, far, 0, BLK, 0, heads - 1, jnp.float32, [group])
-            tokens = [*first, *early_q]
-        elif step == 1:
-            mate = attention_quarter(arrays, None, at, 1, jnp.float32, [group])
-            tokens = [mate, *early_l[0]]
+        if step < 2:
+            early = early_rows(at, queries, keys, values, within, step, tail * step, [group])
+            early_l.append(across(early))
+            tokens = [*early, *(early_q if step == 0 else early_l[0])]
         elif step == 2:
-            tokens = [*early_l[1]]
-        group, before = add_step(mine, bit, group, got, before, tokens)
+            first = attention_rows(arrays, None, at, far, BLK, HALF, 0, heads - 1, jnp.float32, [group])
+            tokens = [*first]
+        if bit * 2 < seq_size:
+            group, before = add_step(mine, bit, group, got, before, tokens)
         bit, step = bit * 2, step + 1
 
-    def far_unit(i, tokens, cost=None):
-        return attention_rows(
-            arrays, before, at, far, i * HALF, HALF, 0, heads - 1, jnp.bfloat16, tokens, cost
-        )
-
-    one = late_rows(queries, before, at, far, first, heads - 1, True, [])
+    def far_rows(start, size, tokens, cost=None):
+        return attention_rows(arrays, before, at, far, start, size, 0, heads - 1, jnp.bfloat16, tokens, cost)
+
+    *one, before = late_rows(queries, before, at, far, BLK, first, heads - 1, True, early_l[1], (mine, bit // 2, got))
     x1 = across(one)
-    (mate,) = late_rows(queries, before, at, (1,), [mate], heads, False, one)
+    two = far_rows(0, BLK, one)
+    x2 = across(two)
+    mate = attention_quarter(arrays, before, at, 1, jnp.bfloat16, two)
     mated = swap(mate, "head", 4, 1)
-    two = far_unit(2, [mate])
-    x2 = across(two)
-    three = far_unit(3, [*two, *x1], LONG)
+    own = attention_quarter(arrays, before, at, 0, jnp.bfloat16, [mate])
+    three = far_rows(BLK + HALF, HALF, [own, *x1], LONG)
     x3 = across(three)
-    own = attention_quarter(arrays, before, at, 0, jnp.bfloat16, three)
-    x = [[(y, 0) for y in x1], [(y, HALF) for y in x1], [(y, 0) for y in x2], [(y, 0) for y in x3]]
     out = None
-    for i in range(units):
-        block, row = i * HALF // BLK, i * HALF % BLK
+    low, high = early_l
+    for row, size, (y2, y3) in ((BLK, HALF, x1), (0, BLK, x2), (BLK + HALF, HALF, x3)):
+        l2, l3 = [(y, row) for y in low] if row < BLK else [(y, row - BLK) for y in high]
+        q2, q3 = [(y, row) for y in early_q] if row < share - tail else [(y, BLK) for y in high]
+        o2, o3 = early_out(size, l2, l3, q2, q3, x1[0], x1[1])
         out = norm_rows(
-            at, gain, share, i * HALF, (own, i * HALF), (mated, i * HALF),
-            x[i][0], x[i][1], (early_l[block][0], row), (early_l[block][1], row),
-            (early_q[0], i * HALF), (early_q[1], i * HALF), x1[0], x1[1], out,
+            at, gain, share, row, size, (own, row), (mated, row), (y2, 0), (y3, 0), (o2, 0), (o3, 0), out
         )
     return out
 

time: 81.5 us -> 71.5 us (0.88)
  waiting for transfers between devices: 18.1 us -> 10.7 us
  local copies, waits for them, and re-layouts: 3.59 us -> 1.08 us
  starting transfers between devices: 17.4 us -> 18.7 us
  Pallas kernels: 41.3 us -> 40.3 us
    ppermute x16, waiting for transfers between devices: 18.1 us -> 10.7 us  [swap(): return lax.ppermute(x, axis, [(i, i ^ bit) for i in range(size)])]
    pallas_call x1, Pallas kernels: 6.92 us -> 3.97 us  [block_states(): pl.pallas_call(functools.partial(state_kernel, parts, len(tokens)), in_sp...]
    unnamed x18 -> x12, local copies, waits for them, and re-layouts: 2.52 us -> 0.03 us
    pallas_call x2 -> x6, Pallas kernels: 4.41 us -> 6.13 us  [the longest x2 4.29 us: early_rows(): pl.pallas_call(functools.partial(early_kernel, tail), grid_spec=pltpu.Pre...]
    ppermute x16, starting transfers between devices: 17.4 us -> 18.7 us  [swap(): return lax.ppermute(x, axis, [(i, i ^ bit) for i in range(size)])]
    pallas_call x4 -> x3, Pallas kernels: 10.2 us -> 9.14 us  [norm_rows(): pl.pallas_call(norm_kernel, grid_spec=pltpu.PrefetchScalarGridSpec(num_sc...]
    pallas_call x2, Pallas kernels: 8.84 us -> 9.71 us  [attention_quarter(): pl.pallas_call(kernel, grid_spec=pltpu.PrefetchScalarGridSpec(num_scalar_...]
  transfers between devices with their start and end apart: 16 -> 16, of which waited for: 3 -> 4; matrix products, arithmetic and copies ran while one was open for 0% -> 0% of each run, Pallas kernels for 45% -> 52%
where the time goes in v3:
time: 71.5 us; the launch traced here: 71.1 us
  Pallas kernels  40.3 us (56%)
  starting transfers between devices  18.7 us (26%)
  waiting for transfers between devices  10.7 us (15%)
  local copies, waits for them, and re-layouts  1.08 us (2%)
    ppermute x16, starting transfers between devices, swap(): return lax.ppermute(x, axis, [(i, i ^ bit) for i in range(size)])  18.7 us
    ppermute x16, waiting for transfers between devices, swap(): return lax.ppermute(x, axis, [(i, i ^ bit) for i in range(size)])  10.7 us
    pallas_call x3, Pallas kernels, attention_rows(): pl.pallas_call(kernel, grid_spec=pltpu.PrefetchScalarGridSpec(num_scalar_...  10.3 us
    pallas_call x2, Pallas kernels, attention_quarter(): pl.pallas_call(kernel, grid_spec=pltpu.PrefetchScalarGridSpec(num_scalar_...  9.71 us
    pallas_call x3, Pallas kernels, norm_rows(): pl.pallas_call(norm_kernel, grid_spec=pltpu.PrefetchScalarGridSpec(num_sc...  9.14 us
    pallas_call x2, Pallas kernels, early_rows(): pl.pallas_call(functools.partial(early_kernel, tail), grid_spec=pltpu.Pre...  4.29 us
    pallas_call x1, Pallas kernels, block_states(): pl.pallas_call(functools.partial(state_kernel, parts, len(tokens)), in_sp...  3.97 us
  transfers between devices with their start and end apart: 16, of which 4 were waited for; matrix products, arithmetic and copies ran while one was open for 0% of the time, Pallas kernels for 52%

profile of v3, /device:TPU:1, one launch (start us, length us, event | category | flops | bytes accessed | tf_op | source)
XLA Modules:
  0.0 71.1 jit_solution(548317862068796559)
XLA Ops:
  0.0 1.1 %constant_dynamic-slice_fusion = (bf16[768,128]{1,0:T(8,128)(2,1)S(1)}, bf16[768,128]{1,0:T(8,128)(2,1)S(1)}) fusion(bf16[4096,512]{1,0:T(8,128)(2,1)} %q_ref.13, s32[]{:T(128)S(6)} %select_n.7, s32[]{:T(128)S(6)} %select_n.6), kind=kLoop, calls=%fused_computation | loop fusion | bytes 786440 | tf_op jit(solution)/shard_map/dynamic_slice | solution.py:433
  1.1 2.7 %collective-permute-start.2 = (bf16[768,128]{1,0:T(8,128)(2,1)S(1)}, bf16[768,128]{1,0:T(8,128)(2,1)S(1)}, u32[]{:S(2)}, u32[]{:S(2)}) collective-permute-start(bf16[768,128]{1,0:T(8,128)(2,1)S(1)} %get-tuple-element.55.rest_1_), channel_id=1, source_target_pairs={{0,3},{1,2},{2,1},{3,0},{4,7},{5,6},{6,5},{7,4},{8,11},{9,10},{10,... | collective-permute-start | bytes 589832 | tf_op jit(solution)/shard_map/ppermute | solution.py:415
  3.7 0.0 collective-permute-start.1
  3.7 4.0 %block_states.1 = (f32[8,4,128,128]{3,2,1,0:T(8,128)S(1)}, bf16[4,128,128]{2,1,0:T(8,128)(2,1)S(1)}) custom-call(bf16[4096,512]{1,0:T(8,128)(2,1)} %k_ref.15, bf16[4096,512]{1,0:T(8,128)(2,1)} %v_ref.15, bf16[768,128]{1,0:T(8,128)(2,1)S(1)} %get-tuple-element.56.rest_0_, bf16[768,128]{1,0:T(8,128)(2,1)S(1)} %get-tuple-element.55.rest_1_), custom_call_target="tpu_custom_call" | custom-call | flops 1024 | bytes 1024 | tf_op jit(solution)/shard_map/block_states/pallas_call | solution.py:61
  7.7 0.0 copy-start
  7.7 1.6 %collective-permute-start = (bf16[4,128,128]{2,1,0:T(8,128)(2,1)S(1)}, bf16[4,128,128]{2,1,0:T(8,128)(2,1)}, u32[]{:S(2)}, u32[]{:S(2)}) collective-permute-start(bf16[4,128,128]{2,1,0:T(8,128)(2,1)S(1)} %get-tuple-element.31.rest_0_.total_ref), channel_id=1, source_target_pairs={{0,4},{4,0},{8,12},{12,8},{16,20},{20,16},{24,28},{28,24},{1,5},{5... | collective-permute-start | bytes 393224 | tf_op jit(solution)/shard_map/ppermute | solution.py:415
  9.3 2.1 %early_rows.2 = (bf16[512,128]{1,0:T(8,128)(2,1)S(1)}, bf16[512,128]{1,0:T(8,128)(2,1)S(1)}) custom-call(s32[1]{0:T(128)} %bitcast.head_ref.ids_ref.quarter_ref, bf16[4096,512]{1,0:T(8,128)(2,1)} %q_ref.13, bf16[4096,512]{1,0:T(8,128)(2,1)} %k_ref.15, bf16[4096,512]{1,0:T(8,128)(2,1)} %v_ref.15, f32[8,4,128,128]{3,2,1,0:T(8,128)S(1)} %get-tuple-element.30.within_ref, ...), custom_call_target="tpu_custom_call" | custom-call | flops 1024 | bytes 1024 | tf_op jit(solution)/shard_map/early_rows/pallas_call | solution.py:228
  11.4 1.3 %collective-permute-start.4 = (bf16[512,128]{1,0:T(8,128)(2,1)S(1)}, bf16[512,128]{1,0:T(8,128)(2,1)S(1)}, u32[]{:S(2)}, u32[]{:S(2)}) collective-permute-start(bf16[512,128]{1,0:T(8,128)(2,1)S(1)} %get-tuple-element.32.rest_0_), channel_id=1, source_target_pairs={{0,2},{1,3},{2,0},{3,1},{4,6},{5,7},{6,4},{7,5},{8,10},{9,11},{10,... | collective-permute-start | bytes 393224 | tf_op jit(solution)/shard_map/ppermute | solution.py:415
  12.7 0.9 %collective-permute-start.5 = (bf16[512,128]{1,0:T(8,128)(2,1)S(1)}, bf16[512,128]{1,0:T(8,128)(2,1)S(1)}, u32[]{:S(2)}, u32[]{:S(2)}) collective-permute-start(bf16[512,128]{1,0:T(8,128)(2,1)S(1)} %get-tuple-element.33.rest_1_), channel_id=1, source_target_pairs={{0,3},{1,2},{2,1},{3,0},{4,7},{5,6},{6,5},{7,4},{8,11},{9,10},{10,... | collective-permute-start | bytes 393224 | tf_op jit(solution)/shard_map/ppermute | solution.py:415
  13.6 0.0 collective-permute-done.got_ref
  13.6 0.0 collective-permute-done.2.rest_3_.q3_ref
  13.6 0.0 collective-permute-done.1.rest_2_.q2_ref
  13.6 1.0 %add_step.2 = (bf16[4,128,128]{2,1,0:T(8,128)(2,1)S(1)}, f32[4,128,128]{2,1,0:T(8,128)S(1)}) custom-call(s32[1]{0:T(128)} %bitcast.2.mine_ref.refs_5_, bf16[4,128,128]{2,1,0:T(8,128)(2,1)S(1)} %get-tuple-element.31.rest_0_.total_ref, bf16[4,128,128]{2,1,0:T(8,128)(2,1)} %collective-permute-done.got_ref, bf16[512,128]{1,0:T(8,128)(2,1)S(1)} %get-tuple-element.32.rest_0_, ...), custom_call_target="tpu_custom_call" | custom-call | flops 1024 | bytes 1024 | tf_op jit(solution)/shard_map/add_step/pallas_call | solution.py:399
  14.6 1.4 %collective-permute-start.3 = (bf16[4,128,128]{2,1,0:T(8,128)(2,1)S(1)}, bf16[4,128,128]{2,1,0:T(8,128)(2,1)S(1)}, u32[]{:S(2)}, u32[]{:S(2)}) collective-permute-start(bf16[4,128,128]{2,1,0:T(8,128)(2,1)S(1)} %get-tuple-element.34.rest_1_.total_ref), channel_id=1, source_target_pairs={{0,8},{4,12},{8,0},{12,4},{16,24},{20,28},{24,16},{28,20},{1,9},{5... | collective-permute-start | bytes 393224 | tf_op jit(solution)/shard_map/ppermute | solution.py:415
  16.0 2.2 %early_rows.3 = (bf16[768,128]{1,0:T(8,128)(2,1)S(1)}, bf16[768,128]{1,0:T(8,128)(2,1)S(1)}) custom-call(s32[1]{0:T(128)} %bitcast.head_ref.ids_ref.quarter_ref, bf16[4096,512]{1,0:T(8,128)(2,1)} %q_ref.13, bf16[4096,512]{1,0:T(8,128)(2,1)} %k_ref.15, bf16[4096,512]{1,0:T(8,128)(2,1)} %v_ref.15, f32[8,4,128,128]{3,2,1,0:T(8,128)S(1)} %get-tuple-element.30.within_ref, ...), custom_call_target="tpu_custom_call" | custom-call | flops 1024 | bytes 1024 | tf_op jit(solution)/shard_map/early_rows/pallas_call | solution.py:228
  18.1 1.3 %collective-permute-start.7 = (bf16[768,128]{1,0:T(8,128)(2,1)S(1)}, bf16[768,128]{1,0:T(8,128)(2,1)S(1)}, u32[]{:S(2)}, u32[]{:S(2)}) collective-permute-start(bf16[768,128]{1,0:T(8,128)(2,1)S(1)} %get-tuple-element.36.rest_1_), channel_id=1, source_target_pairs={{0,2},{1,3},{2,0},{3,1},{4,6},{5,7},{6,4},{7,5},{8,10},{9,11},{10,... | collective-permute-start | bytes 589832 | tf_op jit(solution)/shard_map/ppermute | solution.py:415
  19.4 1.1 %collective-permute-start.8 = (bf16[768,128]{1,0:T(8,128)(2,1)S(1)}, bf16[768,128]{1,0:T(8,128)(2,1)S(1)}, u32[]{:S(2)}, u32[]{:S(2)}) collective-permute-start(bf16[768,128]{1,0:T(8,128)(2,1)S(1)} %get-tuple-element.37.rest_2_), channel_id=1, source_target_pairs={{0,3},{1,2},{2,1},{3,0},{4,7},{5,6},{6,5},{7,4},{8,11},{9,10},{10,... | collective-permute-start | bytes 589832 | tf_op jit(solution)/shard_map/ppermute | solution.py:415
  20.5 0.0 collective-permute-done.4.rest_3_.l2_ref
  20.5 0.0 collective-permute-done.5.rest_4_.l3_ref
  20.5 0.0 collective-permute-done.3.got_ref
  20.5 0.1 add_step.3
  20.6 2.4 %collective-permute-start.6 = (bf16[4,128,128]{2,1,0:T(8,128)(2,1)S(1)}, bf16[4,128,128]{2,1,0:T(8,128)(2,1)S(1)}, u32[]{:S(2)}, u32[]{:S(2)}) collective-permute-start(bf16[4,128,128]{2,1,0:T(8,128)(2,1)S(1)} %get-tuple-element.38.rest_0_), channel_id=1, source_target_pairs={{0,16},{4,20},{8,24},{12,28},{16,0},{20,4},{24,8},{28,12},{1,17},{... | collective-permute-start | bytes 393224 | tf_op jit(solution)/shard_map/ppermute | solution.py:415
  23.0 2.5 %attention_rows.3 = (f32[256,384]{1,0:T(8,128)S(1)}, f32[256,384]{1,0:T(8,128)S(1)}) custom-call(s32[1]{0:T(128)} %bitcast.head_ref.ids_ref.quarter_ref, bf16[4096,512]{1,0:T(8,128)(2,1)} %q_ref.13, bf16[4096,512]{1,0:T(8,128)(2,1)} %k_ref.15, bf16[4096,512]{1,0:T(8,128)(2,1)} %v_ref.15, f32[8,4,128,128]{3,2,1,0:T(8,128)S(1)} %get-tuple-element.30.within_ref, ...), custom_call_target="tpu_custom_call" | custom-call | flops 1024 | bytes 1024 | tf_op jit(solution)/shard_map/attention_rows/pallas_call | solution.py:154
  25.4 0.0 collective-permute-done.7.refs_7_.l2_ref.q2_ref
  25.5 3.9 %collective-permute-done.8.refs_8_.l3_ref.q3_ref = bf16[768,128]{1,0:T(8,128)(2,1)S(1)} collective-permute-done((bf16[768,128]{1,0:T(8,128)(2,1)S(1)}, bf16[768,128]{1,0:T(8,128)(2,1)S(1)}, u32[]{:S(2)}, u32[]{:S(2)}) %collective-permute-start.8) | collective-permute-done | bytes 196640 | tf_op jit(solution)/shard_map/ppermute | solution.py:415
  29.3 0.2 collective-permute-done.6.refs_6_
  29.6 1.3 %late_rows.1 = (bf16[304,384]{1,0:T(8,128)(2,1)S(1)}, bf16[304,384]{1,0:T(8,128)(2,1)S(1)}, f32[4,128,128]{2,1,0:T(8,128)S(1)}) custom-call(s32[1]{0:T(128)} %bitcast.head_ref.ids_ref.quarter_ref, bf16[4096,512]{1,0:T(8,128)(2,1)} %q_ref.13, f32[256,384]{1,0:T(8,128)S(1)} %get-tuple-element.39.refs_1_, bf16[4096,512]{1,0:T(8,128)(2,1)} %q_ref.13, ...), custom_call_target="tpu_custom_call" | custom-call | flops 1024 | bytes 1024 | tf_op jit(solution)/shard_map/late_rows/pallas_call | solution.py:289
  30.9 1.3 %collective-permute-start.10 = (bf16[304,384]{1,0:T(8,128)(2,1)S(1)}, bf16[304,384]{1,0:T(8,128)(2,1)S(1)}, u32[]{:S(2)}, u32[]{:S(2)}) collective-permute-start(bf16[304,384]{1,0:T(8,128)(2,1)S(1)} %get-tuple-element.43.rest_1_), channel_id=1, source_target_pairs={{0,2},{1,3},{2,0},{3,1},{4,6},{5,7},{6,4},{7,5},{8,10},{9,11},{10,... | collective-permute-start | bytes 700424 | tf_op jit(solution)/shard_map/ppermute | solution.py:415
  32.2 1.1 %collective-permute-start.11 = (bf16[304,384]{1,0:T(8,128)(2,1)S(1)}, bf16[304,384]{1,0:T(8,128)(2,1)S(1)}, u32[]{:S(2)}, u32[]{:S(2)}) collective-permute-start(bf16[304,384]{1,0:T(8,128)(2,1)S(1)} %get-tuple-element.44.rest_2_), channel_id=1, source_target_pairs={{0,3},{1,2},{2,1},{3,0},{4,7},{5,6},{6,5},{7,4},{8,11},{9,10},{10,... | collective-permute-start | bytes 700424 | tf_op jit(solution)/shard_map/ppermute | solution.py:415
  33.3 4.5 %attention_rows.4 = (bf16[512,384]{1,0:T(8,128)(2,1)}, bf16[512,384]{1,0:T(8,128)(2,1)}) custom-call(s32[1]{0:T(128)} %bitcast.head_ref.ids_ref.quarter_ref, bf16[4096,512]{1,0:T(8,128)(2,1)} %q_ref.13, bf16[4096,512]{1,0:T(8,128)(2,1)} %k_ref.15, bf16[4096,512]{1,0:T(8,128)(2,1)} %v_ref.15, f32[8,4,128,128]{3,2,1,0:T(8,128)S(1)} %get-tuple-element.30.within_ref, ...), custom_call_target="tpu_custom_call" | custom-call | flops 1024 | bytes 1024 | tf_op jit(solution)/shard_map/attention_rows/pallas_call | solution.py:154
  37.8 1.2 %collective-permute-start.14 = (bf16[512,384]{1,0:T(8,128)(2,1)}, bf16[512,384]{1,0:T(8,128)(2,1)}, u32[]{:S(2)}, u32[]{:S(2)}) collective-permute-start(bf16[512,384]{1,0:T(8,128)(2,1)} %get-tuple-element.45.rest_1_), channel_id=1, source_target_pairs={{0,2},{1,3},{2,0},{3,1},{4,6},{5,7},{6,4},{7,5},{8,10},{9,11},{10,... | collective-permute-start | bytes 1179656 | tf_op jit(solution)/shard_map/ppermute | solution.py:415
  39.0 5.2 %attention_quarter.2.rest_1_ = bf16[1024,512]{1,0:T(8,128)(2,1)} custom-call(s32[1]{0:T(128)} %bitcast.head_ref.ids_ref.quarter_ref, bf16[4096,512]{1,0:T(8,128)(2,1)} %q_ref.13, bf16[4096,512]{1,0:T(8,128)(2,1)} %k_ref.15, bf16[4096,512]{1,0:T(8,128)(2,1)} %v_ref.15, f32[8,4,128,128]{3,2,1,0:T(8,128)} %copy-done, ...), custom_call_target="tpu_custom_call" | custom-call | flops 1024 | bytes 1024 | tf_op jit(solution)/shard_map/attention_quarter/pallas_call | solution.py:187
  44.3 0.3 collective-permute-start.15
  44.6 4.5 %attention_quarter.3.rest_1_.own_ref = bf16[1024,512]{1,0:T(8,128)(2,1)S(1)} custom-call(s32[1]{0:T(128)} %bitcast.head_ref.ids_ref.quarter_ref, bf16[4096,512]{1,0:T(8,128)(2,1)} %q_ref.13, bf16[4096,512]{1,0:T(8,128)(2,1)} %k_ref.15, bf16[4096,512]{1,0:T(8,128)(2,1)} %v_ref.15, f32[8,4,128,128]{3,2,1,0:T(8,128)} %copy-done, ...), custom_call_target="tpu_custom_call" | custom-call | flops 1024 | bytes 1024 | tf_op jit(solution)/shard_map/attention_quarter/pallas_call | solution.py:187
  49.0 0.4 collective-permute-start.9
  49.5 0.0 collective-permute-done.11.rest_3_.b3_ref.x3_ref
  49.5 0.0 copy-start.5
  49.5 3.4 %attention_rows.5 = (bf16[256,384]{1,0:T(8,128)(2,1)S(1)}, bf16[256,384]{1,0:T(8,128)(2,1)S(1)}) custom-call(s32[1]{0:T(128)} %bitcast.head_ref.ids_ref.quarter_ref, bf16[4096,512]{1,0:T(8,128)(2,1)} %q_ref.13, bf16[4096,512]{1,0:T(8,128)(2,1)} %k_ref.15, bf16[4096,512]{1,0:T(8,128)(2,1)} %v_ref.15, f32[8,4,128,128]{3,2,1,0:T(8,128)} %copy-done, ...), custom_call_target="tpu_custom_call" | custom-call | flops 999999995904 | bytes 1024 | tf_op jit(solution)/shard_map/attention_rows/pallas_call | solution.py:154
  52.9 1.3 %collective-permute-start.12 = (bf16[256,384]{1,0:T(8,128)(2,1)S(1)}, bf16[256,384]{1,0:T(8,128)(2,1)S(1)}, u32[]{:S(2)}, u32[]{:S(2)}) collective-permute-start(bf16[256,384]{1,0:T(8,128)(2,1)S(1)} %get-tuple-element.47), channel_id=1, source_target_pairs={{0,2},{1,3},{2,0},{3,1},{4,6},{5,7},{6,4},{7,5},{8,10},{9,11},{10,... | collective-permute-start | bytes 589832 | tf_op jit(solution)/shard_map/ppermute | solution.py:415
  54.2 0.6 collective-permute-start.13
  54.7 0.2 early_out.4
  55.0 0.2 early_out.5
  55.1 0.2 early_out.3
  55.3 2.4 %norm_rows.3.rest_0_ = bf16[1024,2048]{1,0:T(8,128)(2,1)} custom-call(s32[1]{0:T(128)} %bitcast.head_ref.ids_ref.quarter_ref, f32[1,2048]{1,0:T(1,128)S(1)} %bitcast.3, bf16[1024,512]{1,0:T(8,128)(2,1)S(1)} %attention_quarter.3.rest_1_.own_ref, bf16[1024,512]{1,0:T(8,128)(2,1)} %collective-permute-done.9.mate_ref, ...), custom_call_target="tpu_custom_call" | custom-call | flops 1024 | bytes 1024 | tf_op jit(solution)/shard_map/norm_rows/pallas_call | solution.py:370
  57.8 3.7 %collective-permute-done.15.x3_ref = bf16[512,384]{1,0:T(8,128)(2,1)} collective-permute-done((bf16[512,384]{1,0:T(8,128)(2,1)}, bf16[512,384]{1,0:T(8,128)(2,1)}, u32[]{:S(2)}, u32[]{:S(2)}) %collective-permute-start.15) | collective-permute-done | bytes 393248 | tf_op jit(solution)/shard_map/ppermute | solution.py:415
  61.5 4.3 %norm_rows.4.rest_0_ = bf16[1024,2048]{1,0:T(8,128)(2,1)} custom-call(s32[1]{0:T(128)} %bitcast.head_ref.ids_ref.quarter_ref, f32[1,2048]{1,0:T(1,128)S(1)} %bitcast.4, bf16[1024,512]{1,0:T(8,128)(2,1)S(1)} %attention_quarter.3.rest_1_.own_ref, bf16[1024,512]{1,0:T(8,128)(2,1)} %collective-permute-done.9.mate_ref, ...), custom_call_target="tpu_custom_call", output_to_operand_aliasing={{}: (8, {})} | custom-call | flops 1024 | bytes 1024 | tf_op jit(solution)/shard_map/norm_rows/pallas_call | solution.py:370
  65.8 2.8 %collective-permute-done.13.x3_ref = bf16[256,384]{1,0:T(8,128)(2,1)S(1)} collective-permute-done((bf16[256,384]{1,0:T(8,128)(2,1)S(1)}, bf16[256,384]{1,0:T(8,128)(2,1)S(1)}, u32[]{:S(2)}, u32[]{:S(2)}) %collective-permute-start.13) | collective-permute-done | bytes 196640 | tf_op jit(solution)/shard_map/ppermute | solution.py:415
  68.7 2.4 %norm_rows.5 = bf16[1024,2048]{1,0:T(8,128)(2,1)} custom-call(s32[1]{0:T(128)} %bitcast.head_ref.ids_ref.quarter_ref, f32[1,2048]{1,0:T(1,128)S(1)} %bitcast.5, bf16[1024,512]{1,0:T(8,128)(2,1)S(1)} %attention_quarter.3.rest_1_.own_ref, bf16[1024,512]{1,0:T(8,128)(2,1)} %collective-permute-done.9.mate_ref, ...), custom_call_target="tpu_custom_call", output_to_operand_aliasing={{}: (8, {})} | custom-call | flops 1024 | bytes 1024 | tf_op jit(solution)/shard_map/norm_rows/pallas_call | solution.py:370
  (14 shorter events, 0.0 us)
Async XLA Ops:
  1.1 12.6 %collective-permute-start.2 = (bf16[768,128]{1,0:T(8,128)(2,1)S(1)}, bf16[768,128]{1,0:T(8,128)(2,1)S(1)}, u32[]{:S(2)}, u32[]{:S(2)}) collective-permute-start(bf16[768,128]{1,0:T(8,128)(2,1)S(1)} %get-tuple-element.55.rest_1_), channel_id=1, source_target_pairs={{0,3},{1,2},{2,1},{3,0},{4,7},{5,6},{6,5},{7,4},{8,11},{9,10},{10,... | collective-permute-start | bytes 589832 | tf_op jit(solution)/shard_map/ppermute | solution.py:415
  3.7 9.9 %collective-permute-start.1 = (bf16[768,128]{1,0:T(8,128)(2,1)S(1)}, bf16[768,128]{1,0:T(8,128)(2,1)S(1)}, u32[]{:S(2)}, u32[]{:S(2)}) collective-permute-start(bf16[768,128]{1,0:T(8,128)(2,1)S(1)} %get-tuple-element.56.rest_0_), channel_id=1, source_target_pairs={{0,2},{1,3},{2,0},{3,1},{4,6},{5,7},{6,4},{7,5},{8,10},{9,11},{10,... | collective-permute-start | bytes 589832 | tf_op jit(solution)/shard_map/ppermute | solution.py:415
  7.7 25.6 %copy-start = (f32[8,4,128,128]{3,2,1,0:T(8,128)}, f32[8,4,128,128]{3,2,1,0:T(8,128)S(1)}, u32[]{:S(2)}) copy-start(f32[8,4,128,128]{3,2,1,0:T(8,128)S(1)} %get-tuple-element.30.within_ref) | copy-start | bytes 6291460
  7.7 5.9 %collective-permute-start = (bf16[4,128,128]{2,1,0:T(8,128)(2,1)S(1)}, bf16[4,128,128]{2,1,0:T(8,128)(2,1)}, u32[]{:S(2)}, u32[]{:S(2)}) collective-permute-start(bf16[4,128,128]{2,1,0:T(8,128)(2,1)S(1)} %get-tuple-element.31.rest_0_.total_ref), channel_id=1, source_target_pairs={{0,4},{4,0},{8,12},{12,8},{16,20},{20,16},{24,28},{28,24},{1,5},{5... | collective-permute-start | bytes 393224 | tf_op jit(solution)/shard_map/ppermute | solution.py:415
  11.4 9.1 %collective-permute-start.4 = (bf16[512,128]{1,0:T(8,128)(2,1)S(1)}, bf16[512,128]{1,0:T(8,128)(2,1)S(1)}, u32[]{:S(2)}, u32[]{:S(2)}) collective-permute-start(bf16[512,128]{1,0:T(8,128)(2,1)S(1)} %get-tuple-element.32.rest_0_), channel_id=1, source_target_pairs={{0,2},{1,3},{2,0},{3,1},{4,6},{5,7},{6,4},{7,5},{8,10},{9,11},{10,... | collective-permute-start | bytes 393224 | tf_op jit(solution)/shard_map/ppermute | solution.py:415
  12.7 7.8 %collective-permute-start.5 = (bf16[512,128]{1,0:T(8,128)(2,1)S(1)}, bf16[512,128]{1,0:T(8,128)(2,1)S(1)}, u32[]{:S(2)}, u32[]{:S(2)}) collective-permute-start(bf16[512,128]{1,0:T(8,128)(2,1)S(1)} %get-tuple-element.33.rest_1_), channel_id=1, source_target_pairs={{0,3},{1,2},{2,1},{3,0},{4,7},{5,6},{6,5},{7,4},{8,11},{9,10},{10,... | collective-permute-start | bytes 393224 | tf_op jit(solution)/shard_map/ppermute | solution.py:415
  14.6 5.9 %collective-permute-start.3 = (bf16[4,128,128]{2,1,0:T(8,128)(2,1)S(1)}, bf16[4,128,128]{2,1,0:T(8,128)(2,1)S(1)}, u32[]{:S(2)}, u32[]{:S(2)}) collective-permute-start(bf16[4,128,128]{2,1,0:T(8,128)(2,1)S(1)} %get-tuple-element.34.rest_1_.total_ref), channel_id=1, source_target_pairs={{0,8},{4,12},{8,0},{12,4},{16,24},{20,28},{24,16},{28,20},{1,9},{5... | collective-permute-start | bytes 393224 | tf_op jit(solution)/shard_map/ppermute | solution.py:415
  18.1 7.3 %collective-permute-start.7 = (bf16[768,128]{1,0:T(8,128)(2,1)S(1)}, bf16[768,128]{1,0:T(8,128)(2,1)S(1)}, u32[]{:S(2)}, u32[]{:S(2)}) collective-permute-start(bf16[768,128]{1,0:T(8,128)(2,1)S(1)} %get-tuple-element.36.rest_1_), channel_id=1, source_target_pairs={{0,2},{1,3},{2,0},{3,1},{4,6},{5,7},{6,4},{7,5},{8,10},{9,11},{10,... | collective-permute-start | bytes 589832 | tf_op jit(solution)/shard_map/ppermute | solution.py:415
  19.4 9.9 %collective-permute-start.8 = (bf16[768,128]{1,0:T(8,128)(2,1)S(1)}, bf16[768,128]{1,0:T(8,128)(2,1)S(1)}, u32[]{:S(2)}, u32[]{:S(2)}) collective-permute-start(bf16[768,128]{1,0:T(8,128)(2,1)S(1)} %get-tuple-element.37.rest_2_), channel_id=1, source_target_pairs={{0,3},{1,2},{2,1},{3,0},{4,7},{5,6},{6,5},{7,4},{8,11},{9,10},{10,... | collective-permute-start | bytes 589832 | tf_op jit(solution)/shard_map/ppermute | solution.py:415
  20.6 9.0 %collective-permute-start.6 = (bf16[4,128,128]{2,1,0:T(8,128)(2,1)S(1)}, bf16[4,128,128]{2,1,0:T(8,128)(2,1)S(1)}, u32[]{:S(2)}, u32[]{:S(2)}) collective-permute-start(bf16[4,128,128]{2,1,0:T(8,128)(2,1)S(1)} %get-tuple-element.38.rest_0_), channel_id=1, source_target_pairs={{0,16},{4,20},{8,24},{12,28},{16,0},{20,4},{24,8},{28,12},{1,17},{... | collective-permute-start | bytes 393224 | tf_op jit(solution)/shard_map/ppermute | solution.py:415
  25.5 5.4 %copy-start.1 = (bf16[768,128]{1,0:T(8,128)(2,1)}, bf16[768,128]{1,0:T(8,128)(2,1)S(1)}, u32[]{:S(2)}) copy-start(bf16[768,128]{1,0:T(8,128)(2,1)S(1)} %collective-permute-done.7.refs_7_.l2_ref.q2_ref) | copy-start | bytes 589828
  29.3 1.6 %copy-start.3 = (bf16[768,128]{1,0:T(8,128)(2,1)}, bf16[768,128]{1,0:T(8,128)(2,1)S(1)}, u32[]{:S(2)}) copy-start(bf16[768,128]{1,0:T(8,128)(2,1)S(1)} %collective-permute-done.8.refs_8_.l3_ref.q3_ref) | copy-start | bytes 589828
  30.9 18.6 %collective-permute-start.10 = (bf16[304,384]{1,0:T(8,128)(2,1)S(1)}, bf16[304,384]{1,0:T(8,128)(2,1)S(1)}, u32[]{:S(2)}, u32[]{:S(2)}) collective-permute-start(bf16[304,384]{1,0:T(8,128)(2,1)S(1)} %get-tuple-element.43.rest_1_), channel_id=1, source_target_pairs={{0,2},{1,3},{2,0},{3,1},{4,6},{5,7},{6,4},{7,5},{8,10},{9,11},{10,... | collective-permute-start | bytes 700424 | tf_op jit(solution)/shard_map/ppermute | solution.py:415
  32.2 17.3 %collective-permute-start.11 = (bf16[304,384]{1,0:T(8,128)(2,1)S(1)}, bf16[304,384]{1,0:T(8,128)(2,1)S(1)}, u32[]{:S(2)}, u32[]{:S(2)}) collective-permute-start(bf16[304,384]{1,0:T(8,128)(2,1)S(1)} %get-tuple-element.44.rest_2_), channel_id=1, source_target_pairs={{0,3},{1,2},{2,1},{3,0},{4,7},{5,6},{6,5},{7,4},{8,11},{9,10},{10,... | collective-permute-start | bytes 700424 | tf_op jit(solution)/shard_map/ppermute | solution.py:415
  37.8 19.9 %collective-permute-start.14 = (bf16[512,384]{1,0:T(8,128)(2,1)}, bf16[512,384]{1,0:T(8,128)(2,1)}, u32[]{:S(2)}, u32[]{:S(2)}) collective-permute-start(bf16[512,384]{1,0:T(8,128)(2,1)} %get-tuple-element.45.rest_1_), channel_id=1, source_target_pairs={{0,2},{1,3},{2,0},{3,1},{4,6},{5,7},{6,4},{7,5},{8,10},{9,11},{10,... | collective-permute-start | bytes 1179656 | tf_op jit(solution)/shard_map/ppermute | solution.py:415
  44.3 17.2 %collective-permute-start.15 = (bf16[512,384]{1,0:T(8,128)(2,1)}, bf16[512,384]{1,0:T(8,128)(2,1)}, u32[]{:S(2)}, u32[]{:S(2)}) collective-permute-start(bf16[512,384]{1,0:T(8,128)(2,1)} %get-tuple-element.46.rest_2_), channel_id=1, source_target_pairs={{0,3},{1,2},{2,1},{3,0},{4,7},{5,6},{6,5},{7,4},{8,11},{9,10},{10,... | collective-permute-start | bytes 1179656 | tf_op jit(solution)/shard_map/ppermute | solution.py:415
  49.0 6.3 %collective-permute-start.9 = (bf16[1024,512]{1,0:T(8,128)(2,1)}, bf16[1024,512]{1,0:T(8,128)(2,1)}, u32[]{:S(2)}, u32[]{:S(2)}) collective-permute-start(bf16[1024,512]{1,0:T(8,128)(2,1)} %attention_quarter.2.rest_1_), channel_id=1, source_target_pairs={{0,1},{1,0},{2,3},{3,2},{4,5},{5,4},{6,7},{7,6},{8,9},{9,8},{10,11... | collective-permute-start | bytes 3145736 | tf_op jit(solution)/shard_map/ppermute | solution.py:415
  49.5 5.5 %copy-start.2 = (bf16[768,128]{1,0:T(8,128)(2,1)S(1)}, bf16[768,128]{1,0:T(8,128)(2,1)}, u32[]{:S(2)}) copy-start(bf16[768,128]{1,0:T(8,128)(2,1)} %copy-done.1) | copy-start | bytes 589828
  49.5 5.5 %copy-start.4 = (bf16[768,128]{1,0:T(8,128)(2,1)S(1)}, bf16[768,128]{1,0:T(8,128)(2,1)}, u32[]{:S(2)}) copy-start(bf16[768,128]{1,0:T(8,128)(2,1)} %copy-done.3) | copy-start | bytes 589828
  49.5 5.9 %copy-start.5 = (f32[2048]{0:T(1024)S(1)}, f32[2048]{0:T(1024)}, u32[]{:S(2)}) copy-start(f32[2048]{0:T(1024)} %param.7) | copy-start | bytes 24580
  52.9 13.0 %collective-permute-start.12 = (bf16[256,384]{1,0:T(8,128)(2,1)S(1)}, bf16[256,384]{1,0:T(8,128)(2,1)S(1)}, u32[]{:S(2)}, u32[]{:S(2)}) collective-permute-start(bf16[256,384]{1,0:T(8,128)(2,1)S(1)} %get-tuple-element.47), channel_id=1, source_target_pairs={{0,2},{1,3},{2,0},{3,1},{4,6},{5,7},{6,4},{7,5},{8,10},{9,11},{10,... | collective-permute-start | bytes 589832 | tf_op jit(solution)/shard_map/ppermute | solution.py:415
  54.2 14.5 %collective-permute-start.13 = (bf16[256,384]{1,0:T(8,128)(2,1)S(1)}, bf16[256,384]{1,0:T(8,128)(2,1)S(1)}, u32[]{:S(2)}, u32[]{:S(2)}) collective-permute-start(bf16[256,384]{1,0:T(8,128)(2,1)S(1)} %get-tuple-element.48), channel_id=1, source_target_pairs={{0,3},{1,2},{2,1},{3,0},{4,7},{5,6},{6,5},{7,4},{8,11},{9,10},{10,... | collective-permute-start | bytes 589832 | tf_op jit(solution)/shard_map/ppermute | solution.py:415

commit v4 on v3

--- a/solution.py
+++ b/solution.py
@@ -43,7 +43,7 @@
             at = pl.ds(n * BLK, BLK)
             for h in range(heads):
                 cols = pl.ds(h * DH, DH)
-                within_ref[n, h] = acc[h]
+                within_ref[n, h] = acc[h].astype(jnp.bfloat16)
                 acc[h] = acc[h] + lax.dot_general(
                     k_buf[at, cols], v_buf[at, cols], (((0,), (0,)), ((), ())),
                     preferred_element_type=jnp.float32,
@@ -63,7 +63,7 @@
         in_specs=[anywhere, anywhere] + [anywhere] * len(tokens),
         out_specs=[vmem, vmem],
         out_shape=[
-            jax.ShapeDtypeStruct((blocks, heads, DH, DH), jnp.float32),
+            jax.ShapeDtypeStruct((blocks, heads, DH, DH), jnp.bfloat16),
             jax.ShapeDtypeStruct((heads, DH, DH), jnp.bfloat16),
         ],
         scratch_shapes=[
@@ -78,14 +78,14 @@
     )(keys, values, *tokens)
 
 
-def attend(first, halves, heads, q_ref, k_ref, v_ref, within_ref, before_ref, out_ref):
+def attend(first, halves, heads, q_ref, k_ref, v_ref, within_ref, before_ref, *out_refs):
     row = lax.broadcasted_iota(jnp.int32, (HALF, HALF), 0)
     col = lax.broadcasted_iota(jnp.int32, (HALF, HALF), 1)
     for h in range(heads):
         cols = pl.ds(h * DH, DH)
         state = within_ref[0, h]
         if before_ref is not None:
-            state = state + before_ref[h]
+            state = state.astype(jnp.float32) + before_ref[h]
         q = q_ref[:, cols]
         out = jnp.dot(q, state.astype(jnp.bfloat16), preferred_element_type=jnp.float32)
         outs = [out[i * HALF:(i + 1) * HALF] for i in range(halves)]
@@ -107,10 +107,14 @@
             for i in range(start, halves):
                 outs[i] = outs[i] + more[(i - start) * HALF:(i - start + 1) * HALF]
         for i in range(halves):
-            out_ref[pl.ds(i * HALF, HALF), cols] = outs[i].astype(out_ref.dtype)
-
-
-def attention_rows(arrays, before, at, sides, start, size, head, heads, kind, tokens, cost=None):
+            part = HALF if len(out_refs) == 1 else HALF * halves // len(out_refs)
+            for r in range(0, HALF, part):
+                out_ref = out_refs[0] if len(out_refs) == 1 else out_refs[(i * HALF + r) // part]
+                low_row = i * HALF if len(out_refs) == 1 else 0
+                out_ref[pl.ds(low_row, part), cols] = outs[i][r:r + part].astype(out_ref.dtype)
+
+
+def attention_rows(arrays, before, at, sides, start, size, head, heads, kind, tokens, cost=None, cut=1):
     queries, keys, values, within = arrays
     rows, width = queries.shape
     share = rows // 4
@@ -145,11 +149,12 @@
 
     def kernel(ids_ref, q_ref, k_ref, v_ref, within_ref, *rest):
         before_ref = None if before is None else rest[0]
-        outs = rest[len(rest) - count:]
+        outs = rest[len(rest) - count * cut:]
         for n in range(count):
             @pl.when(pl.program_id(0) == n)
             def _(n=n):
-                attend(first, halves, heads, q_ref, k_ref, v_ref, within_ref, before_ref, outs[n])
+                mine = outs[n * cut:(n + 1) * cut]
+                attend(first, halves, heads, q_ref, k_ref, v_ref, within_ref, before_ref, *mine)
 
     return pl.pallas_call(
         kernel,
@@ -157,9 +162,9 @@
             num_scalar_prefetch=1,
             grid=(count,),
             in_specs=in_specs,
-            out_specs=[pl.BlockSpec((size, span), lambda n, s: (0, 0))] * count,
+            out_specs=[pl.BlockSpec((size // cut, span), lambda n, s: (0, 0))] * (count * cut),
         ),
-        out_shape=[jax.ShapeDtypeStruct((size, span), kind)] * count,
+        out_shape=[jax.ShapeDtypeStruct((size // cut, span), kind)] * (count * cut),
         compiler_params=params(),
         cost_estimate=COST if cost is None else cost,
         name="attention_rows",
@@ -333,6 +338,58 @@
     )(l2[0], l3[0], q2[0], q3[0], b2, b3)
 
 
+def gather_kernel(own_ref, mate_ref, o2_ref, o3_ref, out_ref):
+    first = 0
+    for ref in (own_ref, mate_ref, o2_ref, o3_ref):
+        out_ref[:, pl.ds(first, ref.shape[1])] = ref[...]
+        first += ref.shape[1]
+
+
+def gather_rows(size, *pairs):
+    def at(pair):
+        index = pair[1] // size
+        return pl.BlockSpec((size, pair[0].shape[1]), lambda n: (index, 0))
+
+    width = sum(pair[0].shape[1] for pair in pairs)
+    return pl.pallas_call(
+        gather_kernel,
+        grid=(1,),
+        in_specs=[at(pair) for pair in pairs],
+        out_specs=pl.BlockSpec((size, width), lambda n: (0, 0)),
+        out_shape=jax.ShapeDtypeStruct((size, width), jnp.bfloat16),
+        compiler_params=params(),
+        cost_estimate=COST,
+        name="gather_rows",
+    )(*[pair[0] for pair in pairs])
+
+
+def norm_last(head, gain, share, row, near, x2, x3, out):
+    size, narrow = x2.shape
+    width = narrow + DH
+    index = row // size
+    vmem = pl.BlockSpec(memory_space=pltpu.VMEM)
+
+    def kernel(head_ref, gain_ref, near_ref, x2_ref, x3_ref, old_ref, out_ref):
+        cut = [0, width, 2 * width, 2 * width + DH, 2 * width + 2 * DH]
+        refs = [near_ref.at[:, pl.ds(a, b - a)] for a, b in zip(cut, cut[1:])]
+        norm_kernel(head_ref, gain_ref, refs[0], refs[1], x2_ref, x3_ref, refs[2], refs[3], out_ref)
+
+    return pl.pallas_call(
+        kernel,
+        grid_spec=pltpu.PrefetchScalarGridSpec(
+            num_scalar_prefetch=1,
+            grid=(1,),
+            in_specs=[vmem] * 4 + [pl.BlockSpec(memory_space=pl.ANY)],
+            out_specs=pl.BlockSpec((size, 4 * width), lambda n, s: (index, 0)),
+        ),
+        out_shape=jax.ShapeDtypeStruct((share, 4 * width), jnp.bfloat16),
+        input_output_aliases={5: 0},
+        compiler_params=params(),
+        cost_estimate=COST,
+        name="norm_last",
+    )(head, gain, near, x2, x3, out)
+
+
 def norm_kernel(head_ref, gain_ref, own_ref, mate_ref, x2_ref, x3_ref, o2_ref, o3_ref, *rest):
     out_ref = rest[-1]
     head = head_ref[0]
@@ -341,10 +398,12 @@
         (own_ref, 0, 0), (mate_ref, 1, 0), (x2_ref, 2, 0), (o2_ref, 2, width - DH), (x3_ref, 3, 0),
         (o3_ref, 3, width - DH),
     )
-    total = 0.0
+    total = jnp.zeros((own_ref.shape[0], DH), jnp.float32)
     for ref, _, _ in pieces:
-        wide = ref[...].astype(jnp.float32)
-        total += jnp.sum(wide * wide, axis=-1, keepdims=True)
+        for c in range(ref.shape[1] // DH):
+            wide = ref[:, pl.ds(c * DH, DH)].astype(jnp.float32)
+            total += wide * wide
+    total = jnp.sum(total, axis=-1, keepdims=True)
     scale = lax.rsqrt(total / (4 * width) + EPS)
     for ref, partner, offset in pieces:
         at = pl.multiple_of((head ^ partner) * width + offset, DH)
@@ -450,8 +509,8 @@
             group, before = add_step(mine, bit, group, got, before, tokens)
         bit, step = bit * 2, step + 1
 
-    def far_rows(start, size, tokens, cost=None):
-        return attention_rows(arrays, before, at, far, start, size, 0, heads - 1, jnp.bfloat16, tokens, cost)
+    def far_rows(start, size, tokens, cost=None, cut=1):
+        return attention_rows(arrays, before, at, far, start, size, 0, heads - 1, jnp.bfloat16, tokens, cost, cut)
 
     *one, before = late_rows(queries, before, at, far, BLK, first, heads - 1, True, early_l[1], (mine, bit // 2, got))
     x1 = across(one)
@@ -460,18 +519,21 @@
     mate = attention_quarter(arrays, before, at, 1, jnp.bfloat16, two)
     mated = swap(mate, "head", 4, 1)
     own = attention_quarter(arrays, before, at, 0, jnp.bfloat16, [mate])
-    three = far_rows(BLK + HALF, HALF, [own, *x1], LONG)
-    x3 = across(three)
+    three = far_rows(BLK + HALF, HALF, [own, *x1], LONG, 2)
+    x3, x4 = across(three[0::2]), across(three[1::2])
     out = None
     low, high = early_l
+    end = share - HALF // 2
     for row, size, (y2, y3) in ((BLK, HALF, x1), (0, BLK, x2), (BLK + HALF, HALF, x3)):
         l2, l3 = [(y, row) for y in low] if row < BLK else [(y, row - BLK) for y in high]
         q2, q3 = [(y, row) for y in early_q] if row < share - tail else [(y, BLK) for y in high]
         o2, o3 = early_out(size, l2, l3, q2, q3, x1[0], x1[1])
+        size = min(size, end - row)
         out = norm_rows(
             at, gain, share, row, size, (own, row), (mated, row), (y2, 0), (y3, 0), (o2, 0), (o3, 0), out
         )
-    return out
+    near = gather_rows(share - end, (own, end), (mated, end), (o2, HALF // 2), (o3, HALF // 2))
+    return norm_last(at, gain, share, end, near, x4[0], x4[1], out)
 
 
 def solution(mesh):

time: 71.5 us -> 70 us (0.979)
  waiting for transfers between devices: 10.7 us -> 7.54 us
  starting transfers between devices: 18.7 us -> 20.3 us
    ppermute x16 -> x18, waiting for transfers between devices: 10.7 us -> 7.54 us  [swap(): return lax.ppermute(x, axis, [(i, i ^ bit) for i in range(size)])]
    pallas_call x0 -> x2, Pallas kernels: none -> 2 us  [the longest x1 1.06 us: norm_last(): pl.pallas_call(kernel, grid_spec=pltpu.PrefetchScalarGridSpec(num_scalar_...]
    ppermute x16 -> x18, starting transfers between devices: 18.7 us -> 20.3 us  [swap(): return lax.ppermute(x, axis, [(i, i ^ bit) for i in range(size)])]
    pallas_call x2, Pallas kernels: 1.02 us -> 0.12 us  [add_step(): pl.pallas_call(functools.partial(add_kernel, bit, before is not None), in...]
    pallas_call x3, Pallas kernels: 9.14 us -> 8.41 us  [norm_rows(): pl.pallas_call(norm_kernel, grid_spec=pltpu.PrefetchScalarGridSpec(num_sc...]
  transfers between devices with their start and end apart: 16 -> 18, of which waited for: 4 -> 4; matrix products, arithmetic and copies ran while one was open for 0% -> 0% of each run, Pallas kernels for 52% -> 55%
where the time goes in v4:
time: 70 us; the launch traced here: 69.6 us
  Pallas kernels  40.5 us (58%)
  starting transfers between devices  20.3 us (29%)
  waiting for transfers between devices  7.54 us (11%)
  local copies, waits for them, and re-layouts  1.08 us (2%)
    ppermute x18, starting transfers between devices, swap(): return lax.ppermute(x, axis, [(i, i ^ bit) for i in range(size)])  20.3 us
    pallas_call x3, Pallas kernels, attention_rows(): pl.pallas_call(kernel, grid_spec=pltpu.PrefetchScalarGridSpec(num_scalar_...  10.3 us
    pallas_call x2, Pallas kernels, attention_quarter(): pl.pallas_call(kernel, grid_spec=pltpu.PrefetchScalarGridSpec(num_scalar_...  9.58 us
    pallas_call x3, Pallas kernels, norm_rows(): pl.pallas_call(norm_kernel, grid_spec=pltpu.PrefetchScalarGridSpec(num_sc...  8.41 us
    ppermute x18, waiting for transfers between devices, swap(): return lax.ppermute(x, axis, [(i, i ^ bit) for i in range(size)])  7.54 us
    pallas_call x2, Pallas kernels, early_rows(): pl.pallas_call(functools.partial(early_kernel, tail), grid_spec=pltpu.Pre...  4.28 us
    pallas_call x1, Pallas kernels, block_states(): pl.pallas_call(functools.partial(state_kernel, parts, len(tokens)), in_sp...  3.97 us
  transfers between devices with their start and end apart: 18, of which 4 were waited for; matrix products, arithmetic and copies ran while one was open for 0% of the time, Pallas kernels for 55%

profile of v4, /device:TPU:1, one launch (start us, length us, event | category | flops | bytes accessed | tf_op | source)
XLA Modules:
  0.0 69.6 jit_solution(13905596807866525016)
XLA Ops:
  0.0 1.1 %constant_dynamic-slice_fusion = (bf16[768,128]{1,0:T(8,128)(2,1)S(1)}, bf16[768,128]{1,0:T(8,128)(2,1)S(1)}) fusion(bf16[4096,512]{1,0:T(8,128)(2,1)} %q_ref.13, s32[]{:T(128)S(6)} %select_n.7, s32[]{:T(128)S(6)} %select_n.6), kind=kLoop, calls=%fused_computation | loop fusion | bytes 786440 | tf_op jit(solution)/shard_map/dynamic_slice | solution.py:492
  1.1 2.7 %collective-permute-start.2 = (bf16[768,128]{1,0:T(8,128)(2,1)S(1)}, bf16[768,128]{1,0:T(8,128)(2,1)S(1)}, u32[]{:S(2)}, u32[]{:S(2)}) collective-permute-start(bf16[768,128]{1,0:T(8,128)(2,1)S(1)} %get-tuple-element.59.rest_1_), channel_id=1, source_target_pairs={{0,3},{1,2},{2,1},{3,0},{4,7},{5,6},{6,5},{7,4},{8,11},{9,10},{10,... | collective-permute-start | bytes 589832 | tf_op jit(solution)/shard_map/ppermute | solution.py:474
  3.7 4.0 %block_states.1 = (bf16[8,4,128,128]{3,2,1,0:T(8,128)(2,1)S(1)}, bf16[4,128,128]{2,1,0:T(8,128)(2,1)S(1)}) custom-call(bf16[4096,512]{1,0:T(8,128)(2,1)} %k_ref.15, bf16[4096,512]{1,0:T(8,128)(2,1)} %v_ref.15, bf16[768,128]{1,0:T(8,128)(2,1)S(1)} %get-tuple-element.60.rest_0_, bf16[768,128]{1,0:T(8,128)(2,1)S(1)} %get-tuple-element.59.rest_1_), custom_call_target="tpu_custom_call" | custom-call | flops 1024 | bytes 1024 | tf_op jit(solution)/shard_map/block_states/pallas_call | solution.py:61
  7.7 1.6 %collective-permute-start = (bf16[4,128,128]{2,1,0:T(8,128)(2,1)S(1)}, bf16[4,128,128]{2,1,0:T(8,128)(2,1)S(1)}, u32[]{:S(2)}, u32[]{:S(2)}) collective-permute-start(bf16[4,128,128]{2,1,0:T(8,128)(2,1)S(1)} %get-tuple-element.33.rest_0_.total_ref), channel_id=1, source_target_pairs={{0,4},{4,0},{8,12},{12,8},{16,20},{20,16},{24,28},{28,24},{1,5},{5... | collective-permute-start | bytes 393224 | tf_op jit(solution)/shard_map/ppermute | solution.py:474
  9.3 2.1 %early_rows.2 = (bf16[512,128]{1,0:T(8,128)(2,1)S(1)}, bf16[512,128]{1,0:T(8,128)(2,1)S(1)}) custom-call(s32[1]{0:T(128)} %bitcast.head_ref.ids_ref.quarter_ref, bf16[4096,512]{1,0:T(8,128)(2,1)} %q_ref.13, bf16[4096,512]{1,0:T(8,128)(2,1)} %k_ref.15, bf16[4096,512]{1,0:T(8,128)(2,1)} %v_ref.15, bf16[8,4,128,128]{3,2,1,0:T(8,128)(2,1)S(1)} %get-tuple-element.32.within_ref, ...), custom_call_target="tpu_custom_call" | custom-call | flops 1024 | bytes 1024 | tf_op jit(solution)/shard_map/early_rows/pallas_call | solution.py:233
  11.4 1.3 %collective-permute-start.4 = (bf16[512,128]{1,0:T(8,128)(2,1)S(1)}, bf16[512,128]{1,0:T(8,128)(2,1)S(1)}, u32[]{:S(2)}, u32[]{:S(2)}) collective-permute-start(bf16[512,128]{1,0:T(8,128)(2,1)S(1)} %get-tuple-element.34.rest_0_), channel_id=1, source_target_pairs={{0,2},{1,3},{2,0},{3,1},{4,6},{5,7},{6,4},{7,5},{8,10},{9,11},{10,... | collective-permute-start | bytes 393224 | tf_op jit(solution)/shard_map/ppermute | solution.py:474
  12.7 0.9 %collective-permute-start.5 = (bf16[512,128]{1,0:T(8,128)(2,1)S(1)}, bf16[512,128]{1,0:T(8,128)(2,1)S(1)}, u32[]{:S(2)}, u32[]{:S(2)}) collective-permute-start(bf16[512,128]{1,0:T(8,128)(2,1)S(1)} %get-tuple-element.35.rest_1_), channel_id=1, source_target_pairs={{0,3},{1,2},{2,1},{3,0},{4,7},{5,6},{6,5},{7,4},{8,11},{9,10},{10,... | collective-permute-start | bytes 393224 | tf_op jit(solution)/shard_map/ppermute | solution.py:474
  13.6 0.0 collective-permute-done.got_ref
  13.6 0.0 collective-permute-done.2.rest_3_.q3_ref
  13.6 0.0 collective-permute-done.1.rest_2_.q2_ref
  13.6 0.1 add_step.2
  13.7 1.4 %collective-permute-start.3 = (bf16[4,128,128]{2,1,0:T(8,128)(2,1)S(1)}, bf16[4,128,128]{2,1,0:T(8,128)(2,1)S(1)}, u32[]{:S(2)}, u32[]{:S(2)}) collective-permute-start(bf16[4,128,128]{2,1,0:T(8,128)(2,1)S(1)} %get-tuple-element.36.rest_1_.total_ref), channel_id=1, source_target_pairs={{0,8},{4,12},{8,0},{12,4},{16,24},{20,28},{24,16},{28,20},{1,9},{5... | collective-permute-start | bytes 393224 | tf_op jit(solution)/shard_map/ppermute | solution.py:474
  15.0 2.2 %early_rows.3 = (bf16[768,128]{1,0:T(8,128)(2,1)S(1)}, bf16[768,128]{1,0:T(8,128)(2,1)S(1)}) custom-call(s32[1]{0:T(128)} %bitcast.head_ref.ids_ref.quarter_ref, bf16[4096,512]{1,0:T(8,128)(2,1)} %q_ref.13, bf16[4096,512]{1,0:T(8,128)(2,1)} %k_ref.15, bf16[4096,512]{1,0:T(8,128)(2,1)} %v_ref.15, bf16[8,4,128,128]{3,2,1,0:T(8,128)(2,1)S(1)} %get-tuple-element.32.within_ref, ...), custom_call_target="tpu_custom_call" | custom-call | flops 1024 | bytes 1024 | tf_op jit(solution)/shard_map/early_rows/pallas_call | solution.py:233
  17.2 1.3 %collective-permute-start.7 = (bf16[768,128]{1,0:T(8,128)(2,1)S(1)}, bf16[768,128]{1,0:T(8,128)(2,1)S(1)}, u32[]{:S(2)}, u32[]{:S(2)}) collective-permute-start(bf16[768,128]{1,0:T(8,128)(2,1)S(1)} %get-tuple-element.38.rest_1_), channel_id=1, source_target_pairs={{0,2},{1,3},{2,0},{3,1},{4,6},{5,7},{6,4},{7,5},{8,10},{9,11},{10,... | collective-permute-start | bytes 589832 | tf_op jit(solution)/shard_map/ppermute | solution.py:474
  18.5 1.1 %collective-permute-start.8 = (bf16[768,128]{1,0:T(8,128)(2,1)S(1)}, bf16[768,128]{1,0:T(8,128)(2,1)S(1)}, u32[]{:S(2)}, u32[]{:S(2)}) collective-permute-start(bf16[768,128]{1,0:T(8,128)(2,1)S(1)} %get-tuple-element.39.rest_2_), channel_id=1, source_target_pairs={{0,3},{1,2},{2,1},{3,0},{4,7},{5,6},{6,5},{7,4},{8,11},{9,10},{10,... | collective-permute-start | bytes 589832 | tf_op jit(solution)/shard_map/ppermute | solution.py:474
  19.6 0.0 collective-permute-done.4.rest_3_.l2_ref
  19.6 0.0 collective-permute-done.5.rest_4_.l3_ref
  19.6 0.0 collective-permute-done.3.got_ref
  19.6 0.1 add_step.3
  19.7 2.4 %collective-permute-start.6 = (bf16[4,128,128]{2,1,0:T(8,128)(2,1)S(1)}, bf16[4,128,128]{2,1,0:T(8,128)(2,1)S(1)}, u32[]{:S(2)}, u32[]{:S(2)}) collective-permute-start(bf16[4,128,128]{2,1,0:T(8,128)(2,1)S(1)} %get-tuple-element.40.rest_0_), channel_id=1, source_target_pairs={{0,16},{4,20},{8,24},{12,28},{16,0},{20,4},{24,8},{28,12},{1,17},{... | collective-permute-start | bytes 393224 | tf_op jit(solution)/shard_map/ppermute | solution.py:474
  22.1 2.5 %attention_rows.3 = (f32[256,384]{1,0:T(8,128)S(1)}, f32[256,384]{1,0:T(8,128)S(1)}) custom-call(s32[1]{0:T(128)} %bitcast.head_ref.ids_ref.quarter_ref, bf16[4096,512]{1,0:T(8,128)(2,1)} %q_ref.13, bf16[4096,512]{1,0:T(8,128)(2,1)} %k_ref.15, bf16[4096,512]{1,0:T(8,128)(2,1)} %v_ref.15, bf16[8,4,128,128]{3,2,1,0:T(8,128)(2,1)S(1)} %get-tuple-element.32.within_ref, ...), custom_call_target="tpu_custom_call" | custom-call | flops 1024 | bytes 1024 | tf_op jit(solution)/shard_map/attention_rows/pallas_call | solution.py:159
  24.5 3.8 %collective-permute-done.8.refs_8_.l3_ref.q3_ref = bf16[768,128]{1,0:T(8,128)(2,1)S(1)} collective-permute-done((bf16[768,128]{1,0:T(8,128)(2,1)S(1)}, bf16[768,128]{1,0:T(8,128)(2,1)S(1)}, u32[]{:S(2)}, u32[]{:S(2)}) %collective-permute-start.8) | collective-permute-done | bytes 196640 | tf_op jit(solution)/shard_map/ppermute | solution.py:474
  28.4 0.1 collective-permute-done.6.refs_6_
  28.5 1.3 %late_rows.1 = (bf16[304,384]{1,0:T(8,128)(2,1)S(1)}, bf16[304,384]{1,0:T(8,128)(2,1)S(1)}, f32[4,128,128]{2,1,0:T(8,128)S(1)}) custom-call(s32[1]{0:T(128)} %bitcast.head_ref.ids_ref.quarter_ref, bf16[4096,512]{1,0:T(8,128)(2,1)} %q_ref.13, f32[256,384]{1,0:T(8,128)S(1)} %get-tuple-element.41.refs_1_, bf16[4096,512]{1,0:T(8,128)(2,1)} %q_ref.13, ...), custom_call_target="tpu_custom_call" | custom-call | flops 1024 | bytes 1024 | tf_op jit(solution)/shard_map/late_rows/pallas_call | solution.py:294
  29.9 1.3 %collective-permute-start.10 = (bf16[304,384]{1,0:T(8,128)(2,1)S(1)}, bf16[304,384]{1,0:T(8,128)(2,1)S(1)}, u32[]{:S(2)}, u32[]{:S(2)}) collective-permute-start(bf16[304,384]{1,0:T(8,128)(2,1)S(1)} %get-tuple-element.45.rest_1_), channel_id=1, source_target_pairs={{0,2},{1,3},{2,0},{3,1},{4,6},{5,7},{6,4},{7,5},{8,10},{9,11},{10,... | collective-permute-start | bytes 700424 | tf_op jit(solution)/shard_map/ppermute | solution.py:474
  31.1 1.3 %collective-permute-start.11 = (bf16[304,384]{1,0:T(8,128)(2,1)S(1)}, bf16[304,384]{1,0:T(8,128)(2,1)S(1)}, u32[]{:S(2)}, u32[]{:S(2)}) collective-permute-start(bf16[304,384]{1,0:T(8,128)(2,1)S(1)} %get-tuple-element.46.rest_2_), channel_id=1, source_target_pairs={{0,3},{1,2},{2,1},{3,0},{4,7},{5,6},{6,5},{7,4},{8,11},{9,10},{10,... | collective-permute-start | bytes 700424 | tf_op jit(solution)/shard_map/ppermute | solution.py:474
  32.4 4.5 %attention_rows.4 = (bf16[512,384]{1,0:T(8,128)(2,1)}, bf16[512,384]{1,0:T(8,128)(2,1)}) custom-call(s32[1]{0:T(128)} %bitcast.head_ref.ids_ref.quarter_ref, bf16[4096,512]{1,0:T(8,128)(2,1)} %q_ref.13, bf16[4096,512]{1,0:T(8,128)(2,1)} %k_ref.15, bf16[4096,512]{1,0:T(8,128)(2,1)} %v_ref.15, bf16[8,4,128,128]{3,2,1,0:T(8,128)(2,1)S(1)} %get-tuple-element.32.within_ref, ...), custom_call_target="tpu_custom_call" | custom-call | flops 1024 | bytes 1024 | tf_op jit(solution)/shard_map/attention_rows/pallas_call | solution.py:159
  36.9 1.2 %collective-permute-start.16 = (bf16[512,384]{1,0:T(8,128)(2,1)}, bf16[512,384]{1,0:T(8,128)(2,1)}, u32[]{:S(2)}, u32[]{:S(2)}) collective-permute-start(bf16[512,384]{1,0:T(8,128)(2,1)} %get-tuple-element.47.rest_1_), channel_id=1, source_target_pairs={{0,2},{1,3},{2,0},{3,1},{4,6},{5,7},{6,4},{7,5},{8,10},{9,11},{10,... | collective-permute-start | bytes 1179656 | tf_op jit(solution)/shard_map/ppermute | solution.py:474
  38.1 5.2 %attention_quarter.2.rest_1_ = bf16[1024,512]{1,0:T(8,128)(2,1)} custom-call(s32[1]{0:T(128)} %bitcast.head_ref.ids_ref.quarter_ref, bf16[4096,512]{1,0:T(8,128)(2,1)} %q_ref.13, bf16[4096,512]{1,0:T(8,128)(2,1)} %k_ref.15, bf16[4096,512]{1,0:T(8,128)(2,1)} %v_ref.15, bf16[8,4,128,128]{3,2,1,0:T(8,128)(2,1)S(1)} %get-tuple-element.32.within_ref, ...), custom_call_target="tpu_custom_call" | custom-call | flops 1024 | bytes 1024 | tf_op jit(solution)/shard_map/attention_quarter/pallas_call | solution.py:192
  43.3 0.3 collective-permute-start.17
  43.6 4.4 %attention_quarter.3.own_ref.rest_1_ = bf16[1024,512]{1,0:T(8,128)(2,1)S(1)} custom-call(s32[1]{0:T(128)} %bitcast.head_ref.ids_ref.quarter_ref, bf16[4096,512]{1,0:T(8,128)(2,1)} %q_ref.13, bf16[4096,512]{1,0:T(8,128)(2,1)} %k_ref.15, bf16[4096,512]{1,0:T(8,128)(2,1)} %v_ref.15, bf16[8,4,128,128]{3,2,1,0:T(8,128)(2,1)S(1)} %get-tuple-element.32.within_ref, ...), custom_call_target="tpu_custom_call" | custom-call | flops 1024 | bytes 1024 | tf_op jit(solution)/shard_map/attention_quarter/pallas_call | solution.py:192
  48.0 0.4 collective-permute-start.9
  48.5 3.3 %attention_rows.5 = (bf16[128,384]{1,0:T(8,128)(2,1)S(1)}, bf16[128,384]{1,0:T(8,128)(2,1)S(1)}, bf16[128,384]{1,0:T(8,128)(2,1)S(1)}, bf16[128,384]{1,0:T(8,128)(2,1)S(1)}) custom-call(s32[1]{0:T(128)} %bitcast.head_ref.ids_ref.quarter_ref, bf16[4096,512]{1,0:T(8,128)(2,1)} %q_ref.13, bf16[4096,512]{1,0:T(8,128)(2,1)} %k_ref.15, bf16[4096,512]{1,0:T(8,128)(2,1)} %v_ref.15, ...), custom_call_target="tpu_custom_call" | custom-call | flops 999999995904 | bytes 1024 | tf_op jit(solution)/shard_map/attention_rows/pallas_call | solution.py:159
  51.8 0.0 copy-start.4
  51.8 1.3 %collective-permute-start.12 = (bf16[128,384]{1,0:T(8,128)(2,1)S(1)}, bf16[128,384]{1,0:T(8,128)(2,1)S(1)}, u32[]{:S(2)}, u32[]{:S(2)}) collective-permute-start(bf16[128,384]{1,0:T(8,128)(2,1)S(1)} %get-tuple-element.51), channel_id=1, source_target_pairs={{0,2},{1,3},{2,0},{3,1},{4,6},{5,7},{6,4},{7,5},{8,10},{9,11},{10,... | collective-permute-start | bytes 294920 | tf_op jit(solution)/shard_map/ppermute | solution.py:474
  53.0 0.3 collective-permute-start.14
  53.3 1.7 %collective-permute-start.15 = (bf16[128,384]{1,0:T(8,128)(2,1)S(1)}, bf16[128,384]{1,0:T(8,128)(2,1)S(1)}, u32[]{:S(2)}, u32[]{:S(2)}) collective-permute-start(bf16[128,384]{1,0:T(8,128)(2,1)S(1)} %get-tuple-element.54), channel_id=1, source_target_pairs={{0,3},{1,2},{2,1},{3,0},{4,7},{5,6},{6,5},{7,4},{8,11},{9,10},{10,... | collective-permute-start | bytes 294920 | tf_op jit(solution)/shard_map/ppermute | solution.py:474
  55.0 0.1 collective-permute-start.13
  55.1 0.2 early_out.4
  55.3 0.2 early_out.5
  55.5 0.2 early_out.3
  55.7 0.9 %gather_rows.1.near_ref = bf16[128,1280]{1,0:T(8,128)(2,1)S(1)} custom-call(bf16[1024,512]{1,0:T(8,128)(2,1)S(1)} %attention_quarter.3.own_ref.rest_1_, bf16[1024,512]{1,0:T(8,128)(2,1)} %collective-permute-done.9.mate_ref, bf16[256,128]{1,0:T(8,128)(2,1)S(1)} %get-tuple-element.49.o2_ref, bf16[256,128]{1,0:T(8,128)(2,1)S(1)} %get-tuple-element.50.o3_ref), custom_call_target="tpu_custom_call" | custom-call | flops 1024 | bytes 1024 | tf_op jit(solution)/shard_map/gather_rows/pallas_call | solution.py:354
  56.6 2.3 %norm_rows.3.rest_0_ = bf16[1024,2048]{1,0:T(8,128)(2,1)} custom-call(s32[1]{0:T(128)} %bitcast.head_ref.ids_ref.quarter_ref, f32[1,2048]{1,0:T(1,128)S(1)} %bitcast.3, bf16[1024,512]{1,0:T(8,128)(2,1)S(1)} %attention_quarter.3.own_ref.rest_1_, bf16[1024,512]{1,0:T(8,128)(2,1)} %collective-permute-done.9.mate_ref, ...), custom_call_target="tpu_custom_call" | custom-call | flops 1024 | bytes 1024 | tf_op jit(solution)/shard_map/norm_rows/pallas_call | solution.py:429
  58.9 1.7 %collective-permute-done.17.x3_ref = bf16[512,384]{1,0:T(8,128)(2,1)} collective-permute-done((bf16[512,384]{1,0:T(8,128)(2,1)}, bf16[512,384]{1,0:T(8,128)(2,1)}, u32[]{:S(2)}, u32[]{:S(2)}) %collective-permute-start.17) | collective-permute-done | bytes 393248 | tf_op jit(solution)/shard_map/ppermute | solution.py:474
  60.6 4.2 %norm_rows.4.rest_0_ = bf16[1024,2048]{1,0:T(8,128)(2,1)} custom-call(s32[1]{0:T(128)} %bitcast.head_ref.ids_ref.quarter_ref, f32[1,2048]{1,0:T(1,128)S(1)} %bitcast.4, bf16[1024,512]{1,0:T(8,128)(2,1)S(1)} %attention_quarter.3.own_ref.rest_1_, bf16[1024,512]{1,0:T(8,128)(2,1)} %collective-permute-done.9.mate_ref, ...), custom_call_target="tpu_custom_call", output_to_operand_aliasing={{}: (8, {})} | custom-call | flops 1024 | bytes 1024 | tf_op jit(solution)/shard_map/norm_rows/pallas_call | solution.py:429
  64.8 1.8 %collective-permute-done.15.x3_ref = bf16[128,384]{1,0:T(8,128)(2,1)S(1)} collective-permute-done((bf16[128,384]{1,0:T(8,128)(2,1)S(1)}, bf16[128,384]{1,0:T(8,128)(2,1)S(1)}, u32[]{:S(2)}, u32[]{:S(2)}) %collective-permute-start.15) | collective-permute-done | bytes 98336 | tf_op jit(solution)/shard_map/ppermute | solution.py:474
  66.6 2.0 %norm_rows.5.old_ref = bf16[1024,2048]{1,0:T(8,128)(2,1)} custom-call(s32[1]{0:T(128)} %bitcast.head_ref.ids_ref.quarter_ref, f32[1,2048]{1,0:T(1,128)S(1)} %bitcast.5, bf16[1024,512]{1,0:T(8,128)(2,1)S(1)} %attention_quarter.3.own_ref.rest_1_, bf16[1024,512]{1,0:T(8,128)(2,1)} %collective-permute-done.9.mate_ref, ...), custom_call_target="tpu_custom_call", output_to_operand_aliasing={{}: (8, {})} | custom-call | flops 1024 | bytes 1024 | tf_op jit(solution)/shard_map/norm_rows/pallas_call | solution.py:429
  68.6 1.1 %norm_last.1 = bf16[1024,2048]{1,0:T(8,128)(2,1)} custom-call(s32[1]{0:T(128)} %bitcast.head_ref.ids_ref.quarter_ref, f32[1,2048]{1,0:T(1,128)S(1)} %bitcast.6, bf16[128,1280]{1,0:T(8,128)(2,1)S(1)} %gather_rows.1.near_ref, bf16[128,384]{1,0:T(8,128)(2,1)S(1)} %collective-permute-done.12.x2_ref, ...), custom_call_target="tpu_custom_call", output_to_operand_aliasing={{}: (5, {})} | custom-call | flops 1024 | bytes 1024 | tf_op jit(solution)/shard_map/norm_last/pallas_call | solution.py:377
  (18 shorter events, 0.0 us)
Async XLA Ops:
  1.1 12.5 %collective-permute-start.2 = (bf16[768,128]{1,0:T(8,128)(2,1)S(1)}, bf16[768,128]{1,0:T(8,128)(2,1)S(1)}, u32[]{:S(2)}, u32[]{:S(2)}) collective-permute-start(bf16[768,128]{1,0:T(8,128)(2,1)S(1)} %get-tuple-element.59.rest_1_), channel_id=1, source_target_pairs={{0,3},{1,2},{2,1},{3,0},{4,7},{5,6},{6,5},{7,4},{8,11},{9,10},{10,... | collective-permute-start | bytes 589832 | tf_op jit(solution)/shard_map/ppermute | solution.py:474
  3.7 9.9 %collective-permute-start.1 = (bf16[768,128]{1,0:T(8,128)(2,1)S(1)}, bf16[768,128]{1,0:T(8,128)(2,1)S(1)}, u32[]{:S(2)}, u32[]{:S(2)}) collective-permute-start(bf16[768,128]{1,0:T(8,128)(2,1)S(1)} %get-tuple-element.60.rest_0_), channel_id=1, source_target_pairs={{0,2},{1,3},{2,0},{3,1},{4,6},{5,7},{6,4},{7,5},{8,10},{9,11},{10,... | collective-permute-start | bytes 589832 | tf_op jit(solution)/shard_map/ppermute | solution.py:474
  7.7 5.9 %collective-permute-start = (bf16[4,128,128]{2,1,0:T(8,128)(2,1)S(1)}, bf16[4,128,128]{2,1,0:T(8,128)(2,1)S(1)}, u32[]{:S(2)}, u32[]{:S(2)}) collective-permute-start(bf16[4,128,128]{2,1,0:T(8,128)(2,1)S(1)} %get-tuple-element.33.rest_0_.total_ref), channel_id=1, source_target_pairs={{0,4},{4,0},{8,12},{12,8},{16,20},{20,16},{24,28},{28,24},{1,5},{5... | collective-permute-start | bytes 393224 | tf_op jit(solution)/shard_map/ppermute | solution.py:474
  11.4 8.2 %collective-permute-start.4 = (bf16[512,128]{1,0:T(8,128)(2,1)S(1)}, bf16[512,128]{1,0:T(8,128)(2,1)S(1)}, u32[]{:S(2)}, u32[]{:S(2)}) collective-permute-start(bf16[512,128]{1,0:T(8,128)(2,1)S(1)} %get-tuple-element.34.rest_0_), channel_id=1, source_target_pairs={{0,2},{1,3},{2,0},{3,1},{4,6},{5,7},{6,4},{7,5},{8,10},{9,11},{10,... | collective-permute-start | bytes 393224 | tf_op jit(solution)/shard_map/ppermute | solution.py:474
  12.7 6.9 %collective-permute-start.5 = (bf16[512,128]{1,0:T(8,128)(2,1)S(1)}, bf16[512,128]{1,0:T(8,128)(2,1)S(1)}, u32[]{:S(2)}, u32[]{:S(2)}) collective-permute-start(bf16[512,128]{1,0:T(8,128)(2,1)S(1)} %get-tuple-element.35.rest_1_), channel_id=1, source_target_pairs={{0,3},{1,2},{2,1},{3,0},{4,7},{5,6},{6,5},{7,4},{8,11},{9,10},{10,... | collective-permute-start | bytes 393224 | tf_op jit(solution)/shard_map/ppermute | solution.py:474
  13.7 5.9 %collective-permute-start.3 = (bf16[4,128,128]{2,1,0:T(8,128)(2,1)S(1)}, bf16[4,128,128]{2,1,0:T(8,128)(2,1)S(1)}, u32[]{:S(2)}, u32[]{:S(2)}) collective-permute-start(bf16[4,128,128]{2,1,0:T(8,128)(2,1)S(1)} %get-tuple-element.36.rest_1_.total_ref), channel_id=1, source_target_pairs={{0,8},{4,12},{8,0},{12,4},{16,24},{20,28},{24,16},{28,20},{1,9},{5... | collective-permute-start | bytes 393224 | tf_op jit(solution)/shard_map/ppermute | solution.py:474
  17.2 7.3 %collective-permute-start.7 = (bf16[768,128]{1,0:T(8,128)(2,1)S(1)}, bf16[768,128]{1,0:T(8,128)(2,1)S(1)}, u32[]{:S(2)}, u32[]{:S(2)}) collective-permute-start(bf16[768,128]{1,0:T(8,128)(2,1)S(1)} %get-tuple-element.38.rest_1_), channel_id=1, source_target_pairs={{0,2},{1,3},{2,0},{3,1},{4,6},{5,7},{6,4},{7,5},{8,10},{9,11},{10,... | collective-permute-start | bytes 589832 | tf_op jit(solution)/shard_map/ppermute | solution.py:474
  18.5 9.9 %collective-permute-start.8 = (bf16[768,128]{1,0:T(8,128)(2,1)S(1)}, bf16[768,128]{1,0:T(8,128)(2,1)S(1)}, u32[]{:S(2)}, u32[]{:S(2)}) collective-permute-start(bf16[768,128]{1,0:T(8,128)(2,1)S(1)} %get-tuple-element.39.rest_2_), channel_id=1, source_target_pairs={{0,3},{1,2},{2,1},{3,0},{4,7},{5,6},{6,5},{7,4},{8,11},{9,10},{10,... | collective-permute-start | bytes 589832 | tf_op jit(solution)/shard_map/ppermute | solution.py:474
  19.7 8.9 %collective-permute-start.6 = (bf16[4,128,128]{2,1,0:T(8,128)(2,1)S(1)}, bf16[4,128,128]{2,1,0:T(8,128)(2,1)S(1)}, u32[]{:S(2)}, u32[]{:S(2)}) collective-permute-start(bf16[4,128,128]{2,1,0:T(8,128)(2,1)S(1)} %get-tuple-element.40.rest_0_), channel_id=1, source_target_pairs={{0,16},{4,20},{8,24},{12,28},{16,0},{20,4},{24,8},{28,12},{1,17},{... | collective-permute-start | bytes 393224 | tf_op jit(solution)/shard_map/ppermute | solution.py:474
  24.5 5.3 %copy-start = (bf16[768,128]{1,0:T(8,128)(2,1)}, bf16[768,128]{1,0:T(8,128)(2,1)S(1)}, u32[]{:S(2)}) copy-start(bf16[768,128]{1,0:T(8,128)(2,1)S(1)} %collective-permute-done.7.refs_7_.l2_ref.q2_ref) | copy-start | bytes 589828
  28.4 1.5 %copy-start.2 = (bf16[768,128]{1,0:T(8,128)(2,1)}, bf16[768,128]{1,0:T(8,128)(2,1)S(1)}, u32[]{:S(2)}) copy-start(bf16[768,128]{1,0:T(8,128)(2,1)S(1)} %collective-permute-done.8.refs_8_.l3_ref.q3_ref) | copy-start | bytes 589828
  29.9 18.6 %collective-permute-start.10 = (bf16[304,384]{1,0:T(8,128)(2,1)S(1)}, bf16[304,384]{1,0:T(8,128)(2,1)S(1)}, u32[]{:S(2)}, u32[]{:S(2)}) collective-permute-start(bf16[304,384]{1,0:T(8,128)(2,1)S(1)} %get-tuple-element.45.rest_1_), channel_id=1, source_target_pairs={{0,2},{1,3},{2,0},{3,1},{4,6},{5,7},{6,4},{7,5},{8,10},{9,11},{10,... | collective-permute-start | bytes 700424 | tf_op jit(solution)/shard_map/ppermute | solution.py:474
  31.1 17.3 %collective-permute-start.11 = (bf16[304,384]{1,0:T(8,128)(2,1)S(1)}, bf16[304,384]{1,0:T(8,128)(2,1)S(1)}, u32[]{:S(2)}, u32[]{:S(2)}) collective-permute-start(bf16[304,384]{1,0:T(8,128)(2,1)S(1)} %get-tuple-element.46.rest_2_), channel_id=1, source_target_pairs={{0,3},{1,2},{2,1},{3,0},{4,7},{5,6},{6,5},{7,4},{8,11},{9,10},{10,... | collective-permute-start | bytes 700424 | tf_op jit(solution)/shard_map/ppermute | solution.py:474
  36.9 16.4 %collective-permute-start.16 = (bf16[512,384]{1,0:T(8,128)(2,1)}, bf16[512,384]{1,0:T(8,128)(2,1)}, u32[]{:S(2)}, u32[]{:S(2)}) collective-permute-start(bf16[512,384]{1,0:T(8,128)(2,1)} %get-tuple-element.47.rest_1_), channel_id=1, source_target_pairs={{0,2},{1,3},{2,0},{3,1},{4,6},{5,7},{6,4},{7,5},{8,10},{9,11},{10,... | collective-permute-start | bytes 1179656 | tf_op jit(solution)/shard_map/ppermute | solution.py:474
  43.3 17.3 %collective-permute-start.17 = (bf16[512,384]{1,0:T(8,128)(2,1)}, bf16[512,384]{1,0:T(8,128)(2,1)}, u32[]{:S(2)}, u32[]{:S(2)}) collective-permute-start(bf16[512,384]{1,0:T(8,128)(2,1)} %get-tuple-element.48.rest_2_), channel_id=1, source_target_pairs={{0,3},{1,2},{2,1},{3,0},{4,7},{5,6},{6,5},{7,4},{8,11},{9,10},{10,... | collective-permute-start | bytes 1179656 | tf_op jit(solution)/shard_map/ppermute | solution.py:474
  48.0 7.0 %collective-permute-start.9 = (bf16[1024,512]{1,0:T(8,128)(2,1)}, bf16[1024,512]{1,0:T(8,128)(2,1)}, u32[]{:S(2)}, u32[]{:S(2)}) collective-permute-start(bf16[1024,512]{1,0:T(8,128)(2,1)} %attention_quarter.2.rest_1_), channel_id=1, source_target_pairs={{0,1},{1,0},{2,3},{3,2},{4,5},{5,4},{6,7},{7,6},{8,9},{9,8},{10,11... | collective-permute-start | bytes 3145736 | tf_op jit(solution)/shard_map/ppermute | solution.py:474
  48.5 6.8 %copy-start.1 = (bf16[768,128]{1,0:T(8,128)(2,1)S(1)}, bf16[768,128]{1,0:T(8,128)(2,1)}, u32[]{:S(2)}) copy-start(bf16[768,128]{1,0:T(8,128)(2,1)} %copy-done) | copy-start | bytes 589828
  48.5 6.8 %copy-start.3 = (bf16[768,128]{1,0:T(8,128)(2,1)S(1)}, bf16[768,128]{1,0:T(8,128)(2,1)}, u32[]{:S(2)}) copy-start(bf16[768,128]{1,0:T(8,128)(2,1)} %copy-done.2) | copy-start | bytes 589828
  51.8 4.8 %copy-start.4 = (f32[2048]{0:T(1024)S(1)}, f32[2048]{0:T(1024)}, u32[]{:S(2)}) copy-start(f32[2048]{0:T(1024)} %param.7) | copy-start | bytes 24580
  51.8 16.8 %collective-permute-start.12 = (bf16[128,384]{1,0:T(8,128)(2,1)S(1)}, bf16[128,384]{1,0:T(8,128)(2,1)S(1)}, u32[]{:S(2)}, u32[]{:S(2)}) collective-permute-start(bf16[128,384]{1,0:T(8,128)(2,1)S(1)} %get-tuple-element.51), channel_id=1, source_target_pairs={{0,2},{1,3},{2,0},{3,1},{4,6},{5,7},{6,4},{7,5},{8,10},{9,11},{10,... | collective-permute-start | bytes 294920 | tf_op jit(solution)/shard_map/ppermute | solution.py:474
  53.0 11.8 %collective-permute-start.14 = (bf16[128,384]{1,0:T(8,128)(2,1)S(1)}, bf16[128,384]{1,0:T(8,128)(2,1)S(1)}, u32[]{:S(2)}, u32[]{:S(2)}) collective-permute-start(bf16[128,384]{1,0:T(8,128)(2,1)S(1)} %get-tuple-element.53), channel_id=1, source_target_pairs={{0,2},{1,3},{2,0},{3,1},{4,6},{5,7},{6,4},{7,5},{8,10},{9,11},{10,... | collective-permute-start | bytes 294920 | tf_op jit(solution)/shard_map/ppermute | solution.py:474
  53.3 13.3 %collective-permute-start.15 = (bf16[128,384]{1,0:T(8,128)(2,1)S(1)}, bf16[128,384]{1,0:T(8,128)(2,1)S(1)}, u32[]{:S(2)}, u32[]{:S(2)}) collective-permute-start(bf16[128,384]{1,0:T(8,128)(2,1)S(1)} %get-tuple-element.54), channel_id=1, source_target_pairs={{0,3},{1,2},{2,1},{3,0},{4,7},{5,6},{6,5},{7,4},{8,11},{9,10},{10,... | collective-permute-start | bytes 294920 | tf_op jit(solution)/shard_map/ppermute | solution.py:474
  55.0 13.6 %collective-permute-start.13 = (bf16[128,384]{1,0:T(8,128)(2,1)S(1)}, bf16[128,384]{1,0:T(8,128)(2,1)S(1)}, u32[]{:S(2)}, u32[]{:S(2)}) collective-permute-start(bf16[128,384]{1,0:T(8,128)(2,1)S(1)} %get-tuple-element.52), channel_id=1, source_target_pairs={{0,3},{1,2},{2,1},{3,0},{4,7},{5,6},{6,5},{7,4},{8,11},{9,10},{10,... | collective-permute-start | bytes 294920 | tf_op jit(solution)/shard_map/ppermute | solution.py:474

commit v5 on v4

--- a/solution.py
+++ b/solution.py
@@ -114,7 +114,7 @@
                 out_ref[pl.ds(low_row, part), cols] = outs[i][r:r + part].astype(out_ref.dtype)
 
 
-def attention_rows(arrays, before, at, sides, start, size, head, heads, kind, tokens, cost=None, cut=1):
+def attention_rows(arrays, before, at, sides, start, size, head, heads, kind, tokens, cost=None, cut=1, keep=False):
     queries, keys, values, within = arrays
     rows, width = queries.shape
     share = rows // 4
@@ -149,12 +149,14 @@
 
     def kernel(ids_ref, q_ref, k_ref, v_ref, within_ref, *rest):
         before_ref = None if before is None else rest[0]
-        outs = rest[len(rest) - count * cut:]
+        outs = rest[len(rest) - count * (cut + keep):]
         for n in range(count):
             @pl.when(pl.program_id(0) == n)
             def _(n=n):
                 mine = outs[n * cut:(n + 1) * cut]
                 attend(first, halves, heads, q_ref, k_ref, v_ref, within_ref, before_ref, *mine)
+                if keep:
+                    outs[count * cut + n][...] = q_ref[...]
 
     return pl.pallas_call(
         kernel,
@@ -162,9 +164,10 @@
             num_scalar_prefetch=1,
             grid=(count,),
             in_specs=in_specs,
-            out_specs=[pl.BlockSpec((size // cut, span), lambda n, s: (0, 0))] * (count * cut),
+            out_specs=[pl.BlockSpec((size // cut, span), lambda n, s: (0, 0))] * (count * (cut + keep)),
         ),
-        out_shape=[jax.ShapeDtypeStruct((size // cut, span), kind)] * (count * cut),
+        out_shape=[jax.ShapeDtypeStruct((size // cut, span), kind)] * (count * cut)
+        + [jax.ShapeDtypeStruct((size, span), jnp.bfloat16)] * (count * keep),
         compiler_params=params(),
         cost_estimate=COST if cost is None else cost,
         name="attention_rows",
@@ -258,28 +261,32 @@
         size = q_ref.shape[0]
         for h in range(heads):
             cols = pl.ds(h * DH, DH)
-            out = local_ref[:, cols] + jnp.dot(
+            out = local_ref[:, cols].astype(jnp.float32) + jnp.dot(
                 q_ref[:, cols], before_ref[h].astype(jnp.bfloat16), preferred_element_type=jnp.float32
             )
             out_ref[pl.ds(0, size), cols] = out.astype(jnp.bfloat16)
-        if embed:
+        if embed and n == 0:
             low = before_ref[heads].astype(jnp.bfloat16)
             for c in range(heads):
                 high = min((c + 1) * EXTRA, DH)
                 out_ref[pl.ds(size, high - c * EXTRA), pl.ds(c * DH, DH)] = low[c * EXTRA:high]
 
 
-def late_rows(queries, before, at, sides, start, locals_, heads, embed, tokens, last=None):
-    count = len(sides)
+def late_rows(at, queries, locals_, before, heads, embed, tokens, last):
+    count = len(queries)
     size, span = locals_[0].shape
-    steps = 1 if embed else size // BLK
-    rows = size // steps
-    share = queries.shape[0] // 4
+    rows, steps = size, 1
     in_specs, operands = [], []
     for n in range(count):
-        in_specs.append(pl.BlockSpec((rows, span), lambda i, s, side=sides[n]: ((s[0] ^ side) * (share // rows) + start // rows + i, 0)))
-        in_specs.append(pl.BlockSpec((rows, span), lambda i, s: (i, 0)))
-        operands += [queries, locals_[n]]
+        whole = pl.BlockSpec((rows, span), lambda i, s: (i, 0))
+        if isinstance(queries[n], tuple):
+            array, side = queries[n]
+            per = array.shape[0] // 4 // rows
+            in_specs += [pl.BlockSpec((rows, span), lambda i, s, side=side: ((s[0] ^ side) * per, 0)), whole]
+            operands += [array, locals_[n]]
+        else:
+            in_specs += [whole, whole]
+            operands += [queries[n], locals_[n]]
     state = pl.BlockSpec(before.shape, lambda i, s: (0, 0, 0))
     in_specs.append(state)
     operands.append(before)
@@ -297,45 +304,54 @@
             num_scalar_prefetch=1,
             grid=(steps,),
             in_specs=in_specs,
-            out_specs=[pl.BlockSpec((rows + more, span), lambda i, s: (i, 0))] * count + out_specs,
+            out_specs=[
+                pl.BlockSpec((rows + (more if n == 0 else 0), span), lambda i, s: (i, 0)) for n in range(count)
+            ] + out_specs,
         ),
-        out_shape=[jax.ShapeDtypeStruct((size + more, span), jnp.bfloat16)] * count + out_shape,
+        out_shape=[
+            jax.ShapeDtypeStruct((size + (more if n == 0 else 0), span), jnp.bfloat16) for n in range(count)
+        ] + out_shape,
         compiler_params=params(),
         cost_estimate=COST,
         name="late_rows",
     )(at, *operands, *tokens)
 
 
-def early_out_kernel(l2_ref, l3_ref, q2_ref, q3_ref, b2_ref, b3_ref, o2_ref, o3_ref):
-    for l_ref, q_ref, b_ref, o_ref in ((l2_ref, q2_ref, b2_ref, o2_ref), (l3_ref, q3_ref, b3_ref, o3_ref)):
+def early_out_kernel(*refs):
+    ins, outs = refs[:-2], refs[-2:]
+    for side in range(2):
+        low_ref, high_ref, q_ref, b_ref = ins[side::2]
+        out_ref = outs[side]
         parts = []
         for c in range(b_ref.shape[1] // DH):
             high = min((c + 1) * EXTRA, DH)
             parts.append(b_ref[pl.ds(b_ref.shape[0] - EXTRA, high - c * EXTRA), pl.ds(c * DH, DH)])
         state = jnp.concatenate(parts, axis=0)
-        out = l_ref[...].astype(jnp.float32) + jnp.dot(q_ref[...], state, preferred_element_type=jnp.float32)
-        o_ref[...] = out.astype(jnp.bfloat16)
-
-
-def early_out(size, l2, l3, q2, q3, b2, b3):
-    def at(pair):
-        index = pair[1] // size
-        return pl.BlockSpec((size, DH), lambda n: (index, 0))
-
+        size, held, first = out_ref.shape[0], q_ref.shape[0], low_ref.shape[0]
+        query = jnp.concatenate([q_ref[...], high_ref[pl.ds(size - first, size - held), :]], axis=0)
+        late = jnp.dot(query, state, preferred_element_type=jnp.float32)
+        low = low_ref[...].astype(jnp.float32) + late[:first]
+        out_ref[pl.ds(0, first), :] = low.astype(jnp.bfloat16)
+        high = high_ref[pl.ds(0, size - first), :].astype(jnp.float32) + late[first:]
+        out_ref[pl.ds(first, size - first), :] = high.astype(jnp.bfloat16)
+
+
+def early_out(size, low, high, query, states):
     def full(array):
         return pl.BlockSpec(array.shape, lambda n: (0, 0))
 
     out = jax.ShapeDtypeStruct((size, DH), jnp.bfloat16)
+    operands = [*low, *high, *query, *states]
     return pl.pallas_call(
         early_out_kernel,
         grid=(1,),
-        in_specs=[at(l2), at(l3), at(q2), at(q3), full(b2), full(b3)],
+        in_specs=[full(y) for y in operands],
         out_specs=[pl.BlockSpec((size, DH), lambda n: (0, 0))] * 2,
         out_shape=[out, out],
         compiler_params=params(),
         cost_estimate=COST,
         name="early_out",
-    )(l2[0], l3[0], q2[0], q3[0], b2, b3)
+    )(*operands)
 
 
 def gather_kernel(own_ref, mate_ref, o2_ref, o3_ref, out_ref):
@@ -503,8 +519,11 @@
             early_l.append(across(early))
             tokens = [*early, *(early_q if step == 0 else early_l[0])]
         elif step == 2:
-            first = attention_rows(arrays, None, at, far, BLK, HALF, 0, heads - 1, jnp.float32, [group])
-            tokens = [*first]
+            first = attention_rows(
+                arrays, None, at, far, BLK, HALF, 0, heads - 1, jnp.float32, [group], keep=True
+            )
+            second = attention_rows(arrays, None, at, far, 0, BLK, 0, heads - 1, jnp.bfloat16, first)
+            tokens = [*first, *second]
         if bit * 2 < seq_size:
             group, before = add_step(mine, bit, group, got, before, tokens)
         bit, step = bit * 2, step + 1
@@ -512,27 +531,27 @@
     def far_rows(start, size, tokens, cost=None, cut=1):
         return attention_rows(arrays, before, at, far, start, size, 0, heads - 1, jnp.bfloat16, tokens, cost, cut)
 
-    *one, before = late_rows(queries, before, at, far, BLK, first, heads - 1, True, early_l[1], (mine, bit // 2, got))
+    *one, before = late_rows(
+        at, first[2:], first[:2], before, heads - 1, True, [*early_l[1], *second], (mine, bit // 2, got)
+    )
     x1 = across(one)
-    two = far_rows(0, BLK, one)
+    two = late_rows(at, [(queries, k) for k in far], second, before, heads - 1, False, one, None)
     x2 = across(two)
     mate = attention_quarter(arrays, before, at, 1, jnp.bfloat16, two)
     mated = swap(mate, "head", 4, 1)
     own = attention_quarter(arrays, before, at, 0, jnp.bfloat16, [mate])
     three = far_rows(BLK + HALF, HALF, [own, *x1], LONG, 2)
     x3, x4 = across(three[0::2]), across(three[1::2])
+    state = lax.slice(x1[0], (HALF, 0), (HALF + EXTRA, x1[0].shape[1]))
+    other = swap(state, "head", 4, 1)
+    o2, o3 = early_out(share, *early_l, early_q, [state, other])
     out = None
-    low, high = early_l
     end = share - HALF // 2
-    for row, size, (y2, y3) in ((BLK, HALF, x1), (0, BLK, x2), (BLK + HALF, HALF, x3)):
-        l2, l3 = [(y, row) for y in low] if row < BLK else [(y, row - BLK) for y in high]
-        q2, q3 = [(y, row) for y in early_q] if row < share - tail else [(y, BLK) for y in high]
-        o2, o3 = early_out(size, l2, l3, q2, q3, x1[0], x1[1])
-        size = min(size, end - row)
+    for row, size, (y2, y3) in ((BLK, HALF, x1), (0, BLK, x2), (BLK + HALF, HALF // 2, x3)):
         out = norm_rows(
-            at, gain, share, row, size, (own, row), (mated, row), (y2, 0), (y3, 0), (o2, 0), (o3, 0), out
+            at, gain, share, row, size, (own, row), (mated, row), (y2, 0), (y3, 0), (o2, row), (o3, row), out
         )
-    near = gather_rows(share - end, (own, end), (mated, end), (o2, HALF // 2), (o3, HALF // 2))
+    near = gather_rows(share - end, (own, end), (mated, end), (o2, end), (o3, end))
     return norm_last(at, gain, share, end, near, x4[0], x4[1], out)
 
 

time: 70 us -> 68.3 us (0.976)
  waiting for transfers between devices: 7.54 us -> 3.79 us
  Pallas kernels: 40.5 us -> 41.4 us
  local copies, waits for them, and re-layouts: 1.08 us -> 1.79 us
    ppermute x18 -> x19, waiting for transfers between devices: 7.54 us -> 3.79 us  [swap(): return lax.ppermute(x, axis, [(i, i ^ bit) for i in range(size)])]
    pallas_call x1 -> x2, Pallas kernels: 1.29 us -> 2.56 us  [late_rows(): pl.pallas_call(functools.partial(late_kernel, count, heads, embed, bit),...]
    pallas_call x3, Pallas kernels: 10.3 us -> 9.42 us  [attention_rows(): pl.pallas_call(kernel, grid_spec=pltpu.PrefetchScalarGridSpec(num_scalar_...]
    ppermute x18 -> x19, starting transfers between devices: 20.3 us -> 20.7 us  [swap(): return lax.ppermute(x, axis, [(i, i ^ bit) for i in range(size)])]
  transfers between devices with their start and end apart: 18 -> 19, of which waited for: 4 -> 4; matrix products, arithmetic and copies ran while one was open for 0% -> 1% of each run, Pallas kernels for 55% -> 59%
where the time goes in v5:
time: 68.3 us; the launch traced here: 67.8 us
  Pallas kernels  41.4 us (61%)
  starting transfers between devices  20.7 us (30%)
  waiting for transfers between devices  3.79 us (6%)
  local copies, waits for them, and re-layouts  1.79 us (3%)
    ppermute x19, starting transfers between devices, swap(): return lax.ppermute(x, axis, [(i, i ^ bit) for i in range(size)])  20.7 us
    pallas_call x2, Pallas kernels, attention_quarter(): pl.pallas_call(kernel, grid_spec=pltpu.PrefetchScalarGridSpec(num_scalar_...  9.6 us
    pallas_call x3, Pallas kernels, attention_rows(): pl.pallas_call(kernel, grid_spec=pltpu.PrefetchScalarGridSpec(num_scalar_...  9.42 us
    pallas_call x3, Pallas kernels, norm_rows(): pl.pallas_call(norm_kernel, grid_spec=pltpu.PrefetchScalarGridSpec(num_sc...  8.42 us
    pallas_call x2, Pallas kernels, early_rows(): pl.pallas_call(functools.partial(early_kernel, tail), grid_spec=pltpu.Pre...  4.28 us
    pallas_call x1, Pallas kernels, block_states(): pl.pallas_call(functools.partial(state_kernel, parts, len(tokens)), in_sp...  3.97 us
    ppermute x19, waiting for transfers between devices, swap(): return lax.ppermute(x, axis, [(i, i ^ bit) for i in range(size)])  3.79 us
    pallas_call x2, Pallas kernels, late_rows(): pl.pallas_call(functools.partial(late_kernel, count, heads, embed, bit),...  2.56 us
  transfers between devices with their start and end apart: 19, of which 4 were waited for; matrix products, arithmetic and copies ran while one was open for 1% of the time, Pallas kernels for 59%

profile of v5, /device:TPU:1, one launch (start us, length us, event | category | flops | bytes accessed | tf_op | source)
XLA Modules:
  0.0 67.8 jit_solution(805096398783307958)
XLA Ops:
  0.0 1.1 %constant_dynamic-slice_fusion = (bf16[768,128]{1,0:T(8,128)(2,1)S(1)}, bf16[768,128]{1,0:T(8,128)(2,1)S(1)}) fusion(bf16[4096,512]{1,0:T(8,128)(2,1)} %q_ref.13, s32[]{:T(128)S(6)} %select_n.7, s32[]{:T(128)S(6)} %select_n.6), kind=kLoop, calls=%fused_computation | loop fusion | bytes 786440 | tf_op jit(solution)/shard_map/dynamic_slice | solution.py:508
  1.1 2.7 %collective-permute-start.2 = (bf16[768,128]{1,0:T(8,128)(2,1)S(1)}, bf16[768,128]{1,0:T(8,128)(2,1)S(1)}, u32[]{:S(2)}, u32[]{:S(2)}) collective-permute-start(bf16[768,128]{1,0:T(8,128)(2,1)S(1)} %get-tuple-element.59.rest_1_), channel_id=1, source_target_pairs={{0,3},{1,2},{2,1},{3,0},{4,7},{5,6},{6,5},{7,4},{8,11},{9,10},{10,... | collective-permute-start | bytes 589832 | tf_op jit(solution)/shard_map/ppermute | solution.py:490
  3.7 0.0 collective-permute-start.1
  3.7 4.0 %block_states.1 = (bf16[8,4,128,128]{3,2,1,0:T(8,128)(2,1)S(1)}, bf16[4,128,128]{2,1,0:T(8,128)(2,1)S(1)}) custom-call(bf16[4096,512]{1,0:T(8,128)(2,1)} %k_ref.15, bf16[4096,512]{1,0:T(8,128)(2,1)} %v_ref.15, bf16[768,128]{1,0:T(8,128)(2,1)S(1)} %get-tuple-element.60.rest_0_, bf16[768,128]{1,0:T(8,128)(2,1)S(1)} %get-tuple-element.59.rest_1_), custom_call_target="tpu_custom_call" | custom-call | flops 1024 | bytes 1024 | tf_op jit(solution)/shard_map/block_states/pallas_call | solution.py:61
  7.7 1.6 %collective-permute-start = (bf16[4,128,128]{2,1,0:T(8,128)(2,1)S(1)}, bf16[4,128,128]{2,1,0:T(8,128)(2,1)S(1)}, u32[]{:S(2)}, u32[]{:S(2)}) collective-permute-start(bf16[4,128,128]{2,1,0:T(8,128)(2,1)S(1)} %get-tuple-element.33.rest_0_.total_ref), channel_id=1, source_target_pairs={{0,4},{4,0},{8,12},{12,8},{16,20},{20,16},{24,28},{28,24},{1,5},{5... | collective-permute-start | bytes 393224 | tf_op jit(solution)/shard_map/ppermute | solution.py:490
  9.3 2.1 %early_rows.2 = (bf16[512,128]{1,0:T(8,128)(2,1)S(1)}, bf16[512,128]{1,0:T(8,128)(2,1)S(1)}) custom-call(s32[1]{0:T(128)} %bitcast.head_ref.ids_ref.quarter_ref, bf16[4096,512]{1,0:T(8,128)(2,1)} %q_ref.13, bf16[4096,512]{1,0:T(8,128)(2,1)} %k_ref.15, bf16[4096,512]{1,0:T(8,128)(2,1)} %v_ref.15, bf16[8,4,128,128]{3,2,1,0:T(8,128)(2,1)S(1)} %get-tuple-element.32.within_ref, ...), custom_call_target="tpu_custom_call" | custom-call | flops 1024 | bytes 1024 | tf_op jit(solution)/shard_map/early_rows/pallas_call | solution.py:236
  11.4 1.3 %collective-permute-start.4 = (bf16[512,128]{1,0:T(8,128)(2,1)S(1)}, bf16[512,128]{1,0:T(8,128)(2,1)S(1)}, u32[]{:S(2)}, u32[]{:S(2)}) collective-permute-start(bf16[512,128]{1,0:T(8,128)(2,1)S(1)} %get-tuple-element.34.rest_0_), channel_id=1, source_target_pairs={{0,2},{1,3},{2,0},{3,1},{4,6},{5,7},{6,4},{7,5},{8,10},{9,11},{10,... | collective-permute-start | bytes 393224 | tf_op jit(solution)/shard_map/ppermute | solution.py:490
  12.7 0.9 %collective-permute-start.5 = (bf16[512,128]{1,0:T(8,128)(2,1)S(1)}, bf16[512,128]{1,0:T(8,128)(2,1)S(1)}, u32[]{:S(2)}, u32[]{:S(2)}) collective-permute-start(bf16[512,128]{1,0:T(8,128)(2,1)S(1)} %get-tuple-element.35.rest_1_), channel_id=1, source_target_pairs={{0,3},{1,2},{2,1},{3,0},{4,7},{5,6},{6,5},{7,4},{8,11},{9,10},{10,... | collective-permute-start | bytes 393224 | tf_op jit(solution)/shard_map/ppermute | solution.py:490
  13.6 0.0 collective-permute-done.1.rest_2_.refs_4_
  13.6 0.1 add_step.2
  13.7 1.4 %collective-permute-start.3 = (bf16[4,128,128]{2,1,0:T(8,128)(2,1)S(1)}, bf16[4,128,128]{2,1,0:T(8,128)(2,1)S(1)}, u32[]{:S(2)}, u32[]{:S(2)}) collective-permute-start(bf16[4,128,128]{2,1,0:T(8,128)(2,1)S(1)} %get-tuple-element.36.rest_1_.total_ref), channel_id=1, source_target_pairs={{0,8},{4,12},{8,0},{12,4},{16,24},{20,28},{24,16},{28,20},{1,9},{5... | collective-permute-start | bytes 393224 | tf_op jit(solution)/shard_map/ppermute | solution.py:490
  15.0 2.2 %early_rows.3 = (bf16[768,128]{1,0:T(8,128)(2,1)S(1)}, bf16[768,128]{1,0:T(8,128)(2,1)S(1)}) custom-call(s32[1]{0:T(128)} %bitcast.head_ref.ids_ref.quarter_ref, bf16[4096,512]{1,0:T(8,128)(2,1)} %q_ref.13, bf16[4096,512]{1,0:T(8,128)(2,1)} %k_ref.15, bf16[4096,512]{1,0:T(8,128)(2,1)} %v_ref.15, bf16[8,4,128,128]{3,2,1,0:T(8,128)(2,1)S(1)} %get-tuple-element.32.within_ref, ...), custom_call_target="tpu_custom_call" | custom-call | flops 1024 | bytes 1024 | tf_op jit(solution)/shard_map/early_rows/pallas_call | solution.py:236
  17.2 1.3 %collective-permute-start.7 = (bf16[768,128]{1,0:T(8,128)(2,1)S(1)}, bf16[768,128]{1,0:T(8,128)(2,1)S(1)}, u32[]{:S(2)}, u32[]{:S(2)}) collective-permute-start(bf16[768,128]{1,0:T(8,128)(2,1)S(1)} %get-tuple-element.38.rest_1_), channel_id=1, source_target_pairs={{0,2},{1,3},{2,0},{3,1},{4,6},{5,7},{6,4},{7,5},{8,10},{9,11},{10,... | collective-permute-start | bytes 589832 | tf_op jit(solution)/shard_map/ppermute | solution.py:490
  18.5 1.1 %collective-permute-start.8 = (bf16[768,128]{1,0:T(8,128)(2,1)S(1)}, bf16[768,128]{1,0:T(8,128)(2,1)S(1)}, u32[]{:S(2)}, u32[]{:S(2)}) collective-permute-start(bf16[768,128]{1,0:T(8,128)(2,1)S(1)} %get-tuple-element.39.rest_2_), channel_id=1, source_target_pairs={{0,3},{1,2},{2,1},{3,0},{4,7},{5,6},{6,5},{7,4},{8,11},{9,10},{10,... | collective-permute-start | bytes 589832 | tf_op jit(solution)/shard_map/ppermute | solution.py:490
  19.6 0.0 collective-permute-done.3.got_ref
  19.6 0.1 add_step.3
  19.7 2.4 %collective-permute-start.6 = (bf16[4,128,128]{2,1,0:T(8,128)(2,1)S(1)}, bf16[4,128,128]{2,1,0:T(8,128)(2,1)S(1)}, u32[]{:S(2)}, u32[]{:S(2)}) collective-permute-start(bf16[4,128,128]{2,1,0:T(8,128)(2,1)S(1)} %get-tuple-element.40.rest_0_), channel_id=1, source_target_pairs={{0,16},{4,20},{8,24},{12,28},{16,0},{20,4},{24,8},{28,12},{1,17},{... | collective-permute-start | bytes 393224 | tf_op jit(solution)/shard_map/ppermute | solution.py:490
  22.1 2.5 %attention_rows.3 = (f32[256,384]{1,0:T(8,128)S(1)}, f32[256,384]{1,0:T(8,128)S(1)}, bf16[256,384]{1,0:T(8,128)(2,1)S(1)}, bf16[256,384]{1,0:T(8,128)(2,1)S(1)}) custom-call(s32[1]{0:T(128)} %bitcast.head_ref.ids_ref.quarter_ref, bf16[4096,512]{1,0:T(8,128)(2,1)} %q_ref.13, bf16[4096,512]{1,0:T(8,128)(2,1)} %k_ref.15, bf16[4096,512]{1,0:T(8,128)(2,1)} %v_ref.15, ...), custom_call_target="tpu_custom_call" | custom-call | flops 1024 | bytes 1024 | tf_op jit(solution)/shard_map/attention_rows/pallas_call | solution.py:161
  24.5 3.7 %attention_rows.4 = (bf16[512,384]{1,0:T(8,128)(2,1)S(1)}, bf16[512,384]{1,0:T(8,128)(2,1)S(1)}) custom-call(s32[1]{0:T(128)} %bitcast.head_ref.ids_ref.quarter_ref, bf16[4096,512]{1,0:T(8,128)(2,1)} %q_ref.13, bf16[4096,512]{1,0:T(8,128)(2,1)} %k_ref.15, bf16[4096,512]{1,0:T(8,128)(2,1)} %v_ref.15, ...), custom_call_target="tpu_custom_call" | custom-call | flops 1024 | bytes 1024 | tf_op jit(solution)/shard_map/attention_rows/pallas_call | solution.py:161
  28.2 0.0 collective-permute-done.7.refs_7_.refs_2_
  28.2 0.1 collective-permute-done.8.refs_8_.refs_3_
  28.4 0.1 collective-permute-done.6.refs_6_
  28.5 0.3 late_rows.2
  28.8 0.1 copy-done
  28.9 1.2 %collective-permute-start.10 = (bf16[304,384]{1,0:T(8,128)(2,1)S(1)}, bf16[304,384]{1,0:T(8,128)(2,1)S(1)}, u32[]{:S(2)}, u32[]{:S(2)}) collective-permute-start(bf16[304,384]{1,0:T(8,128)(2,1)S(1)} %get-tuple-element.49.refs_5_), channel_id=1, source_target_pairs={{0,2},{1,3},{2,0},{3,1},{4,6},{5,7},{6,4},{7,5},{8,10},{9,11},{10,... | collective-permute-start | bytes 700424 | tf_op jit(solution)/shard_map/ppermute | solution.py:490
  30.1 1.2 %collective-permute-start.12 = (bf16[256,384]{1,0:T(8,128)(2,1)S(1)}, bf16[256,384]{1,0:T(8,128)(2,1)S(1)}, u32[]{:S(2)}, u32[]{:S(2)}) collective-permute-start(bf16[256,384]{1,0:T(8,128)(2,1)S(1)} %get-tuple-element.50.refs_6_), channel_id=1, source_target_pairs={{0,3},{1,2},{2,1},{3,0},{4,7},{5,6},{6,5},{7,4},{8,11},{9,10},{10,... | collective-permute-start | bytes 589832 | tf_op jit(solution)/shard_map/ppermute | solution.py:490
  31.3 2.3 %late_rows.3 = (bf16[512,384]{1,0:T(8,128)(2,1)}, bf16[512,384]{1,0:T(8,128)(2,1)}) custom-call(s32[1]{0:T(128)} %bitcast.head_ref.ids_ref.quarter_ref, bf16[4096,512]{1,0:T(8,128)(2,1)} %q_ref.13, bf16[512,384]{1,0:T(8,128)(2,1)S(1)} %get-tuple-element.46.refs_9_.refs_1_, bf16[4096,512]{1,0:T(8,128)(2,1)} %q_ref.13, ...), custom_call_target="tpu_custom_call" | custom-call | flops 1024 | bytes 1024 | tf_op jit(solution)/shard_map/late_rows/pallas_call | solution.py:301
  33.6 1.2 %collective-permute-start.17 = (bf16[512,384]{1,0:T(8,128)(2,1)}, bf16[512,384]{1,0:T(8,128)(2,1)}, u32[]{:S(2)}, u32[]{:S(2)}) collective-permute-start(bf16[512,384]{1,0:T(8,128)(2,1)} %get-tuple-element.51.rest_1_), channel_id=1, source_target_pairs={{0,2},{1,3},{2,0},{3,1},{4,6},{5,7},{6,4},{7,5},{8,10},{9,11},{10,... | collective-permute-start | bytes 1179656 | tf_op jit(solution)/shard_map/ppermute | solution.py:490
  34.9 5.2 %attention_quarter.2.rest_1_ = bf16[1024,512]{1,0:T(8,128)(2,1)} custom-call(s32[1]{0:T(128)} %bitcast.head_ref.ids_ref.quarter_ref, bf16[4096,512]{1,0:T(8,128)(2,1)} %q_ref.13, bf16[4096,512]{1,0:T(8,128)(2,1)} %k_ref.15, bf16[4096,512]{1,0:T(8,128)(2,1)} %v_ref.15, bf16[8,4,128,128]{3,2,1,0:T(8,128)(2,1)S(1)} %get-tuple-element.32.within_ref, ...), custom_call_target="tpu_custom_call" | custom-call | flops 1024 | bytes 1024 | tf_op jit(solution)/shard_map/attention_quarter/pallas_call | solution.py:195
  40.1 0.3 collective-permute-start.18
  40.4 4.4 %attention_quarter.3.own_ref.rest_1_ = bf16[1024,512]{1,0:T(8,128)(2,1)S(1)} custom-call(s32[1]{0:T(128)} %bitcast.head_ref.ids_ref.quarter_ref, bf16[4096,512]{1,0:T(8,128)(2,1)} %q_ref.13, bf16[4096,512]{1,0:T(8,128)(2,1)} %k_ref.15, bf16[4096,512]{1,0:T(8,128)(2,1)} %v_ref.15, bf16[8,4,128,128]{3,2,1,0:T(8,128)(2,1)S(1)} %get-tuple-element.32.within_ref, ...), custom_call_target="tpu_custom_call" | custom-call | flops 1024 | bytes 1024 | tf_op jit(solution)/shard_map/attention_quarter/pallas_call | solution.py:195
  44.8 0.4 collective-permute-start.9
  45.2 0.0 collective-permute-done.10.rest_2_.x2_ref
  45.2 0.6 slice.4.refs_6_
  45.8 0.2 collective-permute-start.11
  46.0 3.3 %attention_rows.5 = (bf16[128,384]{1,0:T(8,128)(2,1)S(1)}, bf16[128,384]{1,0:T(8,128)(2,1)S(1)}, bf16[128,384]{1,0:T(8,128)(2,1)S(1)}, bf16[128,384]{1,0:T(8,128)(2,1)S(1)}) custom-call(s32[1]{0:T(128)} %bitcast.head_ref.ids_ref.quarter_ref, bf16[4096,512]{1,0:T(8,128)(2,1)} %q_ref.13, bf16[4096,512]{1,0:T(8,128)(2,1)} %k_ref.15, bf16[4096,512]{1,0:T(8,128)(2,1)} %v_ref.15, ...), custom_call_target="tpu_custom_call" | custom-call | flops 999999995904 | bytes 1024 | tf_op jit(solution)/shard_map/attention_rows/pallas_call | solution.py:161
  49.3 1.1 %collective-permute-start.13 = (bf16[128,384]{1,0:T(8,128)(2,1)S(1)}, bf16[128,384]{1,0:T(8,128)(2,1)S(1)}, u32[]{:S(2)}, u32[]{:S(2)}) collective-permute-start(bf16[128,384]{1,0:T(8,128)(2,1)S(1)} %get-tuple-element.55), channel_id=1, source_target_pairs={{0,2},{1,3},{2,0},{3,1},{4,6},{5,7},{6,4},{7,5},{8,10},{9,11},{10,... | collective-permute-start | bytes 294920 | tf_op jit(solution)/shard_map/ppermute | solution.py:490
  50.4 0.4 collective-permute-start.15
  50.8 2.0 %collective-permute-start.16 = (bf16[128,384]{1,0:T(8,128)(2,1)S(1)}, bf16[128,384]{1,0:T(8,128)(2,1)S(1)}, u32[]{:S(2)}, u32[]{:S(2)}) collective-permute-start(bf16[128,384]{1,0:T(8,128)(2,1)S(1)} %get-tuple-element.58), channel_id=1, source_target_pairs={{0,3},{1,2},{2,1},{3,0},{4,7},{5,6},{6,5},{7,4},{8,11},{9,10},{10,... | collective-permute-start | bytes 294920 | tf_op jit(solution)/shard_map/ppermute | solution.py:490
  52.8 0.1 collective-permute-start.14
  52.9 1.1 %early_out.1 = (bf16[1024,128]{1,0:T(8,128)(2,1)S(1)}, bf16[1024,128]{1,0:T(8,128)(2,1)S(1)}) custom-call(bf16[512,128]{1,0:T(8,128)(2,1)S(1)} %collective-permute-done.4.rest_3_.refs_0_, bf16[512,128]{1,0:T(8,128)(2,1)S(1)} %collective-permute-done.5.rest_4_.refs_1_, bf16[768,128]{1,0:T(8,128)(2,1)S(1)} %copy-done.1, bf16[768,128]{1,0:T(8,128)(2,1)S(1)} %copy-done.3, ...), custom_call_target="tpu_custom_call" | custom-call | flops 1024 | bytes 1024 | tf_op jit(solution)/shard_map/early_out/pallas_call | solution.py:345
  54.0 0.9 %gather_rows.1.near_ref = bf16[128,1280]{1,0:T(8,128)(2,1)S(1)} custom-call(bf16[1024,512]{1,0:T(8,128)(2,1)S(1)} %attention_quarter.3.own_ref.rest_1_, bf16[1024,512]{1,0:T(8,128)(2,1)} %collective-permute-done.9.mate_ref, bf16[1024,128]{1,0:T(8,128)(2,1)S(1)} %get-tuple-element.53.o2_ref, bf16[1024,128]{1,0:T(8,128)(2,1)S(1)} %get-tuple-element.54.o3_ref), custom_call_target="tpu_custom_call" | custom-call | flops 1024 | bytes 1024 | tf_op jit(solution)/shard_map/gather_rows/pallas_call | solution.py:370
  54.9 2.3 %norm_rows.3.rest_0_ = bf16[1024,2048]{1,0:T(8,128)(2,1)} custom-call(s32[1]{0:T(128)} %bitcast.head_ref.ids_ref.quarter_ref, f32[1,2048]{1,0:T(1,128)S(1)} %bitcast.3, bf16[1024,512]{1,0:T(8,128)(2,1)S(1)} %attention_quarter.3.own_ref.rest_1_, bf16[1024,512]{1,0:T(8,128)(2,1)} %collective-permute-done.9.mate_ref, ...), custom_call_target="tpu_custom_call" | custom-call | flops 1024 | bytes 1024 | tf_op jit(solution)/shard_map/norm_rows/pallas_call | solution.py:445
  57.2 1.6 %collective-permute-done.18.x3_ref = bf16[512,384]{1,0:T(8,128)(2,1)} collective-permute-done((bf16[512,384]{1,0:T(8,128)(2,1)}, bf16[512,384]{1,0:T(8,128)(2,1)}, u32[]{:S(2)}, u32[]{:S(2)}) %collective-permute-start.18) | collective-permute-done | bytes 393248 | tf_op jit(solution)/shard_map/ppermute | solution.py:490
  58.8 4.2 %norm_rows.4.rest_0_ = bf16[1024,2048]{1,0:T(8,128)(2,1)} custom-call(s32[1]{0:T(128)} %bitcast.head_ref.ids_ref.quarter_ref, f32[1,2048]{1,0:T(1,128)S(1)} %bitcast.4, bf16[1024,512]{1,0:T(8,128)(2,1)S(1)} %attention_quarter.3.own_ref.rest_1_, bf16[1024,512]{1,0:T(8,128)(2,1)} %collective-permute-done.9.mate_ref, ...), custom_call_target="tpu_custom_call", output_to_operand_aliasing={{}: (8, {})} | custom-call | flops 1024 | bytes 1024 | tf_op jit(solution)/shard_map/norm_rows/pallas_call | solution.py:445
  63.0 1.8 %collective-permute-done.16.x3_ref = bf16[128,384]{1,0:T(8,128)(2,1)S(1)} collective-permute-done((bf16[128,384]{1,0:T(8,128)(2,1)S(1)}, bf16[128,384]{1,0:T(8,128)(2,1)S(1)}, u32[]{:S(2)}, u32[]{:S(2)}) %collective-permute-start.16) | collective-permute-done | bytes 98336 | tf_op jit(solution)/shard_map/ppermute | solution.py:490
  64.8 2.0 %norm_rows.5.old_ref = bf16[1024,2048]{1,0:T(8,128)(2,1)} custom-call(s32[1]{0:T(128)} %bitcast.head_ref.ids_ref.quarter_ref, f32[1,2048]{1,0:T(1,128)S(1)} %bitcast.5, bf16[1024,512]{1,0:T(8,128)(2,1)S(1)} %attention_quarter.3.own_ref.rest_1_, bf16[1024,512]{1,0:T(8,128)(2,1)} %collective-permute-done.9.mate_ref, ...), custom_call_target="tpu_custom_call", output_to_operand_aliasing={{}: (8, {})} | custom-call | flops 1024 | bytes 1024 | tf_op jit(solution)/shard_map/norm_rows/pallas_call | solution.py:445
  66.8 1.1 %norm_last.1 = bf16[1024,2048]{1,0:T(8,128)(2,1)} custom-call(s32[1]{0:T(128)} %bitcast.head_ref.ids_ref.quarter_ref, f32[1,2048]{1,0:T(1,128)S(1)} %bitcast.6, bf16[128,1280]{1,0:T(8,128)(2,1)S(1)} %gather_rows.1.near_ref, bf16[128,384]{1,0:T(8,128)(2,1)S(1)} %collective-permute-done.13.x2_ref, ...), custom_call_target="tpu_custom_call", output_to_operand_aliasing={{}: (5, {})} | custom-call | flops 1024 | bytes 1024 | tf_op jit(solution)/shard_map/norm_last/pallas_call | solution.py:393
  (20 shorter events, 0.0 us)
Async XLA Ops:
  1.1 12.5 %collective-permute-start.2 = (bf16[768,128]{1,0:T(8,128)(2,1)S(1)}, bf16[768,128]{1,0:T(8,128)(2,1)S(1)}, u32[]{:S(2)}, u32[]{:S(2)}) collective-permute-start(bf16[768,128]{1,0:T(8,128)(2,1)S(1)} %get-tuple-element.59.rest_1_), channel_id=1, source_target_pairs={{0,3},{1,2},{2,1},{3,0},{4,7},{5,6},{6,5},{7,4},{8,11},{9,10},{10,... | collective-permute-start | bytes 589832 | tf_op jit(solution)/shard_map/ppermute | solution.py:490
  3.7 9.9 %collective-permute-start.1 = (bf16[768,128]{1,0:T(8,128)(2,1)S(1)}, bf16[768,128]{1,0:T(8,128)(2,1)S(1)}, u32[]{:S(2)}, u32[]{:S(2)}) collective-permute-start(bf16[768,128]{1,0:T(8,128)(2,1)S(1)} %get-tuple-element.60.rest_0_), channel_id=1, source_target_pairs={{0,2},{1,3},{2,0},{3,1},{4,6},{5,7},{6,4},{7,5},{8,10},{9,11},{10,... | collective-permute-start | bytes 589832 | tf_op jit(solution)/shard_map/ppermute | solution.py:490
  7.7 5.9 %collective-permute-start = (bf16[4,128,128]{2,1,0:T(8,128)(2,1)S(1)}, bf16[4,128,128]{2,1,0:T(8,128)(2,1)S(1)}, u32[]{:S(2)}, u32[]{:S(2)}) collective-permute-start(bf16[4,128,128]{2,1,0:T(8,128)(2,1)S(1)} %get-tuple-element.33.rest_0_.total_ref), channel_id=1, source_target_pairs={{0,4},{4,0},{8,12},{12,8},{16,20},{20,16},{24,28},{28,24},{1,5},{5... | collective-permute-start | bytes 393224 | tf_op jit(solution)/shard_map/ppermute | solution.py:490
  11.4 8.2 %collective-permute-start.4 = (bf16[512,128]{1,0:T(8,128)(2,1)S(1)}, bf16[512,128]{1,0:T(8,128)(2,1)S(1)}, u32[]{:S(2)}, u32[]{:S(2)}) collective-permute-start(bf16[512,128]{1,0:T(8,128)(2,1)S(1)} %get-tuple-element.34.rest_0_), channel_id=1, source_target_pairs={{0,2},{1,3},{2,0},{3,1},{4,6},{5,7},{6,4},{7,5},{8,10},{9,11},{10,... | collective-permute-start | bytes 393224 | tf_op jit(solution)/shard_map/ppermute | solution.py:490
  12.7 6.9 %collective-permute-start.5 = (bf16[512,128]{1,0:T(8,128)(2,1)S(1)}, bf16[512,128]{1,0:T(8,128)(2,1)S(1)}, u32[]{:S(2)}, u32[]{:S(2)}) collective-permute-start(bf16[512,128]{1,0:T(8,128)(2,1)S(1)} %get-tuple-element.35.rest_1_), channel_id=1, source_target_pairs={{0,3},{1,2},{2,1},{3,0},{4,7},{5,6},{6,5},{7,4},{8,11},{9,10},{10,... | collective-permute-start | bytes 393224 | tf_op jit(solution)/shard_map/ppermute | solution.py:490
  13.7 5.9 %collective-permute-start.3 = (bf16[4,128,128]{2,1,0:T(8,128)(2,1)S(1)}, bf16[4,128,128]{2,1,0:T(8,128)(2,1)S(1)}, u32[]{:S(2)}, u32[]{:S(2)}) collective-permute-start(bf16[4,128,128]{2,1,0:T(8,128)(2,1)S(1)} %get-tuple-element.36.rest_1_.total_ref), channel_id=1, source_target_pairs={{0,8},{4,12},{8,0},{12,4},{16,24},{20,28},{24,16},{28,20},{1,9},{5... | collective-permute-start | bytes 393224 | tf_op jit(solution)/shard_map/ppermute | solution.py:490
  17.2 11.0 %collective-permute-start.7 = (bf16[768,128]{1,0:T(8,128)(2,1)S(1)}, bf16[768,128]{1,0:T(8,128)(2,1)S(1)}, u32[]{:S(2)}, u32[]{:S(2)}) collective-permute-start(bf16[768,128]{1,0:T(8,128)(2,1)S(1)} %get-tuple-element.38.rest_1_), channel_id=1, source_target_pairs={{0,2},{1,3},{2,0},{3,1},{4,6},{5,7},{6,4},{7,5},{8,10},{9,11},{10,... | collective-permute-start | bytes 589832 | tf_op jit(solution)/shard_map/ppermute | solution.py:490
  18.5 9.9 %collective-permute-start.8 = (bf16[768,128]{1,0:T(8,128)(2,1)S(1)}, bf16[768,128]{1,0:T(8,128)(2,1)S(1)}, u32[]{:S(2)}, u32[]{:S(2)}) collective-permute-start(bf16[768,128]{1,0:T(8,128)(2,1)S(1)} %get-tuple-element.39.rest_2_), channel_id=1, source_target_pairs={{0,3},{1,2},{2,1},{3,0},{4,7},{5,6},{6,5},{7,4},{8,11},{9,10},{10,... | collective-permute-start | bytes 589832 | tf_op jit(solution)/shard_map/ppermute | solution.py:490
  19.7 8.9 %collective-permute-start.6 = (bf16[4,128,128]{2,1,0:T(8,128)(2,1)S(1)}, bf16[4,128,128]{2,1,0:T(8,128)(2,1)S(1)}, u32[]{:S(2)}, u32[]{:S(2)}) collective-permute-start(bf16[4,128,128]{2,1,0:T(8,128)(2,1)S(1)} %get-tuple-element.40.rest_0_), channel_id=1, source_target_pairs={{0,16},{4,20},{8,24},{12,28},{16,0},{20,4},{24,8},{28,12},{1,17},{... | collective-permute-start | bytes 393224 | tf_op jit(solution)/shard_map/ppermute | solution.py:490
  28.2 0.7 %copy-start = (bf16[768,128]{1,0:T(8,128)(2,1)}, bf16[768,128]{1,0:T(8,128)(2,1)S(1)}, u32[]{:S(2)}) copy-start(bf16[768,128]{1,0:T(8,128)(2,1)S(1)} %collective-permute-done.7.refs_7_.refs_2_) | copy-start | bytes 589828
  28.4 5.3 %copy-start.2 = (bf16[768,128]{1,0:T(8,128)(2,1)}, bf16[768,128]{1,0:T(8,128)(2,1)S(1)}, u32[]{:S(2)}) copy-start(bf16[768,128]{1,0:T(8,128)(2,1)S(1)} %collective-permute-done.8.refs_8_.refs_3_) | copy-start | bytes 589828
  28.9 16.3 %collective-permute-start.10 = (bf16[304,384]{1,0:T(8,128)(2,1)S(1)}, bf16[304,384]{1,0:T(8,128)(2,1)S(1)}, u32[]{:S(2)}, u32[]{:S(2)}) collective-permute-start(bf16[304,384]{1,0:T(8,128)(2,1)S(1)} %get-tuple-element.49.refs_5_), channel_id=1, source_target_pairs={{0,2},{1,3},{2,0},{3,1},{4,6},{5,7},{6,4},{7,5},{8,10},{9,11},{10,... | collective-permute-start | bytes 700424 | tf_op jit(solution)/shard_map/ppermute | solution.py:490
  30.1 15.8 %collective-permute-start.12 = (bf16[256,384]{1,0:T(8,128)(2,1)S(1)}, bf16[256,384]{1,0:T(8,128)(2,1)S(1)}, u32[]{:S(2)}, u32[]{:S(2)}) collective-permute-start(bf16[256,384]{1,0:T(8,128)(2,1)S(1)} %get-tuple-element.50.refs_6_), channel_id=1, source_target_pairs={{0,3},{1,2},{2,1},{3,0},{4,7},{5,6},{6,5},{7,4},{8,11},{9,10},{10,... | collective-permute-start | bytes 589832 | tf_op jit(solution)/shard_map/ppermute | solution.py:490
  33.6 17.2 %collective-permute-start.17 = (bf16[512,384]{1,0:T(8,128)(2,1)}, bf16[512,384]{1,0:T(8,128)(2,1)}, u32[]{:S(2)}, u32[]{:S(2)}) collective-permute-start(bf16[512,384]{1,0:T(8,128)(2,1)} %get-tuple-element.51.rest_1_), channel_id=1, source_target_pairs={{0,2},{1,3},{2,0},{3,1},{4,6},{5,7},{6,4},{7,5},{8,10},{9,11},{10,... | collective-permute-start | bytes 1179656 | tf_op jit(solution)/shard_map/ppermute | solution.py:490
  40.1 18.7 %collective-permute-start.18 = (bf16[512,384]{1,0:T(8,128)(2,1)}, bf16[512,384]{1,0:T(8,128)(2,1)}, u32[]{:S(2)}, u32[]{:S(2)}) collective-permute-start(bf16[512,384]{1,0:T(8,128)(2,1)} %get-tuple-element.52.rest_2_), channel_id=1, source_target_pairs={{0,3},{1,2},{2,1},{3,0},{4,7},{5,6},{6,5},{7,4},{8,11},{9,10},{10,... | collective-permute-start | bytes 1179656 | tf_op jit(solution)/shard_map/ppermute | solution.py:490
  44.8 8.0 %collective-permute-start.9 = (bf16[1024,512]{1,0:T(8,128)(2,1)}, bf16[1024,512]{1,0:T(8,128)(2,1)}, u32[]{:S(2)}, u32[]{:S(2)}) collective-permute-start(bf16[1024,512]{1,0:T(8,128)(2,1)} %attention_quarter.2.rest_1_), channel_id=1, source_target_pairs={{0,1},{1,0},{2,3},{3,2},{4,5},{5,4},{6,7},{7,6},{8,9},{9,8},{10,11... | collective-permute-start | bytes 3145736 | tf_op jit(solution)/shard_map/ppermute | solution.py:490
  45.8 4.6 %collective-permute-start.11 = (bf16[48,384]{1,0:T(8,128)(2,1)}, bf16[48,384]{1,0:T(8,128)(2,1)}, u32[]{:S(2)}, u32[]{:S(2)}) collective-permute-start(bf16[48,384]{1,0:T(8,128)(2,1)} %slice.4.refs_6_), channel_id=1, source_target_pairs={{0,1},{1,0},{2,3},{3,2},{4,5},{5,4},{6,7},{7,6},{8,9},{9,8},{10,11... | collective-permute-start | bytes 110600 | tf_op jit(solution)/shard_map/ppermute | solution.py:490
  46.0 6.9 %copy-start.1 = (bf16[768,128]{1,0:T(8,128)(2,1)S(1)}, bf16[768,128]{1,0:T(8,128)(2,1)}, u32[]{:S(2)}) copy-start(bf16[768,128]{1,0:T(8,128)(2,1)} %copy-done) | copy-start | bytes 589828
  46.0 6.9 %copy-start.3 = (bf16[768,128]{1,0:T(8,128)(2,1)S(1)}, bf16[768,128]{1,0:T(8,128)(2,1)}, u32[]{:S(2)}) copy-start(bf16[768,128]{1,0:T(8,128)(2,1)} %copy-done.2) | copy-start | bytes 589828
  46.0 8.9 %copy-start.4 = (f32[2048]{0:T(1024)S(1)}, f32[2048]{0:T(1024)}, u32[]{:S(2)}) copy-start(f32[2048]{0:T(1024)} %param.7) | copy-start | bytes 24580
  49.3 17.5 %collective-permute-start.13 = (bf16[128,384]{1,0:T(8,128)(2,1)S(1)}, bf16[128,384]{1,0:T(8,128)(2,1)S(1)}, u32[]{:S(2)}, u32[]{:S(2)}) collective-permute-start(bf16[128,384]{1,0:T(8,128)(2,1)S(1)} %get-tuple-element.55), channel_id=1, source_target_pairs={{0,2},{1,3},{2,0},{3,1},{4,6},{5,7},{6,4},{7,5},{8,10},{9,11},{10,... | collective-permute-start | bytes 294920 | tf_op jit(solution)/shard_map/ppermute | solution.py:490
  50.4 12.6 %collective-permute-start.15 = (bf16[128,384]{1,0:T(8,128)(2,1)S(1)}, bf16[128,384]{1,0:T(8,128)(2,1)S(1)}, u32[]{:S(2)}, u32[]{:S(2)}) collective-permute-start(bf16[128,384]{1,0:T(8,128)(2,1)S(1)} %get-tuple-element.57), channel_id=1, source_target_pairs={{0,2},{1,3},{2,0},{3,1},{4,6},{5,7},{6,4},{7,5},{8,10},{9,11},{10,... | collective-permute-start | bytes 294920 | tf_op jit(solution)/shard_map/ppermute | solution.py:490
  50.8 14.0 %collective-permute-start.16 = (bf16[128,384]{1,0:T(8,128)(2,1)S(1)}, bf16[128,384]{1,0:T(8,128)(2,1)S(1)}, u32[]{:S(2)}, u32[]{:S(2)}) collective-permute-start(bf16[128,384]{1,0:T(8,128)(2,1)S(1)} %get-tuple-element.58), channel_id=1, source_target_pairs={{0,3},{1,2},{2,1},{3,0},{4,7},{5,6},{6,5},{7,4},{8,11},{9,10},{10,... | collective-permute-start | bytes 294920 | tf_op jit(solution)/shard_map/ppermute | solution.py:490
  52.8 14.0 %collective-permute-start.14 = (bf16[128,384]{1,0:T(8,128)(2,1)S(1)}, bf16[128,384]{1,0:T(8,128)(2,1)S(1)}, u32[]{:S(2)}, u32[]{:S(2)}) collective-permute-start(bf16[128,384]{1,0:T(8,128)(2,1)S(1)} %get-tuple-element.56), channel_id=1, source_target_pairs={{0,3},{1,2},{2,1},{3,0},{4,7},{5,6},{6,5},{7,4},{8,11},{9,10},{10,... | collective-permute-start | bytes 294920 | tf_op jit(solution)/shard_map/ppermute | solution.py:490

commit v6 on v5

--- a/solution.py
+++ b/solution.py
@@ -17,7 +17,7 @@
 LONG = pl.CostEstimate(flops=10**12, bytes_accessed=1024, transcendentals=0)
 
 
-def params(mib=50):
+def params(mib=49):
     return pltpu.CompilerParams(vmem_limit_bytes=mib * 1024 * 1024)
 
 
@@ -458,6 +458,73 @@
     )(head, *operands)
 
 
+def norm_block_kernel(row, size, places, width, head_ref, *refs):
+    count, tiles = len(places), size // TILE
+    ins = refs[:count + 1]
+    out_ref, gain_buf, *bufs, out_buf, gain_sem, in_sem, out_sem = refs[len(refs) - count - 6:]
+    gain_copy = pltpu.make_async_copy(ins[0], gain_buf, gain_sem)
+    gain_copy.start()
+    copies = []
+    for t in range(tiles):
+        here = pl.ds(t * TILE, TILE)
+        copies.append([])
+        for n in range(count):
+            there = pl.ds(places[n][0] + t * TILE, TILE)
+            copy = pltpu.make_async_copy(ins[n + 1].at[there], bufs[n].at[here], in_sem.at[t, n])
+            copy.start()
+            copies[t].append(copy)
+    gain_copy.wait()
+    head = head_ref[0]
+    sent = []
+    for t in range(tiles):
+        here = pl.ds(t * TILE, TILE)
+        for copy in copies[t]:
+            copy.wait()
+        total = jnp.zeros((TILE, DH), jnp.float32)
+        for buf in bufs:
+            for c in range(buf.shape[1] // DH):
+                wide = buf[here, pl.ds(c * DH, DH)].astype(jnp.float32)
+                total += wide * wide
+        scale = lax.rsqrt(jnp.sum(total, axis=-1, keepdims=True) / (4 * width) + EPS)
+        for buf, (_, partner, offset) in zip(bufs, places):
+            at = pl.multiple_of((head ^ partner) * width + offset, DH)
+            cols = pl.ds(at, buf.shape[1])
+            out_buf[here, cols] = (buf[here, :].astype(jnp.float32) * scale * gain_buf[:, cols]).astype(jnp.bfloat16)
+        copy = pltpu.make_async_copy(out_buf.at[here], out_ref.at[pl.ds(row + t * TILE, TILE)], out_sem.at[t])
+        copy.start()
+        sent.append(copy)
+    for copy in sent:
+        copy.wait()
+
+
+def norm_block(head, gain, share, row, size, own, mate, x2, x3, o2, o3, out):
+    width = own[0].shape[1]
+    pieces = ((own, 0, 0), (mate, 1, 0), (x2, 2, 0), (o2, 2, width - DH), (x3, 3, 0), (o3, 3, width - DH))
+    arrays = [piece[0][0] for piece in pieces]
+    places = [(piece[0][1], piece[1], piece[2]) for piece in pieces]
+    anywhere = pl.BlockSpec(memory_space=pl.ANY)
+    operands = [gain, *arrays] + ([] if out is None else [out])
+    tiles = size // TILE
+    return pl.pallas_call(
+        functools.partial(norm_block_kernel, row, size, places, width),
+        in_specs=[pl.BlockSpec(memory_space=pltpu.SMEM)] + [anywhere] * len(operands),
+        out_specs=anywhere,
+        out_shape=jax.ShapeDtypeStruct((share, 4 * width), jnp.bfloat16),
+        input_output_aliases={} if out is None else {len(operands): 0},
+        scratch_shapes=[pltpu.VMEM(gain.shape, jnp.float32)]
+        + [pltpu.VMEM((size, array.shape[1]), jnp.bfloat16) for array in arrays]
+        + [
+            pltpu.VMEM((size, 4 * width), jnp.bfloat16),
+            pltpu.SemaphoreType.DMA(()),
+            pltpu.SemaphoreType.DMA((tiles, len(arrays))),
+            pltpu.SemaphoreType.DMA((tiles,)),
+        ],
+        compiler_params=params(),
+        cost_estimate=COST,
+        name="norm_block",
+    )(head, *operands)
+
+
 def add_kernel(bit, with_before, mine_ref, total_ref, got_ref, *rest):
     group_ref, after_ref = rest[-2:]
     got = got_ref[...].astype(jnp.float32)
@@ -548,7 +615,8 @@
     out = None
     end = share - HALF // 2
     for row, size, (y2, y3) in ((BLK, HALF, x1), (0, BLK, x2), (BLK + HALF, HALF // 2, x3)):
-        out = norm_rows(
+        norm = norm_block if size == BLK else norm_rows
+        out = norm(
             at, gain, share, row, size, (own, row), (mated, row), (y2, 0), (y3, 0), (o2, row), (o3, row), out
         )
     near = gather_rows(share - end, (own, end), (mated, end), (o2, end), (o3, end))

time: 68.3 us -> 68.3 us (level)
  waiting for transfers between devices: 3.79 us -> 4.64 us
  Pallas kernels: 41.4 us -> 40.6 us
    pallas_call x3 -> x2, Pallas kernels: 8.42 us -> 4.24 us  [norm_rows(): pl.pallas_call(norm_kernel, grid_spec=pltpu.PrefetchScalarGridSpec(num_sc...]
    pallas_call x0 -> x1, Pallas kernels: none -> 3.31 us  [norm_block(): pl.pallas_call(functools.partial(norm_block_kernel, row, size, places, wi...]
    ppermute x19, waiting for transfers between devices: 3.79 us -> 4.64 us  [swap(): return lax.ppermute(x, axis, [(i, i ^ bit) for i in range(size)])]
  transfers between devices with their start and end apart: 19 -> 19, of which waited for: 4 -> 4; matrix products, arithmetic and copies ran while one was open for 1% -> 1% of each run, Pallas kernels for 59% -> 58%
where the time goes in v6:
time: 68.3 us; the launch traced here: 67.8 us
  Pallas kernels  40.6 us (59%)
  starting transfers between devices  20.7 us (30%)
  waiting for transfers between devices  4.64 us (7%)
  local copies, waits for them, and re-layouts  1.79 us (3%)
    ppermute x19, starting transfers between devices, swap(): return lax.ppermute(x, axis, [(i, i ^ bit) for i in range(size)])  20.7 us
    pallas_call x2, Pallas kernels, attention_quarter(): pl.pallas_call(kernel, grid_spec=pltpu.PrefetchScalarGridSpec(num_scalar_...  9.6 us
    pallas_call x3, Pallas kernels, attention_rows(): pl.pallas_call(kernel, grid_spec=pltpu.PrefetchScalarGridSpec(num_scalar_...  9.42 us
    ppermute x19, waiting for transfers between devices, swap(): return lax.ppermute(x, axis, [(i, i ^ bit) for i in range(size)])  4.64 us
    pallas_call x2, Pallas kernels, early_rows(): pl.pallas_call(functools.partial(early_kernel, tail), grid_spec=pltpu.Pre...  4.28 us
    pallas_call x2, Pallas kernels, norm_rows(): pl.pallas_call(norm_kernel, grid_spec=pltpu.PrefetchScalarGridSpec(num_sc...  4.24 us
    pallas_call x1, Pallas kernels, block_states(): pl.pallas_call(functools.partial(state_kernel, parts, len(tokens)), in_sp...  3.97 us
    pallas_call x1, Pallas kernels, norm_block(): pl.pallas_call(functools.partial(norm_block_kernel, row, size, places, wi...  3.31 us
  transfers between devices with their start and end apart: 19, of which 4 were waited for; matrix products, arithmetic and copies ran while one was open for 1% of the time, Pallas kernels for 58%

profile of v6, /device:TPU:1, one launch (start us, length us, event | category | flops | bytes accessed | tf_op | source)
XLA Modules:
  0.0 67.8 jit_solution(8046606346498619936)
XLA Ops:
  0.0 1.1 %constant_dynamic-slice_fusion = (bf16[768,128]{1,0:T(8,128)(2,1)S(1)}, bf16[768,128]{1,0:T(8,128)(2,1)S(1)}) fusion(bf16[4096,512]{1,0:T(8,128)(2,1)} %q_ref.13, s32[]{:T(128)S(6)} %select_n.7, s32[]{:T(128)S(6)} %select_n.6), kind=kLoop, calls=%fused_computation | loop fusion | bytes 786440 | tf_op jit(solution)/shard_map/dynamic_slice | solution.py:575
  1.1 2.7 %collective-permute-start.2 = (bf16[768,128]{1,0:T(8,128)(2,1)S(1)}, bf16[768,128]{1,0:T(8,128)(2,1)S(1)}, u32[]{:S(2)}, u32[]{:S(2)}) collective-permute-start(bf16[768,128]{1,0:T(8,128)(2,1)S(1)} %get-tuple-element.59.rest_1_), channel_id=1, source_target_pairs={{0,3},{1,2},{2,1},{3,0},{4,7},{5,6},{6,5},{7,4},{8,11},{9,10},{10,... | collective-permute-start | bytes 589832 | tf_op jit(solution)/shard_map/ppermute | solution.py:557
  3.7 0.0 collective-permute-start.1
  3.7 4.0 %block_states.1 = (bf16[8,4,128,128]{3,2,1,0:T(8,128)(2,1)S(1)}, bf16[4,128,128]{2,1,0:T(8,128)(2,1)S(1)}) custom-call(bf16[4096,512]{1,0:T(8,128)(2,1)} %k_ref.15, bf16[4096,512]{1,0:T(8,128)(2,1)} %v_ref.15, bf16[768,128]{1,0:T(8,128)(2,1)S(1)} %get-tuple-element.60.rest_0_, bf16[768,128]{1,0:T(8,128)(2,1)S(1)} %get-tuple-element.59.rest_1_), custom_call_target="tpu_custom_call" | custom-call | flops 1024 | bytes 1024 | tf_op jit(solution)/shard_map/block_states/pallas_call | solution.py:61
  7.7 1.6 %collective-permute-start = (bf16[4,128,128]{2,1,0:T(8,128)(2,1)S(1)}, bf16[4,128,128]{2,1,0:T(8,128)(2,1)S(1)}, u32[]{:S(2)}, u32[]{:S(2)}) collective-permute-start(bf16[4,128,128]{2,1,0:T(8,128)(2,1)S(1)} %get-tuple-element.33.rest_0_.total_ref), channel_id=1, source_target_pairs={{0,4},{4,0},{8,12},{12,8},{16,20},{20,16},{24,28},{28,24},{1,5},{5... | collective-permute-start | bytes 393224 | tf_op jit(solution)/shard_map/ppermute | solution.py:557
  9.3 2.1 %early_rows.2 = (bf16[512,128]{1,0:T(8,128)(2,1)S(1)}, bf16[512,128]{1,0:T(8,128)(2,1)S(1)}) custom-call(s32[1]{0:T(128)} %bitcast.head_ref.ids_ref.quarter_ref, bf16[4096,512]{1,0:T(8,128)(2,1)} %q_ref.13, bf16[4096,512]{1,0:T(8,128)(2,1)} %k_ref.15, bf16[4096,512]{1,0:T(8,128)(2,1)} %v_ref.15, bf16[8,4,128,128]{3,2,1,0:T(8,128)(2,1)S(1)} %get-tuple-element.32.within_ref, ...), custom_call_target="tpu_custom_call" | custom-call | flops 1024 | bytes 1024 | tf_op jit(solution)/shard_map/early_rows/pallas_call | solution.py:236
  11.4 1.3 %collective-permute-start.4 = (bf16[512,128]{1,0:T(8,128)(2,1)S(1)}, bf16[512,128]{1,0:T(8,128)(2,1)S(1)}, u32[]{:S(2)}, u32[]{:S(2)}) collective-permute-start(bf16[512,128]{1,0:T(8,128)(2,1)S(1)} %get-tuple-element.34.rest_0_), channel_id=1, source_target_pairs={{0,2},{1,3},{2,0},{3,1},{4,6},{5,7},{6,4},{7,5},{8,10},{9,11},{10,... | collective-permute-start | bytes 393224 | tf_op jit(solution)/shard_map/ppermute | solution.py:557
  12.7 0.9 %collective-permute-start.5 = (bf16[512,128]{1,0:T(8,128)(2,1)S(1)}, bf16[512,128]{1,0:T(8,128)(2,1)S(1)}, u32[]{:S(2)}, u32[]{:S(2)}) collective-permute-start(bf16[512,128]{1,0:T(8,128)(2,1)S(1)} %get-tuple-element.35.rest_1_), channel_id=1, source_target_pairs={{0,3},{1,2},{2,1},{3,0},{4,7},{5,6},{6,5},{7,4},{8,11},{9,10},{10,... | collective-permute-start | bytes 393224 | tf_op jit(solution)/shard_map/ppermute | solution.py:557
  13.6 0.0 collective-permute-done.1.rest_2_.refs_4_
  13.6 0.1 add_step.2
  13.7 1.4 %collective-permute-start.3 = (bf16[4,128,128]{2,1,0:T(8,128)(2,1)S(1)}, bf16[4,128,128]{2,1,0:T(8,128)(2,1)S(1)}, u32[]{:S(2)}, u32[]{:S(2)}) collective-permute-start(bf16[4,128,128]{2,1,0:T(8,128)(2,1)S(1)} %get-tuple-element.36.rest_1_.total_ref), channel_id=1, source_target_pairs={{0,8},{4,12},{8,0},{12,4},{16,24},{20,28},{24,16},{28,20},{1,9},{5... | collective-permute-start | bytes 393224 | tf_op jit(solution)/shard_map/ppermute | solution.py:557
  15.0 2.2 %early_rows.3 = (bf16[768,128]{1,0:T(8,128)(2,1)S(1)}, bf16[768,128]{1,0:T(8,128)(2,1)S(1)}) custom-call(s32[1]{0:T(128)} %bitcast.head_ref.ids_ref.quarter_ref, bf16[4096,512]{1,0:T(8,128)(2,1)} %q_ref.13, bf16[4096,512]{1,0:T(8,128)(2,1)} %k_ref.15, bf16[4096,512]{1,0:T(8,128)(2,1)} %v_ref.15, bf16[8,4,128,128]{3,2,1,0:T(8,128)(2,1)S(1)} %get-tuple-element.32.within_ref, ...), custom_call_target="tpu_custom_call" | custom-call | flops 1024 | bytes 1024 | tf_op jit(solution)/shard_map/early_rows/pallas_call | solution.py:236
  17.2 1.3 %collective-permute-start.7 = (bf16[768,128]{1,0:T(8,128)(2,1)S(1)}, bf16[768,128]{1,0:T(8,128)(2,1)S(1)}, u32[]{:S(2)}, u32[]{:S(2)}) collective-permute-start(bf16[768,128]{1,0:T(8,128)(2,1)S(1)} %get-tuple-element.38.rest_1_), channel_id=1, source_target_pairs={{0,2},{1,3},{2,0},{3,1},{4,6},{5,7},{6,4},{7,5},{8,10},{9,11},{10,... | collective-permute-start | bytes 589832 | tf_op jit(solution)/shard_map/ppermute | solution.py:557
  18.5 1.1 %collective-permute-start.8 = (bf16[768,128]{1,0:T(8,128)(2,1)S(1)}, bf16[768,128]{1,0:T(8,128)(2,1)S(1)}, u32[]{:S(2)}, u32[]{:S(2)}) collective-permute-start(bf16[768,128]{1,0:T(8,128)(2,1)S(1)} %get-tuple-element.39.rest_2_), channel_id=1, source_target_pairs={{0,3},{1,2},{2,1},{3,0},{4,7},{5,6},{6,5},{7,4},{8,11},{9,10},{10,... | collective-permute-start | bytes 589832 | tf_op jit(solution)/shard_map/ppermute | solution.py:557
  19.6 0.0 collective-permute-done.3.got_ref
  19.6 0.1 add_step.3
  19.7 2.4 %collective-permute-start.6 = (bf16[4,128,128]{2,1,0:T(8,128)(2,1)S(1)}, bf16[4,128,128]{2,1,0:T(8,128)(2,1)S(1)}, u32[]{:S(2)}, u32[]{:S(2)}) collective-permute-start(bf16[4,128,128]{2,1,0:T(8,128)(2,1)S(1)} %get-tuple-element.40.rest_0_), channel_id=1, source_target_pairs={{0,16},{4,20},{8,24},{12,28},{16,0},{20,4},{24,8},{28,12},{1,17},{... | collective-permute-start | bytes 393224 | tf_op jit(solution)/shard_map/ppermute | solution.py:557
  22.1 2.5 %attention_rows.3 = (f32[256,384]{1,0:T(8,128)S(1)}, f32[256,384]{1,0:T(8,128)S(1)}, bf16[256,384]{1,0:T(8,128)(2,1)S(1)}, bf16[256,384]{1,0:T(8,128)(2,1)S(1)}) custom-call(s32[1]{0:T(128)} %bitcast.head_ref.ids_ref.quarter_ref, bf16[4096,512]{1,0:T(8,128)(2,1)} %q_ref.13, bf16[4096,512]{1,0:T(8,128)(2,1)} %k_ref.15, bf16[4096,512]{1,0:T(8,128)(2,1)} %v_ref.15, ...), custom_call_target="tpu_custom_call" | custom-call | flops 1024 | bytes 1024 | tf_op jit(solution)/shard_map/attention_rows/pallas_call | solution.py:161
  24.5 3.7 %attention_rows.4 = (bf16[512,384]{1,0:T(8,128)(2,1)S(1)}, bf16[512,384]{1,0:T(8,128)(2,1)S(1)}) custom-call(s32[1]{0:T(128)} %bitcast.head_ref.ids_ref.quarter_ref, bf16[4096,512]{1,0:T(8,128)(2,1)} %q_ref.13, bf16[4096,512]{1,0:T(8,128)(2,1)} %k_ref.15, bf16[4096,512]{1,0:T(8,128)(2,1)} %v_ref.15, ...), custom_call_target="tpu_custom_call" | custom-call | flops 1024 | bytes 1024 | tf_op jit(solution)/shard_map/attention_rows/pallas_call | solution.py:161
  28.2 0.0 collective-permute-done.7.refs_7_.refs_2_
  28.2 0.1 collective-permute-done.8.refs_8_.refs_3_
  28.4 0.1 collective-permute-done.6.refs_6_
  28.5 0.3 late_rows.2
  28.8 0.1 copy-done
  28.9 1.2 %collective-permute-start.10 = (bf16[304,384]{1,0:T(8,128)(2,1)S(1)}, bf16[304,384]{1,0:T(8,128)(2,1)S(1)}, u32[]{:S(2)}, u32[]{:S(2)}) collective-permute-start(bf16[304,384]{1,0:T(8,128)(2,1)S(1)} %get-tuple-element.49.refs_5_), channel_id=1, source_target_pairs={{0,2},{1,3},{2,0},{3,1},{4,6},{5,7},{6,4},{7,5},{8,10},{9,11},{10,... | collective-permute-start | bytes 700424 | tf_op jit(solution)/shard_map/ppermute | solution.py:557
  30.1 1.2 %collective-permute-start.12 = (bf16[256,384]{1,0:T(8,128)(2,1)S(1)}, bf16[256,384]{1,0:T(8,128)(2,1)S(1)}, u32[]{:S(2)}, u32[]{:S(2)}) collective-permute-start(bf16[256,384]{1,0:T(8,128)(2,1)S(1)} %get-tuple-element.50.refs_6_), channel_id=1, source_target_pairs={{0,3},{1,2},{2,1},{3,0},{4,7},{5,6},{6,5},{7,4},{8,11},{9,10},{10,... | collective-permute-start | bytes 589832 | tf_op jit(solution)/shard_map/ppermute | solution.py:557
  31.3 2.3 %late_rows.3 = (bf16[512,384]{1,0:T(8,128)(2,1)}, bf16[512,384]{1,0:T(8,128)(2,1)}) custom-call(s32[1]{0:T(128)} %bitcast.head_ref.ids_ref.quarter_ref, bf16[4096,512]{1,0:T(8,128)(2,1)} %q_ref.13, bf16[512,384]{1,0:T(8,128)(2,1)S(1)} %get-tuple-element.46.refs_9_.refs_1_, bf16[4096,512]{1,0:T(8,128)(2,1)} %q_ref.13, ...), custom_call_target="tpu_custom_call" | custom-call | flops 1024 | bytes 1024 | tf_op jit(solution)/shard_map/late_rows/pallas_call | solution.py:301
  33.6 1.2 %collective-permute-start.17 = (bf16[512,384]{1,0:T(8,128)(2,1)}, bf16[512,384]{1,0:T(8,128)(2,1)}, u32[]{:S(2)}, u32[]{:S(2)}) collective-permute-start(bf16[512,384]{1,0:T(8,128)(2,1)} %get-tuple-element.51.rest_1_), channel_id=1, source_target_pairs={{0,2},{1,3},{2,0},{3,1},{4,6},{5,7},{6,4},{7,5},{8,10},{9,11},{10,... | collective-permute-start | bytes 1179656 | tf_op jit(solution)/shard_map/ppermute | solution.py:557
  34.9 5.2 %attention_quarter.2.rest_1_ = bf16[1024,512]{1,0:T(8,128)(2,1)} custom-call(s32[1]{0:T(128)} %bitcast.head_ref.ids_ref.quarter_ref, bf16[4096,512]{1,0:T(8,128)(2,1)} %q_ref.13, bf16[4096,512]{1,0:T(8,128)(2,1)} %k_ref.15, bf16[4096,512]{1,0:T(8,128)(2,1)} %v_ref.15, bf16[8,4,128,128]{3,2,1,0:T(8,128)(2,1)S(1)} %get-tuple-element.32.within_ref, ...), custom_call_target="tpu_custom_call" | custom-call | flops 1024 | bytes 1024 | tf_op jit(solution)/shard_map/attention_quarter/pallas_call | solution.py:195
  40.1 0.3 collective-permute-start.18
  40.4 4.4 %attention_quarter.3.own_ref.rest_1_.refs_1_ = bf16[1024,512]{1,0:T(8,128)(2,1)S(1)} custom-call(s32[1]{0:T(128)} %bitcast.head_ref.ids_ref.quarter_ref, bf16[4096,512]{1,0:T(8,128)(2,1)} %q_ref.13, bf16[4096,512]{1,0:T(8,128)(2,1)} %k_ref.15, bf16[4096,512]{1,0:T(8,128)(2,1)} %v_ref.15, bf16[8,4,128,128]{3,2,1,0:T(8,128)(2,1)S(1)} %get-tuple-element.32.within_ref, ...), custom_call_target="tpu_custom_call" | custom-call | flops 1024 | bytes 1024 | tf_op jit(solution)/shard_map/attention_quarter/pallas_call | solution.py:195
  44.8 0.4 collective-permute-start.9
  45.2 0.0 collective-permute-done.10.rest_2_.x2_ref
  45.2 0.6 slice.4.refs_6_
  45.8 0.2 collective-permute-start.11
  46.0 3.3 %attention_rows.5 = (bf16[128,384]{1,0:T(8,128)(2,1)S(1)}, bf16[128,384]{1,0:T(8,128)(2,1)S(1)}, bf16[128,384]{1,0:T(8,128)(2,1)S(1)}, bf16[128,384]{1,0:T(8,128)(2,1)S(1)}) custom-call(s32[1]{0:T(128)} %bitcast.head_ref.ids_ref.quarter_ref, bf16[4096,512]{1,0:T(8,128)(2,1)} %q_ref.13, bf16[4096,512]{1,0:T(8,128)(2,1)} %k_ref.15, bf16[4096,512]{1,0:T(8,128)(2,1)} %v_ref.15, ...), custom_call_target="tpu_custom_call" | custom-call | flops 999999995904 | bytes 1024 | tf_op jit(solution)/shard_map/attention_rows/pallas_call | solution.py:161
  49.3 1.1 %collective-permute-start.13 = (bf16[128,384]{1,0:T(8,128)(2,1)S(1)}, bf16[128,384]{1,0:T(8,128)(2,1)S(1)}, u32[]{:S(2)}, u32[]{:S(2)}) collective-permute-start(bf16[128,384]{1,0:T(8,128)(2,1)S(1)} %get-tuple-element.55), channel_id=1, source_target_pairs={{0,2},{1,3},{2,0},{3,1},{4,6},{5,7},{6,4},{7,5},{8,10},{9,11},{10,... | collective-permute-start | bytes 294920 | tf_op jit(solution)/shard_map/ppermute | solution.py:557
  50.4 0.4 collective-permute-start.15
  50.8 2.0 %collective-permute-start.16 = (bf16[128,384]{1,0:T(8,128)(2,1)S(1)}, bf16[128,384]{1,0:T(8,128)(2,1)S(1)}, u32[]{:S(2)}, u32[]{:S(2)}) collective-permute-start(bf16[128,384]{1,0:T(8,128)(2,1)S(1)} %get-tuple-element.58), channel_id=1, source_target_pairs={{0,3},{1,2},{2,1},{3,0},{4,7},{5,6},{6,5},{7,4},{8,11},{9,10},{10,... | collective-permute-start | bytes 294920 | tf_op jit(solution)/shard_map/ppermute | solution.py:557
  52.8 0.1 collective-permute-start.14
  52.9 1.1 %early_out.1 = (bf16[1024,128]{1,0:T(8,128)(2,1)S(1)}, bf16[1024,128]{1,0:T(8,128)(2,1)S(1)}) custom-call(bf16[512,128]{1,0:T(8,128)(2,1)S(1)} %collective-permute-done.4.rest_3_.refs_0_, bf16[512,128]{1,0:T(8,128)(2,1)S(1)} %collective-permute-done.5.rest_4_.refs_1_, bf16[768,128]{1,0:T(8,128)(2,1)S(1)} %copy-done.1, bf16[768,128]{1,0:T(8,128)(2,1)S(1)} %copy-done.3, ...), custom_call_target="tpu_custom_call" | custom-call | flops 1024 | bytes 1024 | tf_op jit(solution)/shard_map/early_out/pallas_call | solution.py:345
  54.0 0.9 %gather_rows.1.near_ref = bf16[128,1280]{1,0:T(8,128)(2,1)S(1)} custom-call(bf16[1024,512]{1,0:T(8,128)(2,1)S(1)} %attention_quarter.3.own_ref.rest_1_.refs_1_, bf16[1024,512]{1,0:T(8,128)(2,1)} %collective-permute-done.9.mate_ref.refs_2_, bf16[1024,128]{1,0:T(8,128)(2,1)S(1)} %get-tuple-element.53.o2_ref.refs_4_, ...), custom_call_target="tpu_custom_call" | custom-call | flops 1024 | bytes 1024 | tf_op jit(solution)/shard_map/gather_rows/pallas_call | solution.py:370
  54.9 2.3 %norm_rows.2.refs_7_ = bf16[1024,2048]{1,0:T(8,128)(2,1)} custom-call(s32[1]{0:T(128)} %bitcast.head_ref.ids_ref.quarter_ref, f32[1,2048]{1,0:T(1,128)S(1)} %bitcast.3, bf16[1024,512]{1,0:T(8,128)(2,1)S(1)} %attention_quarter.3.own_ref.rest_1_.refs_1_, bf16[1024,512]{1,0:T(8,128)(2,1)} %collective-permute-done.9.mate_ref.refs_2_, ...), custom_call_target="tpu_custom_call" | custom-call | flops 1024 | bytes 1024 | tf_op jit(solution)/shard_map/norm_rows/pallas_call | solution.py:445
  57.2 1.6 %collective-permute-done.18.refs_5_ = bf16[512,384]{1,0:T(8,128)(2,1)} collective-permute-done((bf16[512,384]{1,0:T(8,128)(2,1)}, bf16[512,384]{1,0:T(8,128)(2,1)}, u32[]{:S(2)}, u32[]{:S(2)}) %collective-permute-start.18) | collective-permute-done | bytes 393248 | tf_op jit(solution)/shard_map/ppermute | solution.py:557
  58.8 3.3 %norm_block.1.rest_0_ = bf16[1024,2048]{1,0:T(8,128)(2,1)} custom-call(s32[1]{0:T(128)} %bitcast.head_ref.ids_ref.quarter_ref, f32[1,2048]{1,0:T(1,128)S(1)} %bitcast.4, bf16[1024,512]{1,0:T(8,128)(2,1)S(1)} %attention_quarter.3.own_ref.rest_1_.refs_1_, bf16[1024,512]{1,0:T(8,128)(2,1)} %collective-permute-done.9.mate_ref.refs_2_, ...), custom_call_target="tpu_custom_call", output_to_operand_aliasing={{}: (8, {})} | custom-call | flops 1024 | bytes 1024 | tf_op jit(solution)/shard_map/norm_block/pallas_call | solution.py:508
  62.1 2.7 %collective-permute-done.16.x3_ref = bf16[128,384]{1,0:T(8,128)(2,1)S(1)} collective-permute-done((bf16[128,384]{1,0:T(8,128)(2,1)S(1)}, bf16[128,384]{1,0:T(8,128)(2,1)S(1)}, u32[]{:S(2)}, u32[]{:S(2)}) %collective-permute-start.16) | collective-permute-done | bytes 98336 | tf_op jit(solution)/shard_map/ppermute | solution.py:557
  64.8 2.0 %norm_rows.3.old_ref = bf16[1024,2048]{1,0:T(8,128)(2,1)} custom-call(s32[1]{0:T(128)} %bitcast.head_ref.ids_ref.quarter_ref, f32[1,2048]{1,0:T(1,128)S(1)} %bitcast.5, bf16[1024,512]{1,0:T(8,128)(2,1)S(1)} %attention_quarter.3.own_ref.rest_1_.refs_1_, bf16[1024,512]{1,0:T(8,128)(2,1)} %collective-permute-done.9.mate_ref.refs_2_, ...), custom_call_target="tpu_custom_call", output_to_operand_aliasing={{}: (8, {})} | custom-call | flops 1024 | bytes 1024 | tf_op jit(solution)/shard_map/norm_rows/pallas_call | solution.py:445
  66.8 1.1 %norm_last.1 = bf16[1024,2048]{1,0:T(8,128)(2,1)} custom-call(s32[1]{0:T(128)} %bitcast.head_ref.ids_ref.quarter_ref, f32[1,2048]{1,0:T(1,128)S(1)} %bitcast.6, bf16[128,1280]{1,0:T(8,128)(2,1)S(1)} %gather_rows.1.near_ref, bf16[128,384]{1,0:T(8,128)(2,1)S(1)} %collective-permute-done.13.x2_ref, ...), custom_call_target="tpu_custom_call", output_to_operand_aliasing={{}: (5, {})} | custom-call | flops 1024 | bytes 1024 | tf_op jit(solution)/shard_map/norm_last/pallas_call | solution.py:393
  (20 shorter events, 0.0 us)
Async XLA Ops:
  1.1 12.5 %collective-permute-start.2 = (bf16[768,128]{1,0:T(8,128)(2,1)S(1)}, bf16[768,128]{1,0:T(8,128)(2,1)S(1)}, u32[]{:S(2)}, u32[]{:S(2)}) collective-permute-start(bf16[768,128]{1,0:T(8,128)(2,1)S(1)} %get-tuple-element.59.rest_1_), channel_id=1, source_target_pairs={{0,3},{1,2},{2,1},{3,0},{4,7},{5,6},{6,5},{7,4},{8,11},{9,10},{10,... | collective-permute-start | bytes 589832 | tf_op jit(solution)/shard_map/ppermute | solution.py:557
  3.7 9.9 %collective-permute-start.1 = (bf16[768,128]{1,0:T(8,128)(2,1)S(1)}, bf16[768,128]{1,0:T(8,128)(2,1)S(1)}, u32[]{:S(2)}, u32[]{:S(2)}) collective-permute-start(bf16[768,128]{1,0:T(8,128)(2,1)S(1)} %get-tuple-element.60.rest_0_), channel_id=1, source_target_pairs={{0,2},{1,3},{2,0},{3,1},{4,6},{5,7},{6,4},{7,5},{8,10},{9,11},{10,... | collective-permute-start | bytes 589832 | tf_op jit(solution)/shard_map/ppermute | solution.py:557
  7.7 5.9 %collective-permute-start = (bf16[4,128,128]{2,1,0:T(8,128)(2,1)S(1)}, bf16[4,128,128]{2,1,0:T(8,128)(2,1)S(1)}, u32[]{:S(2)}, u32[]{:S(2)}) collective-permute-start(bf16[4,128,128]{2,1,0:T(8,128)(2,1)S(1)} %get-tuple-element.33.rest_0_.total_ref), channel_id=1, source_target_pairs={{0,4},{4,0},{8,12},{12,8},{16,20},{20,16},{24,28},{28,24},{1,5},{5... | collective-permute-start | bytes 393224 | tf_op jit(solution)/shard_map/ppermute | solution.py:557
  11.4 8.2 %collective-permute-start.4 = (bf16[512,128]{1,0:T(8,128)(2,1)S(1)}, bf16[512,128]{1,0:T(8,128)(2,1)S(1)}, u32[]{:S(2)}, u32[]{:S(2)}) collective-permute-start(bf16[512,128]{1,0:T(8,128)(2,1)S(1)} %get-tuple-element.34.rest_0_), channel_id=1, source_target_pairs={{0,2},{1,3},{2,0},{3,1},{4,6},{5,7},{6,4},{7,5},{8,10},{9,11},{10,... | collective-permute-start | bytes 393224 | tf_op jit(solution)/shard_map/ppermute | solution.py:557
  12.7 6.9 %collective-permute-start.5 = (bf16[512,128]{1,0:T(8,128)(2,1)S(1)}, bf16[512,128]{1,0:T(8,128)(2,1)S(1)}, u32[]{:S(2)}, u32[]{:S(2)}) collective-permute-start(bf16[512,128]{1,0:T(8,128)(2,1)S(1)} %get-tuple-element.35.rest_1_), channel_id=1, source_target_pairs={{0,3},{1,2},{2,1},{3,0},{4,7},{5,6},{6,5},{7,4},{8,11},{9,10},{10,... | collective-permute-start | bytes 393224 | tf_op jit(solution)/shard_map/ppermute | solution.py:557
  13.7 5.9 %collective-permute-start.3 = (bf16[4,128,128]{2,1,0:T(8,128)(2,1)S(1)}, bf16[4,128,128]{2,1,0:T(8,128)(2,1)S(1)}, u32[]{:S(2)}, u32[]{:S(2)}) collective-permute-start(bf16[4,128,128]{2,1,0:T(8,128)(2,1)S(1)} %get-tuple-element.36.rest_1_.total_ref), channel_id=1, source_target_pairs={{0,8},{4,12},{8,0},{12,4},{16,24},{20,28},{24,16},{28,20},{1,9},{5... | collective-permute-start | bytes 393224 | tf_op jit(solution)/shard_map/ppermute | solution.py:557
  17.2 11.0 %collective-permute-start.7 = (bf16[768,128]{1,0:T(8,128)(2,1)S(1)}, bf16[768,128]{1,0:T(8,128)(2,1)S(1)}, u32[]{:S(2)}, u32[]{:S(2)}) collective-permute-start(bf16[768,128]{1,0:T(8,128)(2,1)S(1)} %get-tuple-element.38.rest_1_), channel_id=1, source_target_pairs={{0,2},{1,3},{2,0},{3,1},{4,6},{5,7},{6,4},{7,5},{8,10},{9,11},{10,... | collective-permute-start | bytes 589832 | tf_op jit(solution)/shard_map/ppermute | solution.py:557
  18.5 9.9 %collective-permute-start.8 = (bf16[768,128]{1,0:T(8,128)(2,1)S(1)}, bf16[768,128]{1,0:T(8,128)(2,1)S(1)}, u32[]{:S(2)}, u32[]{:S(2)}) collective-permute-start(bf16[768,128]{1,0:T(8,128)(2,1)S(1)} %get-tuple-element.39.rest_2_), channel_id=1, source_target_pairs={{0,3},{1,2},{2,1},{3,0},{4,7},{5,6},{6,5},{7,4},{8,11},{9,10},{10,... | collective-permute-start | bytes 589832 | tf_op jit(solution)/shard_map/ppermute | solution.py:557
  19.7 8.9 %collective-permute-start.6 = (bf16[4,128,128]{2,1,0:T(8,128)(2,1)S(1)}, bf16[4,128,128]{2,1,0:T(8,128)(2,1)S(1)}, u32[]{:S(2)}, u32[]{:S(2)}) collective-permute-start(bf16[4,128,128]{2,1,0:T(8,128)(2,1)S(1)} %get-tuple-element.40.rest_0_), channel_id=1, source_target_pairs={{0,16},{4,20},{8,24},{12,28},{16,0},{20,4},{24,8},{28,12},{1,17},{... | collective-permute-start | bytes 393224 | tf_op jit(solution)/shard_map/ppermute | solution.py:557
  28.2 0.7 %copy-start = (bf16[768,128]{1,0:T(8,128)(2,1)}, bf16[768,128]{1,0:T(8,128)(2,1)S(1)}, u32[]{:S(2)}) copy-start(bf16[768,128]{1,0:T(8,128)(2,1)S(1)} %collective-permute-done.7.refs_7_.refs_2_) | copy-start | bytes 589828
  28.4 5.3 %copy-start.2 = (bf16[768,128]{1,0:T(8,128)(2,1)}, bf16[768,128]{1,0:T(8,128)(2,1)S(1)}, u32[]{:S(2)}) copy-start(bf16[768,128]{1,0:T(8,128)(2,1)S(1)} %collective-permute-done.8.refs_8_.refs_3_) | copy-start | bytes 589828
  28.9 16.3 %collective-permute-start.10 = (bf16[304,384]{1,0:T(8,128)(2,1)S(1)}, bf16[304,384]{1,0:T(8,128)(2,1)S(1)}, u32[]{:S(2)}, u32[]{:S(2)}) collective-permute-start(bf16[304,384]{1,0:T(8,128)(2,1)S(1)} %get-tuple-element.49.refs_5_), channel_id=1, source_target_pairs={{0,2},{1,3},{2,0},{3,1},{4,6},{5,7},{6,4},{7,5},{8,10},{9,11},{10,... | collective-permute-start | bytes 700424 | tf_op jit(solution)/shard_map/ppermute | solution.py:557
  30.1 15.8 %collective-permute-start.12 = (bf16[256,384]{1,0:T(8,128)(2,1)S(1)}, bf16[256,384]{1,0:T(8,128)(2,1)S(1)}, u32[]{:S(2)}, u32[]{:S(2)}) collective-permute-start(bf16[256,384]{1,0:T(8,128)(2,1)S(1)} %get-tuple-element.50.refs_6_), channel_id=1, source_target_pairs={{0,3},{1,2},{2,1},{3,0},{4,7},{5,6},{6,5},{7,4},{8,11},{9,10},{10,... | collective-permute-start | bytes 589832 | tf_op jit(solution)/shard_map/ppermute | solution.py:557
  33.6 17.2 %collective-permute-start.17 = (bf16[512,384]{1,0:T(8,128)(2,1)}, bf16[512,384]{1,0:T(8,128)(2,1)}, u32[]{:S(2)}, u32[]{:S(2)}) collective-permute-start(bf16[512,384]{1,0:T(8,128)(2,1)} %get-tuple-element.51.rest_1_), channel_id=1, source_target_pairs={{0,2},{1,3},{2,0},{3,1},{4,6},{5,7},{6,4},{7,5},{8,10},{9,11},{10,... | collective-permute-start | bytes 1179656 | tf_op jit(solution)/shard_map/ppermute | solution.py:557
  40.1 18.7 %collective-permute-start.18 = (bf16[512,384]{1,0:T(8,128)(2,1)}, bf16[512,384]{1,0:T(8,128)(2,1)}, u32[]{:S(2)}, u32[]{:S(2)}) collective-permute-start(bf16[512,384]{1,0:T(8,128)(2,1)} %get-tuple-element.52.rest_2_), channel_id=1, source_target_pairs={{0,3},{1,2},{2,1},{3,0},{4,7},{5,6},{6,5},{7,4},{8,11},{9,10},{10,... | collective-permute-start | bytes 1179656 | tf_op jit(solution)/shard_map/ppermute | solution.py:557
  44.8 8.0 %collective-permute-start.9 = (bf16[1024,512]{1,0:T(8,128)(2,1)}, bf16[1024,512]{1,0:T(8,128)(2,1)}, u32[]{:S(2)}, u32[]{:S(2)}) collective-permute-start(bf16[1024,512]{1,0:T(8,128)(2,1)} %attention_quarter.2.rest_1_), channel_id=1, source_target_pairs={{0,1},{1,0},{2,3},{3,2},{4,5},{5,4},{6,7},{7,6},{8,9},{9,8},{10,11... | collective-permute-start | bytes 3145736 | tf_op jit(solution)/shard_map/ppermute | solution.py:557
  45.8 4.6 %collective-permute-start.11 = (bf16[48,384]{1,0:T(8,128)(2,1)}, bf16[48,384]{1,0:T(8,128)(2,1)}, u32[]{:S(2)}, u32[]{:S(2)}) collective-permute-start(bf16[48,384]{1,0:T(8,128)(2,1)} %slice.4.refs_6_), channel_id=1, source_target_pairs={{0,1},{1,0},{2,3},{3,2},{4,5},{5,4},{6,7},{7,6},{8,9},{9,8},{10,11... | collective-permute-start | bytes 110600 | tf_op jit(solution)/shard_map/ppermute | solution.py:557
  46.0 6.9 %copy-start.1 = (bf16[768,128]{1,0:T(8,128)(2,1)S(1)}, bf16[768,128]{1,0:T(8,128)(2,1)}, u32[]{:S(2)}) copy-start(bf16[768,128]{1,0:T(8,128)(2,1)} %copy-done) | copy-start | bytes 589828
  46.0 6.9 %copy-start.3 = (bf16[768,128]{1,0:T(8,128)(2,1)S(1)}, bf16[768,128]{1,0:T(8,128)(2,1)}, u32[]{:S(2)}) copy-start(bf16[768,128]{1,0:T(8,128)(2,1)} %copy-done.2) | copy-start | bytes 589828
  46.0 8.9 %copy-start.4 = (f32[2048]{0:T(1024)S(1)}, f32[2048]{0:T(1024)}, u32[]{:S(2)}) copy-start(f32[2048]{0:T(1024)} %param.7) | copy-start | bytes 24580
  49.3 17.5 %collective-permute-start.13 = (bf16[128,384]{1,0:T(8,128)(2,1)S(1)}, bf16[128,384]{1,0:T(8,128)(2,1)S(1)}, u32[]{:S(2)}, u32[]{:S(2)}) collective-permute-start(bf16[128,384]{1,0:T(8,128)(2,1)S(1)} %get-tuple-element.55), channel_id=1, source_target_pairs={{0,2},{1,3},{2,0},{3,1},{4,6},{5,7},{6,4},{7,5},{8,10},{9,11},{10,... | collective-permute-start | bytes 294920 | tf_op jit(solution)/shard_map/ppermute | solution.py:557
  50.4 11.7 %collective-permute-start.15 = (bf16[128,384]{1,0:T(8,128)(2,1)S(1)}, bf16[128,384]{1,0:T(8,128)(2,1)S(1)}, u32[]{:S(2)}, u32[]{:S(2)}) collective-permute-start(bf16[128,384]{1,0:T(8,128)(2,1)S(1)} %get-tuple-element.57), channel_id=1, source_target_pairs={{0,2},{1,3},{2,0},{3,1},{4,6},{5,7},{6,4},{7,5},{8,10},{9,11},{10,... | collective-permute-start | bytes 294920 | tf_op jit(solution)/shard_map/ppermute | solution.py:557
  50.8 14.0 %collective-permute-start.16 = (bf16[128,384]{1,0:T(8,128)(2,1)S(1)}, bf16[128,384]{1,0:T(8,128)(2,1)S(1)}, u32[]{:S(2)}, u32[]{:S(2)}) collective-permute-start(bf16[128,384]{1,0:T(8,128)(2,1)S(1)} %get-tuple-element.58), channel_id=1, source_target_pairs={{0,3},{1,2},{2,1},{3,0},{4,7},{5,6},{6,5},{7,4},{8,11},{9,10},{10,... | collective-permute-start | bytes 294920 | tf_op jit(solution)/shard_map/ppermute | solution.py:557
  52.8 14.0 %collective-permute-start.14 = (bf16[128,384]{1,0:T(8,128)(2,1)S(1)}, bf16[128,384]{1,0:T(8,128)(2,1)S(1)}, u32[]{:S(2)}, u32[]{:S(2)}) collective-permute-start(bf16[128,384]{1,0:T(8,128)(2,1)S(1)} %get-tuple-element.56), channel_id=1, source_target_pairs={{0,3},{1,2},{2,1},{3,0},{4,7},{5,6},{6,5},{7,4},{8,11},{9,10},{10,... | collective-permute-start | bytes 294920 | tf_op jit(solution)/shard_map/ppermute | solution.py:557

commit v7 on v6

--- a/solution.py
+++ b/solution.py
@@ -589,7 +589,7 @@
             first = attention_rows(
                 arrays, None, at, far, BLK, HALF, 0, heads - 1, jnp.float32, [group], keep=True
             )
-            second = attention_rows(arrays, None, at, far, 0, BLK, 0, heads - 1, jnp.bfloat16, first)
+            second = attention_rows(arrays, None, at, far[:1], 0, BLK, 0, heads - 1, jnp.bfloat16, first)
             tokens = [*first, *second]
         if bit * 2 < seq_size:
             group, before = add_step(mine, bit, group, got, before, tokens)
@@ -602,7 +602,8 @@
         at, first[2:], first[:2], before, heads - 1, True, [*early_l[1], *second], (mine, bit // 2, got)
     )
     x1 = across(one)
-    two = late_rows(at, [(queries, k) for k in far], second, before, heads - 1, False, one, None)
+    two = late_rows(at, [(queries, far[0])], second, before, heads - 1, False, one, None)
+    two += attention_rows(arrays, before, at, far[1:], 0, BLK, 0, heads - 1, jnp.bfloat16, two)
     x2 = across(two)
     mate = attention_quarter(arrays, before, at, 1, jnp.bfloat16, two)
     mated = swap(mate, "head", 4, 1)

time: 68.3 us -> 68.7 us (level)
  Pallas kernels: 40.6 us -> 42.2 us
  waiting for transfers between devices: 4.64 us -> 3.05 us
    pallas_call x3 -> x4, Pallas kernels: 9.42 us -> 11.3 us  [attention_rows(): pl.pallas_call(kernel, grid_spec=pltpu.PrefetchScalarGridSpec(num_scalar_...]
    ppermute x19, waiting for transfers between devices: 4.64 us -> 3.05 us  [swap(): return lax.ppermute(x, axis, [(i, i ^ bit) for i in range(size)])]
  transfers between devices with their start and end apart: 19 -> 19, of which waited for: 4 -> 3; matrix products, arithmetic and copies ran while one was open for 1% -> 1% of each run, Pallas kernels for 58% -> 60%
where the time goes in v7:
time: 68.7 us; the launch traced here: 68.2 us
  Pallas kernels  42.2 us (61%)
  starting transfers between devices  20.8 us (30%)
  waiting for transfers between devices  3.05 us (4%)
  local copies, waits for them, and re-layouts  1.94 us (3%)
    ppermute x19, starting transfers between devices, swap(): return lax.ppermute(x, axis, [(i, i ^ bit) for i in range(size)])  20.8 us
    pallas_call x4, Pallas kernels, attention_rows(): pl.pallas_call(kernel, grid_spec=pltpu.PrefetchScalarGridSpec(num_scalar_...  11.3 us
    pallas_call x2, Pallas kernels, attention_quarter(): pl.pallas_call(kernel, grid_spec=pltpu.PrefetchScalarGridSpec(num_scalar_...  9.61 us
    pallas_call x2, Pallas kernels, early_rows(): pl.pallas_call(functools.partial(early_kernel, tail), grid_spec=pltpu.Pre...  4.28 us
    pallas_call x2, Pallas kernels, norm_rows(): pl.pallas_call(norm_kernel, grid_spec=pltpu.PrefetchScalarGridSpec(num_sc...  4.24 us
    pallas_call x1, Pallas kernels, block_states(): pl.pallas_call(functools.partial(state_kernel, parts, len(tokens)), in_sp...  3.97 us
    pallas_call x1, Pallas kernels, norm_block(): pl.pallas_call(functools.partial(norm_block_kernel, row, size, places, wi...  3.33 us
    ppermute x19, waiting for transfers between devices, swap(): return lax.ppermute(x, axis, [(i, i ^ bit) for i in range(size)])  3.05 us
  transfers between devices with their start and end apart: 19, of which 3 were waited for; matrix products, arithmetic and copies ran while one was open for 1% of the time, Pallas kernels for 60%

profile of v7, /device:TPU:1, one launch (start us, length us, event | category | flops | bytes accessed | tf_op | source)
XLA Modules:
  0.0 68.2 jit_solution(14520297300720046888)
XLA Ops:
  0.0 1.1 %constant_dynamic-slice_fusion = (bf16[768,128]{1,0:T(8,128)(2,1)S(1)}, bf16[768,128]{1,0:T(8,128)(2,1)S(1)}) fusion(bf16[4096,512]{1,0:T(8,128)(2,1)} %q_ref.15, s32[]{:T(128)S(6)} %select_n.7, s32[]{:T(128)S(6)} %select_n.6), kind=kLoop, calls=%fused_computation | loop fusion | bytes 786440 | tf_op jit(solution)/shard_map/dynamic_slice | solution.py:575
  1.1 2.7 %collective-permute-start.2 = (bf16[768,128]{1,0:T(8,128)(2,1)S(1)}, bf16[768,128]{1,0:T(8,128)(2,1)S(1)}, u32[]{:S(2)}, u32[]{:S(2)}) collective-permute-start(bf16[768,128]{1,0:T(8,128)(2,1)S(1)} %get-tuple-element.51.rest_1_), channel_id=1, source_target_pairs={{0,3},{1,2},{2,1},{3,0},{4,7},{5,6},{6,5},{7,4},{8,11},{9,10},{10,... | collective-permute-start | bytes 589832 | tf_op jit(solution)/shard_map/ppermute | solution.py:557
  3.7 4.0 %block_states.1 = (bf16[8,4,128,128]{3,2,1,0:T(8,128)(2,1)S(1)}, bf16[4,128,128]{2,1,0:T(8,128)(2,1)S(1)}) custom-call(bf16[4096,512]{1,0:T(8,128)(2,1)} %k_ref.17, bf16[4096,512]{1,0:T(8,128)(2,1)} %v_ref.17, bf16[768,128]{1,0:T(8,128)(2,1)S(1)} %get-tuple-element.52.rest_0_, bf16[768,128]{1,0:T(8,128)(2,1)S(1)} %get-tuple-element.51.rest_1_), custom_call_target="tpu_custom_call" | custom-call | flops 1024 | bytes 1024 | tf_op jit(solution)/shard_map/block_states/pallas_call | solution.py:61
  7.7 1.6 %collective-permute-start = (bf16[4,128,128]{2,1,0:T(8,128)(2,1)S(1)}, bf16[4,128,128]{2,1,0:T(8,128)(2,1)S(1)}, u32[]{:S(2)}, u32[]{:S(2)}) collective-permute-start(bf16[4,128,128]{2,1,0:T(8,128)(2,1)S(1)} %get-tuple-element.29.rest_0_.total_ref), channel_id=1, source_target_pairs={{0,4},{4,0},{8,12},{12,8},{16,20},{20,16},{24,28},{28,24},{1,5},{5... | collective-permute-start | bytes 393224 | tf_op jit(solution)/shard_map/ppermute | solution.py:557
  9.3 2.1 %early_rows.2 = (bf16[512,128]{1,0:T(8,128)(2,1)S(1)}, bf16[512,128]{1,0:T(8,128)(2,1)S(1)}) custom-call(s32[1]{0:T(128)} %bitcast.head_ref.ids_ref.quarter_ref, bf16[4096,512]{1,0:T(8,128)(2,1)} %q_ref.15, bf16[4096,512]{1,0:T(8,128)(2,1)} %k_ref.17, bf16[4096,512]{1,0:T(8,128)(2,1)} %v_ref.17, bf16[8,4,128,128]{3,2,1,0:T(8,128)(2,1)S(1)} %get-tuple-element.28.within_ref, ...), custom_call_target="tpu_custom_call" | custom-call | flops 1024 | bytes 1024 | tf_op jit(solution)/shard_map/early_rows/pallas_call | solution.py:236
  11.4 1.3 %collective-permute-start.4 = (bf16[512,128]{1,0:T(8,128)(2,1)S(1)}, bf16[512,128]{1,0:T(8,128)(2,1)S(1)}, u32[]{:S(2)}, u32[]{:S(2)}) collective-permute-start(bf16[512,128]{1,0:T(8,128)(2,1)S(1)} %get-tuple-element.30.rest_0_), channel_id=1, source_target_pairs={{0,2},{1,3},{2,0},{3,1},{4,6},{5,7},{6,4},{7,5},{8,10},{9,11},{10,... | collective-permute-start | bytes 393224 | tf_op jit(solution)/shard_map/ppermute | solution.py:557
  12.7 0.9 %collective-permute-start.5 = (bf16[512,128]{1,0:T(8,128)(2,1)S(1)}, bf16[512,128]{1,0:T(8,128)(2,1)S(1)}, u32[]{:S(2)}, u32[]{:S(2)}) collective-permute-start(bf16[512,128]{1,0:T(8,128)(2,1)S(1)} %get-tuple-element.31.rest_1_), channel_id=1, source_target_pairs={{0,3},{1,2},{2,1},{3,0},{4,7},{5,6},{6,5},{7,4},{8,11},{9,10},{10,... | collective-permute-start | bytes 393224 | tf_op jit(solution)/shard_map/ppermute | solution.py:557
  13.6 0.0 collective-permute-done.got_ref
  13.6 0.0 collective-permute-done.2.rest_3_.refs_5_
  13.6 0.0 collective-permute-done.1.rest_2_.refs_4_
  13.6 0.1 add_step.2
  13.7 1.4 %collective-permute-start.3 = (bf16[4,128,128]{2,1,0:T(8,128)(2,1)S(1)}, bf16[4,128,128]{2,1,0:T(8,128)(2,1)S(1)}, u32[]{:S(2)}, u32[]{:S(2)}) collective-permute-start(bf16[4,128,128]{2,1,0:T(8,128)(2,1)S(1)} %get-tuple-element.32.rest_1_.total_ref), channel_id=1, source_target_pairs={{0,8},{4,12},{8,0},{12,4},{16,24},{20,28},{24,16},{28,20},{1,9},{5... | collective-permute-start | bytes 393224 | tf_op jit(solution)/shard_map/ppermute | solution.py:557
  15.0 2.2 %early_rows.3 = (bf16[768,128]{1,0:T(8,128)(2,1)S(1)}, bf16[768,128]{1,0:T(8,128)(2,1)S(1)}) custom-call(s32[1]{0:T(128)} %bitcast.head_ref.ids_ref.quarter_ref, bf16[4096,512]{1,0:T(8,128)(2,1)} %q_ref.15, bf16[4096,512]{1,0:T(8,128)(2,1)} %k_ref.17, bf16[4096,512]{1,0:T(8,128)(2,1)} %v_ref.17, bf16[8,4,128,128]{3,2,1,0:T(8,128)(2,1)S(1)} %get-tuple-element.28.within_ref, ...), custom_call_target="tpu_custom_call" | custom-call | flops 1024 | bytes 1024 | tf_op jit(solution)/shard_map/early_rows/pallas_call | solution.py:236
  17.2 1.3 %collective-permute-start.7 = (bf16[768,128]{1,0:T(8,128)(2,1)S(1)}, bf16[768,128]{1,0:T(8,128)(2,1)S(1)}, u32[]{:S(2)}, u32[]{:S(2)}) collective-permute-start(bf16[768,128]{1,0:T(8,128)(2,1)S(1)} %get-tuple-element.34.rest_1_), channel_id=1, source_target_pairs={{0,2},{1,3},{2,0},{3,1},{4,6},{5,7},{6,4},{7,5},{8,10},{9,11},{10,... | collective-permute-start | bytes 589832 | tf_op jit(solution)/shard_map/ppermute | solution.py:557
  18.5 1.1 %collective-permute-start.8 = (bf16[768,128]{1,0:T(8,128)(2,1)S(1)}, bf16[768,128]{1,0:T(8,128)(2,1)S(1)}, u32[]{:S(2)}, u32[]{:S(2)}) collective-permute-start(bf16[768,128]{1,0:T(8,128)(2,1)S(1)} %get-tuple-element.35.rest_2_), channel_id=1, source_target_pairs={{0,3},{1,2},{2,1},{3,0},{4,7},{5,6},{6,5},{7,4},{8,11},{9,10},{10,... | collective-permute-start | bytes 589832 | tf_op jit(solution)/shard_map/ppermute | solution.py:557
  19.6 0.0 collective-permute-done.4.rest_3_.refs_0_
  19.6 0.0 collective-permute-done.5.rest_4_.refs_1_
  19.6 0.1 add_step.3
  19.7 2.4 %collective-permute-start.6 = (bf16[4,128,128]{2,1,0:T(8,128)(2,1)S(1)}, bf16[4,128,128]{2,1,0:T(8,128)(2,1)S(1)}, u32[]{:S(2)}, u32[]{:S(2)}) collective-permute-start(bf16[4,128,128]{2,1,0:T(8,128)(2,1)S(1)} %get-tuple-element.36.rest_0_), channel_id=1, source_target_pairs={{0,16},{4,20},{8,24},{12,28},{16,0},{20,4},{24,8},{28,12},{1,17},{... | collective-permute-start | bytes 393224 | tf_op jit(solution)/shard_map/ppermute | solution.py:557
  22.1 2.5 %attention_rows.4 = (f32[256,384]{1,0:T(8,128)S(1)}, f32[256,384]{1,0:T(8,128)S(1)}, bf16[256,384]{1,0:T(8,128)(2,1)S(1)}, bf16[256,384]{1,0:T(8,128)(2,1)S(1)}) custom-call(s32[1]{0:T(128)} %bitcast.head_ref.ids_ref.quarter_ref, bf16[4096,512]{1,0:T(8,128)(2,1)} %q_ref.15, bf16[4096,512]{1,0:T(8,128)(2,1)} %k_ref.17, bf16[4096,512]{1,0:T(8,128)(2,1)} %v_ref.17, ...), custom_call_target="tpu_custom_call" | custom-call | flops 1024 | bytes 1024 | tf_op jit(solution)/shard_map/attention_rows/pallas_call | solution.py:161
  24.5 2.4 %attention_rows.5.refs_9_.refs_1_ = bf16[512,384]{1,0:T(8,128)(2,1)S(1)} custom-call(s32[1]{0:T(128)} %bitcast.head_ref.ids_ref.quarter_ref, bf16[4096,512]{1,0:T(8,128)(2,1)} %q_ref.15, bf16[4096,512]{1,0:T(8,128)(2,1)} %k_ref.17, bf16[4096,512]{1,0:T(8,128)(2,1)} %v_ref.17, bf16[8,4,128,128]{3,2,1,0:T(8,128)(2,1)S(1)} %get-tuple-element.28.within_ref, ...), custom_call_target="tpu_custom_call" | custom-call | flops 1024 | bytes 1024 | tf_op jit(solution)/shard_map/attention_rows/pallas_call | solution.py:161
  27.0 1.4 %collective-permute-done.8.refs_8_.refs_3_ = bf16[768,128]{1,0:T(8,128)(2,1)S(1)} collective-permute-done((bf16[768,128]{1,0:T(8,128)(2,1)S(1)}, bf16[768,128]{1,0:T(8,128)(2,1)S(1)}, u32[]{:S(2)}, u32[]{:S(2)}) %collective-permute-start.8) | collective-permute-done | bytes 196640 | tf_op jit(solution)/shard_map/ppermute | solution.py:557
  28.4 0.1 collective-permute-done.6.refs_6_
  28.5 0.3 late_rows.2
  28.8 0.3 copy-done.2
  29.1 1.2 %collective-permute-start.10 = (bf16[304,384]{1,0:T(8,128)(2,1)S(1)}, bf16[304,384]{1,0:T(8,128)(2,1)S(1)}, u32[]{:S(2)}, u32[]{:S(2)}) collective-permute-start(bf16[304,384]{1,0:T(8,128)(2,1)S(1)} %get-tuple-element.43.refs_3_), channel_id=1, source_target_pairs={{0,2},{1,3},{2,0},{3,1},{4,6},{5,7},{6,4},{7,5},{8,10},{9,11},{10,... | collective-permute-start | bytes 700424 | tf_op jit(solution)/shard_map/ppermute | solution.py:557
  30.3 1.1 %collective-permute-start.12 = (bf16[256,384]{1,0:T(8,128)(2,1)S(1)}, bf16[256,384]{1,0:T(8,128)(2,1)S(1)}, u32[]{:S(2)}, u32[]{:S(2)}) collective-permute-start(bf16[256,384]{1,0:T(8,128)(2,1)S(1)} %get-tuple-element.44.refs_4_), channel_id=1, source_target_pairs={{0,3},{1,2},{2,1},{3,0},{4,7},{5,6},{6,5},{7,4},{8,11},{9,10},{10,... | collective-permute-start | bytes 589832 | tf_op jit(solution)/shard_map/ppermute | solution.py:557
  31.4 2.0 %late_rows.3.rest_1_ = bf16[512,384]{1,0:T(8,128)(2,1)} custom-call(s32[1]{0:T(128)} %bitcast.head_ref.ids_ref.quarter_ref, bf16[4096,512]{1,0:T(8,128)(2,1)} %q_ref.15, bf16[512,384]{1,0:T(8,128)(2,1)S(1)} %attention_rows.5.refs_9_.refs_1_, f32[4,128,128]{2,1,0:T(8,128)S(1)} %get-tuple-element.42.refs_2_.rest_0_, ...), custom_call_target="tpu_custom_call" | custom-call | flops 1024 | bytes 1024 | tf_op jit(solution)/shard_map/late_rows/pallas_call | solution.py:301
  33.4 3.2 %attention_rows.6.rest_2_ = bf16[512,384]{1,0:T(8,128)(2,1)} custom-call(s32[1]{0:T(128)} %bitcast.head_ref.ids_ref.quarter_ref, bf16[4096,512]{1,0:T(8,128)(2,1)} %q_ref.15, bf16[4096,512]{1,0:T(8,128)(2,1)} %k_ref.17, bf16[4096,512]{1,0:T(8,128)(2,1)} %v_ref.17, bf16[8,4,128,128]{3,2,1,0:T(8,128)(2,1)S(1)} %get-tuple-element.28.within_ref, ...), custom_call_target="tpu_custom_call" | custom-call | flops 1024 | bytes 1024 | tf_op jit(solution)/shard_map/attention_rows/pallas_call | solution.py:161
  36.5 0.7 %collective-permute-start.18 = (bf16[512,384]{1,0:T(8,128)(2,1)}, bf16[512,384]{1,0:T(8,128)(2,1)}, u32[]{:S(2)}, u32[]{:S(2)}) collective-permute-start(bf16[512,384]{1,0:T(8,128)(2,1)} %attention_rows.6.rest_2_), channel_id=1, source_target_pairs={{0,3},{1,2},{2,1},{3,0},{4,7},{5,6},{6,5},{7,4},{8,11},{9,10},{10,... | collective-permute-start | bytes 1179656 | tf_op jit(solution)/shard_map/ppermute | solution.py:557
  37.2 5.2 %attention_quarter.2.rest_1_ = bf16[1024,512]{1,0:T(8,128)(2,1)} custom-call(s32[1]{0:T(128)} %bitcast.head_ref.ids_ref.quarter_ref, bf16[4096,512]{1,0:T(8,128)(2,1)} %q_ref.15, bf16[4096,512]{1,0:T(8,128)(2,1)} %k_ref.17, bf16[4096,512]{1,0:T(8,128)(2,1)} %v_ref.17, bf16[8,4,128,128]{3,2,1,0:T(8,128)(2,1)S(1)} %get-tuple-element.28.within_ref, ...), custom_call_target="tpu_custom_call" | custom-call | flops 1024 | bytes 1024 | tf_op jit(solution)/shard_map/attention_quarter/pallas_call | solution.py:195
  42.4 0.5 collective-permute-start.17
  43.0 4.4 %attention_quarter.3.own_ref.rest_1_.refs_1_ = bf16[1024,512]{1,0:T(8,128)(2,1)S(1)} custom-call(s32[1]{0:T(128)} %bitcast.head_ref.ids_ref.quarter_ref, bf16[4096,512]{1,0:T(8,128)(2,1)} %q_ref.15, bf16[4096,512]{1,0:T(8,128)(2,1)} %k_ref.17, bf16[4096,512]{1,0:T(8,128)(2,1)} %v_ref.17, bf16[8,4,128,128]{3,2,1,0:T(8,128)(2,1)S(1)} %get-tuple-element.28.within_ref, ...), custom_call_target="tpu_custom_call" | custom-call | flops 1024 | bytes 1024 | tf_op jit(solution)/shard_map/attention_quarter/pallas_call | solution.py:195
  47.4 1.0 %collective-permute-start.9 = (bf16[1024,512]{1,0:T(8,128)(2,1)}, bf16[1024,512]{1,0:T(8,128)(2,1)}, u32[]{:S(2)}, u32[]{:S(2)}) collective-permute-start(bf16[1024,512]{1,0:T(8,128)(2,1)} %attention_quarter.2.rest_1_), channel_id=1, source_target_pairs={{0,1},{1,0},{2,3},{3,2},{4,5},{5,4},{6,7},{7,6},{8,9},{9,8},{10,11... | collective-permute-start | bytes 3145736 | tf_op jit(solution)/shard_map/ppermute | solution.py:557
  48.4 0.6 slice.4.refs_6_
  49.0 0.0 collective-permute-start.11
  49.0 3.3 %attention_rows.7 = (bf16[128,384]{1,0:T(8,128)(2,1)S(1)}, bf16[128,384]{1,0:T(8,128)(2,1)S(1)}, bf16[128,384]{1,0:T(8,128)(2,1)S(1)}, bf16[128,384]{1,0:T(8,128)(2,1)S(1)}) custom-call(s32[1]{0:T(128)} %bitcast.head_ref.ids_ref.quarter_ref, bf16[4096,512]{1,0:T(8,128)(2,1)} %q_ref.15, bf16[4096,512]{1,0:T(8,128)(2,1)} %k_ref.17, bf16[4096,512]{1,0:T(8,128)(2,1)} %v_ref.17, ...), custom_call_target="tpu_custom_call" | custom-call | flops 999999995904 | bytes 1024 | tf_op jit(solution)/shard_map/attention_rows/pallas_call | solution.py:161
  52.3 1.3 %collective-permute-start.13 = (bf16[128,384]{1,0:T(8,128)(2,1)S(1)}, bf16[128,384]{1,0:T(8,128)(2,1)S(1)}, u32[]{:S(2)}, u32[]{:S(2)}) collective-permute-start(bf16[128,384]{1,0:T(8,128)(2,1)S(1)} %get-tuple-element.47), channel_id=1, source_target_pairs={{0,2},{1,3},{2,0},{3,1},{4,6},{5,7},{6,4},{7,5},{8,10},{9,11},{10,... | collective-permute-start | bytes 294920 | tf_op jit(solution)/shard_map/ppermute | solution.py:557
  53.6 0.3 collective-permute-start.15
  53.8 2.1 %collective-permute-start.16 = (bf16[128,384]{1,0:T(8,128)(2,1)S(1)}, bf16[128,384]{1,0:T(8,128)(2,1)S(1)}, u32[]{:S(2)}, u32[]{:S(2)}) collective-permute-start(bf16[128,384]{1,0:T(8,128)(2,1)S(1)} %get-tuple-element.50), channel_id=1, source_target_pairs={{0,3},{1,2},{2,1},{3,0},{4,7},{5,6},{6,5},{7,4},{8,11},{9,10},{10,... | collective-permute-start | bytes 294920 | tf_op jit(solution)/shard_map/ppermute | solution.py:557
  56.0 0.1 collective-permute-start.14
  56.1 1.1 %early_out.1 = (bf16[1024,128]{1,0:T(8,128)(2,1)S(1)}, bf16[1024,128]{1,0:T(8,128)(2,1)S(1)}) custom-call(bf16[512,128]{1,0:T(8,128)(2,1)S(1)} %collective-permute-done.4.rest_3_.refs_0_, bf16[512,128]{1,0:T(8,128)(2,1)S(1)} %collective-permute-done.5.rest_4_.refs_1_, bf16[768,128]{1,0:T(8,128)(2,1)S(1)} %copy-done.1, bf16[768,128]{1,0:T(8,128)(2,1)S(1)} %copy-done.3, ...), custom_call_target="tpu_custom_call" | custom-call | flops 1024 | bytes 1024 | tf_op jit(solution)/shard_map/early_out/pallas_call | solution.py:345
  57.1 0.9 %gather_rows.1.near_ref = bf16[128,1280]{1,0:T(8,128)(2,1)S(1)} custom-call(bf16[1024,512]{1,0:T(8,128)(2,1)S(1)} %attention_quarter.3.own_ref.rest_1_.refs_1_, bf16[1024,512]{1,0:T(8,128)(2,1)} %collective-permute-done.9.mate_ref.refs_2_, bf16[1024,128]{1,0:T(8,128)(2,1)S(1)} %get-tuple-element.45.o2_ref.refs_4_, ...), custom_call_target="tpu_custom_call" | custom-call | flops 1024 | bytes 1024 | tf_op jit(solution)/shard_map/gather_rows/pallas_call | solution.py:370
  58.1 2.3 %norm_rows.2.refs_7_ = bf16[1024,2048]{1,0:T(8,128)(2,1)} custom-call(s32[1]{0:T(128)} %bitcast.head_ref.ids_ref.quarter_ref, f32[1,2048]{1,0:T(1,128)S(1)} %bitcast.3, bf16[1024,512]{1,0:T(8,128)(2,1)S(1)} %attention_quarter.3.own_ref.rest_1_.refs_1_, bf16[1024,512]{1,0:T(8,128)(2,1)} %collective-permute-done.9.mate_ref.refs_2_, ...), custom_call_target="tpu_custom_call" | custom-call | flops 1024 | bytes 1024 | tf_op jit(solution)/shard_map/norm_rows/pallas_call | solution.py:445
  60.4 3.3 %norm_block.1.rest_0_ = bf16[1024,2048]{1,0:T(8,128)(2,1)} custom-call(s32[1]{0:T(128)} %bitcast.head_ref.ids_ref.quarter_ref, f32[1,2048]{1,0:T(1,128)S(1)} %bitcast.4, bf16[1024,512]{1,0:T(8,128)(2,1)S(1)} %attention_quarter.3.own_ref.rest_1_.refs_1_, bf16[1024,512]{1,0:T(8,128)(2,1)} %collective-permute-done.9.mate_ref.refs_2_, ...), custom_call_target="tpu_custom_call", output_to_operand_aliasing={{}: (8, {})} | custom-call | flops 1024 | bytes 1024 | tf_op jit(solution)/shard_map/norm_block/pallas_call | solution.py:508
  63.7 1.4 %collective-permute-done.16.x3_ref = bf16[128,384]{1,0:T(8,128)(2,1)S(1)} collective-permute-done((bf16[128,384]{1,0:T(8,128)(2,1)S(1)}, bf16[128,384]{1,0:T(8,128)(2,1)S(1)}, u32[]{:S(2)}, u32[]{:S(2)}) %collective-permute-start.16) | collective-permute-done | bytes 98336 | tf_op jit(solution)/shard_map/ppermute | solution.py:557
  65.2 2.0 %norm_rows.3.old_ref = bf16[1024,2048]{1,0:T(8,128)(2,1)} custom-call(s32[1]{0:T(128)} %bitcast.head_ref.ids_ref.quarter_ref, f32[1,2048]{1,0:T(1,128)S(1)} %bitcast.5, bf16[1024,512]{1,0:T(8,128)(2,1)S(1)} %attention_quarter.3.own_ref.rest_1_.refs_1_, bf16[1024,512]{1,0:T(8,128)(2,1)} %collective-permute-done.9.mate_ref.refs_2_, ...), custom_call_target="tpu_custom_call", output_to_operand_aliasing={{}: (8, {})} | custom-call | flops 1024 | bytes 1024 | tf_op jit(solution)/shard_map/norm_rows/pallas_call | solution.py:445
  67.1 1.1 %norm_last.1 = bf16[1024,2048]{1,0:T(8,128)(2,1)} custom-call(s32[1]{0:T(128)} %bitcast.head_ref.ids_ref.quarter_ref, f32[1,2048]{1,0:T(1,128)S(1)} %bitcast.6, bf16[128,1280]{1,0:T(8,128)(2,1)S(1)} %gather_rows.1.near_ref, bf16[128,384]{1,0:T(8,128)(2,1)S(1)} %collective-permute-done.13.x2_ref, ...), custom_call_target="tpu_custom_call", output_to_operand_aliasing={{}: (5, {})} | custom-call | flops 1024 | bytes 1024 | tf_op jit(solution)/shard_map/norm_last/pallas_call | solution.py:393
  (21 shorter events, 0.0 us)
Async XLA Ops:
  1.1 12.5 %collective-permute-start.2 = (bf16[768,128]{1,0:T(8,128)(2,1)S(1)}, bf16[768,128]{1,0:T(8,128)(2,1)S(1)}, u32[]{:S(2)}, u32[]{:S(2)}) collective-permute-start(bf16[768,128]{1,0:T(8,128)(2,1)S(1)} %get-tuple-element.51.rest_1_), channel_id=1, source_target_pairs={{0,3},{1,2},{2,1},{3,0},{4,7},{5,6},{6,5},{7,4},{8,11},{9,10},{10,... | collective-permute-start | bytes 589832 | tf_op jit(solution)/shard_map/ppermute | solution.py:557
  3.7 9.9 %collective-permute-start.1 = (bf16[768,128]{1,0:T(8,128)(2,1)S(1)}, bf16[768,128]{1,0:T(8,128)(2,1)S(1)}, u32[]{:S(2)}, u32[]{:S(2)}) collective-permute-start(bf16[768,128]{1,0:T(8,128)(2,1)S(1)} %get-tuple-element.52.rest_0_), channel_id=1, source_target_pairs={{0,2},{1,3},{2,0},{3,1},{4,6},{5,7},{6,4},{7,5},{8,10},{9,11},{10,... | collective-permute-start | bytes 589832 | tf_op jit(solution)/shard_map/ppermute | solution.py:557
  7.7 5.9 %collective-permute-start = (bf16[4,128,128]{2,1,0:T(8,128)(2,1)S(1)}, bf16[4,128,128]{2,1,0:T(8,128)(2,1)S(1)}, u32[]{:S(2)}, u32[]{:S(2)}) collective-permute-start(bf16[4,128,128]{2,1,0:T(8,128)(2,1)S(1)} %get-tuple-element.29.rest_0_.total_ref), channel_id=1, source_target_pairs={{0,4},{4,0},{8,12},{12,8},{16,20},{20,16},{24,28},{28,24},{1,5},{5... | collective-permute-start | bytes 393224 | tf_op jit(solution)/shard_map/ppermute | solution.py:557
  11.4 8.2 %collective-permute-start.4 = (bf16[512,128]{1,0:T(8,128)(2,1)S(1)}, bf16[512,128]{1,0:T(8,128)(2,1)S(1)}, u32[]{:S(2)}, u32[]{:S(2)}) collective-permute-start(bf16[512,128]{1,0:T(8,128)(2,1)S(1)} %get-tuple-element.30.rest_0_), channel_id=1, source_target_pairs={{0,2},{1,3},{2,0},{3,1},{4,6},{5,7},{6,4},{7,5},{8,10},{9,11},{10,... | collective-permute-start | bytes 393224 | tf_op jit(solution)/shard_map/ppermute | solution.py:557
  12.7 6.9 %collective-permute-start.5 = (bf16[512,128]{1,0:T(8,128)(2,1)S(1)}, bf16[512,128]{1,0:T(8,128)(2,1)S(1)}, u32[]{:S(2)}, u32[]{:S(2)}) collective-permute-start(bf16[512,128]{1,0:T(8,128)(2,1)S(1)} %get-tuple-element.31.rest_1_), channel_id=1, source_target_pairs={{0,3},{1,2},{2,1},{3,0},{4,7},{5,6},{6,5},{7,4},{8,11},{9,10},{10,... | collective-permute-start | bytes 393224 | tf_op jit(solution)/shard_map/ppermute | solution.py:557
  13.7 5.9 %collective-permute-start.3 = (bf16[4,128,128]{2,1,0:T(8,128)(2,1)S(1)}, bf16[4,128,128]{2,1,0:T(8,128)(2,1)S(1)}, u32[]{:S(2)}, u32[]{:S(2)}) collective-permute-start(bf16[4,128,128]{2,1,0:T(8,128)(2,1)S(1)} %get-tuple-element.32.rest_1_.total_ref), channel_id=1, source_target_pairs={{0,8},{4,12},{8,0},{12,4},{16,24},{20,28},{24,16},{28,20},{1,9},{5... | collective-permute-start | bytes 393224 | tf_op jit(solution)/shard_map/ppermute | solution.py:557
  17.2 9.8 %collective-permute-start.7 = (bf16[768,128]{1,0:T(8,128)(2,1)S(1)}, bf16[768,128]{1,0:T(8,128)(2,1)S(1)}, u32[]{:S(2)}, u32[]{:S(2)}) collective-permute-start(bf16[768,128]{1,0:T(8,128)(2,1)S(1)} %get-tuple-element.34.rest_1_), channel_id=1, source_target_pairs={{0,2},{1,3},{2,0},{3,1},{4,6},{5,7},{6,4},{7,5},{8,10},{9,11},{10,... | collective-permute-start | bytes 589832 | tf_op jit(solution)/shard_map/ppermute | solution.py:557
  18.5 9.9 %collective-permute-start.8 = (bf16[768,128]{1,0:T(8,128)(2,1)S(1)}, bf16[768,128]{1,0:T(8,128)(2,1)S(1)}, u32[]{:S(2)}, u32[]{:S(2)}) collective-permute-start(bf16[768,128]{1,0:T(8,128)(2,1)S(1)} %get-tuple-element.35.rest_2_), channel_id=1, source_target_pairs={{0,3},{1,2},{2,1},{3,0},{4,7},{5,6},{6,5},{7,4},{8,11},{9,10},{10,... | collective-permute-start | bytes 589832 | tf_op jit(solution)/shard_map/ppermute | solution.py:557
  19.7 8.9 %collective-permute-start.6 = (bf16[4,128,128]{2,1,0:T(8,128)(2,1)S(1)}, bf16[4,128,128]{2,1,0:T(8,128)(2,1)S(1)}, u32[]{:S(2)}, u32[]{:S(2)}) collective-permute-start(bf16[4,128,128]{2,1,0:T(8,128)(2,1)S(1)} %get-tuple-element.36.rest_0_), channel_id=1, source_target_pairs={{0,16},{4,20},{8,24},{12,28},{16,0},{20,4},{24,8},{28,12},{1,17},{... | collective-permute-start | bytes 393224 | tf_op jit(solution)/shard_map/ppermute | solution.py:557
  27.0 1.9 %copy-start = (bf16[768,128]{1,0:T(8,128)(2,1)}, bf16[768,128]{1,0:T(8,128)(2,1)S(1)}, u32[]{:S(2)}) copy-start(bf16[768,128]{1,0:T(8,128)(2,1)S(1)} %collective-permute-done.7.refs_7_.refs_2_) | copy-start | bytes 589828
  28.4 0.7 %copy-start.2 = (bf16[768,128]{1,0:T(8,128)(2,1)}, bf16[768,128]{1,0:T(8,128)(2,1)S(1)}, u32[]{:S(2)}) copy-start(bf16[768,128]{1,0:T(8,128)(2,1)S(1)} %collective-permute-done.8.refs_8_.refs_3_) | copy-start | bytes 589828
  29.1 19.3 %collective-permute-start.10 = (bf16[304,384]{1,0:T(8,128)(2,1)S(1)}, bf16[304,384]{1,0:T(8,128)(2,1)S(1)}, u32[]{:S(2)}, u32[]{:S(2)}) collective-permute-start(bf16[304,384]{1,0:T(8,128)(2,1)S(1)} %get-tuple-element.43.refs_3_), channel_id=1, source_target_pairs={{0,2},{1,3},{2,0},{3,1},{4,6},{5,7},{6,4},{7,5},{8,10},{9,11},{10,... | collective-permute-start | bytes 700424 | tf_op jit(solution)/shard_map/ppermute | solution.py:557
  30.3 18.7 %collective-permute-start.12 = (bf16[256,384]{1,0:T(8,128)(2,1)S(1)}, bf16[256,384]{1,0:T(8,128)(2,1)S(1)}, u32[]{:S(2)}, u32[]{:S(2)}) collective-permute-start(bf16[256,384]{1,0:T(8,128)(2,1)S(1)} %get-tuple-element.44.refs_4_), channel_id=1, source_target_pairs={{0,3},{1,2},{2,1},{3,0},{4,7},{5,6},{6,5},{7,4},{8,11},{9,10},{10,... | collective-permute-start | bytes 589832 | tf_op jit(solution)/shard_map/ppermute | solution.py:557
  36.5 17.3 %collective-permute-start.18 = (bf16[512,384]{1,0:T(8,128)(2,1)}, bf16[512,384]{1,0:T(8,128)(2,1)}, u32[]{:S(2)}, u32[]{:S(2)}) collective-permute-start(bf16[512,384]{1,0:T(8,128)(2,1)} %attention_rows.6.rest_2_), channel_id=1, source_target_pairs={{0,3},{1,2},{2,1},{3,0},{4,7},{5,6},{6,5},{7,4},{8,11},{9,10},{10,... | collective-permute-start | bytes 1179656 | tf_op jit(solution)/shard_map/ppermute | solution.py:557
  42.4 17.9 %collective-permute-start.17 = (bf16[512,384]{1,0:T(8,128)(2,1)}, bf16[512,384]{1,0:T(8,128)(2,1)}, u32[]{:S(2)}, u32[]{:S(2)}) collective-permute-start(bf16[512,384]{1,0:T(8,128)(2,1)} %late_rows.3.rest_1_), channel_id=1, source_target_pairs={{0,2},{1,3},{2,0},{3,1},{4,6},{5,7},{6,4},{7,5},{8,10},{9,11},{10,... | collective-permute-start | bytes 1179656 | tf_op jit(solution)/shard_map/ppermute | solution.py:557
  47.4 8.6 %collective-permute-start.9 = (bf16[1024,512]{1,0:T(8,128)(2,1)}, bf16[1024,512]{1,0:T(8,128)(2,1)}, u32[]{:S(2)}, u32[]{:S(2)}) collective-permute-start(bf16[1024,512]{1,0:T(8,128)(2,1)} %attention_quarter.2.rest_1_), channel_id=1, source_target_pairs={{0,1},{1,0},{2,3},{3,2},{4,5},{5,4},{6,7},{7,6},{8,9},{9,8},{10,11... | collective-permute-start | bytes 3145736 | tf_op jit(solution)/shard_map/ppermute | solution.py:557
  49.0 4.6 %collective-permute-start.11 = (bf16[48,384]{1,0:T(8,128)(2,1)}, bf16[48,384]{1,0:T(8,128)(2,1)}, u32[]{:S(2)}, u32[]{:S(2)}) collective-permute-start(bf16[48,384]{1,0:T(8,128)(2,1)} %slice.4.refs_6_), channel_id=1, source_target_pairs={{0,1},{1,0},{2,3},{3,2},{4,5},{5,4},{6,7},{7,6},{8,9},{9,8},{10,11... | collective-permute-start | bytes 110600 | tf_op jit(solution)/shard_map/ppermute | solution.py:557
  49.0 7.0 %copy-start.1 = (bf16[768,128]{1,0:T(8,128)(2,1)S(1)}, bf16[768,128]{1,0:T(8,128)(2,1)}, u32[]{:S(2)}) copy-start(bf16[768,128]{1,0:T(8,128)(2,1)} %copy-done) | copy-start | bytes 589828
  49.0 7.0 %copy-start.3 = (bf16[768,128]{1,0:T(8,128)(2,1)S(1)}, bf16[768,128]{1,0:T(8,128)(2,1)}, u32[]{:S(2)}) copy-start(bf16[768,128]{1,0:T(8,128)(2,1)} %copy-done.2) | copy-start | bytes 589828
  49.0 9.1 %copy-start.4 = (f32[2048]{0:T(1024)S(1)}, f32[2048]{0:T(1024)}, u32[]{:S(2)}) copy-start(f32[2048]{0:T(1024)} %param.7) | copy-start | bytes 24580
  52.3 14.8 %collective-permute-start.13 = (bf16[128,384]{1,0:T(8,128)(2,1)S(1)}, bf16[128,384]{1,0:T(8,128)(2,1)S(1)}, u32[]{:S(2)}, u32[]{:S(2)}) collective-permute-start(bf16[128,384]{1,0:T(8,128)(2,1)S(1)} %get-tuple-element.47), channel_id=1, source_target_pairs={{0,2},{1,3},{2,0},{3,1},{4,6},{5,7},{6,4},{7,5},{8,10},{9,11},{10,... | collective-permute-start | bytes 294920 | tf_op jit(solution)/shard_map/ppermute | solution.py:557
  53.6 10.1 %collective-permute-start.15 = (bf16[128,384]{1,0:T(8,128)(2,1)S(1)}, bf16[128,384]{1,0:T(8,128)(2,1)S(1)}, u32[]{:S(2)}, u32[]{:S(2)}) collective-permute-start(bf16[128,384]{1,0:T(8,128)(2,1)S(1)} %get-tuple-element.49), channel_id=1, source_target_pairs={{0,2},{1,3},{2,0},{3,1},{4,6},{5,7},{6,4},{7,5},{8,10},{9,11},{10,... | collective-permute-start | bytes 294920 | tf_op jit(solution)/shard_map/ppermute | solution.py:557
  53.8 11.3 %collective-permute-start.16 = (bf16[128,384]{1,0:T(8,128)(2,1)S(1)}, bf16[128,384]{1,0:T(8,128)(2,1)S(1)}, u32[]{:S(2)}, u32[]{:S(2)}) collective-permute-start(bf16[128,384]{1,0:T(8,128)(2,1)S(1)} %get-tuple-element.50), channel_id=1, source_target_pairs={{0,3},{1,2},{2,1},{3,0},{4,7},{5,6},{6,5},{7,4},{8,11},{9,10},{10,... | collective-permute-start | bytes 294920 | tf_op jit(solution)/shard_map/ppermute | solution.py:557
  56.0 11.1 %collective-permute-start.14 = (bf16[128,384]{1,0:T(8,128)(2,1)S(1)}, bf16[128,384]{1,0:T(8,128)(2,1)S(1)}, u32[]{:S(2)}, u32[]{:S(2)}) collective-permute-start(bf16[128,384]{1,0:T(8,128)(2,1)S(1)} %get-tuple-element.48), channel_id=1, source_target_pairs={{0,3},{1,2},{2,1},{3,0},{4,7},{5,6},{6,5},{7,4},{8,11},{9,10},{10,... | collective-permute-start | bytes 294920 | tf_op jit(solution)/shard_map/ppermute | solution.py:557
